TPU v7x, 32 devices: a whole 2x2x4 slice. The times are simulated.
32 devices in a mesh: groups: 2 (over x), chan: 16 (over z, y, core).
Axes of the slice: x: 2, y: 2, z: 4, core: 2. Of those that a mesh axis runs over, the one named last changes fastest.
Arguments:
- voltages: bfloat16 [2048, 128, 128], P(('groups', 'chan')), parts along dimension 0, may hold values from -8 to 8
- antenna_usable_mask: int32 [2048], P('groups'), parts along dimension 0, may hold values 0 or 1
- channel_flags: int32 [256], P(('groups', 'chan')), parts along dimension 0, may hold values 0 or 1
Outputs:
- solution: float32 [3, 2048], P(None, 'groups'), parts along dimension 1
- channel_fit: float32 [2, 256, 1024], P(None, ('groups', 'chan')), parts along dimension 1
There are 2 independent parts, one for each index of `groups`. A program takes and returns all parts, laid end to end along the dimension named above; each array names one. Nothing has to cross between parts.
All inputs are finite; a program needn't handle non-finite values. No bound on the sum of `channel_flags` on one device may be relied on, other than what follows from the above.
Results may differ from a plain program's by a relative error of at most 0.0003.
Values may be sent and summed in bfloat16 or wider, within the bound.
No kernel may reach another device: no remote copies, remote signals or barrier semaphores. Data moves between devices by JAX's collectives and lax.ppermute only.
A program may use at most 128 MiB of HBM per device.

v0:
```python
import math

import jax
import jax.numpy as jnp
from jax import lax
from jax.sharding import PartitionSpec as P

ITERS = 3


huber_scale = 0.25
damping = 0.5


def channel_normal_terms(visibility_channel, angular_frequency, gain_parameters, antenna_weight):
    inputs = visibility_channel.shape[1]
    angles = gain_parameters[1] + angular_frequency * gain_parameters[2]
    model_re = gain_parameters[0] * jnp.cos(angles)
    model_im = gain_parameters[0] * jnp.sin(angles)
    vis_re = visibility_channel[:inputs].astype(jnp.float32)
    vis_im = visibility_channel[inputs:].astype(jnp.float32)
    pair_re = model_re[:, None] * model_re[None, :] + model_im[:, None] * model_im[None, :]
    pair_im = model_im[:, None] * model_re[None, :] - model_re[:, None] * model_im[None, :]
    residual_real = vis_re - pair_re
    residual_imaginary = vis_im - pair_im
    positions = jnp.arange(inputs)
    baseline_cross_mask = (positions[:, None] != positions[None, :]).astype(jnp.float32)
    robust_weighting = (
        antenna_weight[:, None]
        * antenna_weight[None, :]
        * baseline_cross_mask
        / (
            1.0
            + (residual_real * residual_real + residual_imaginary * residual_imaginary)
            / huber_scale
        )
    )
    prod_re = vis_re * pair_re + vis_im * pair_im
    prod_im = vis_im * pair_re - vis_re * pair_im
    return (
        jnp.sum(robust_weighting * prod_re, axis=1),
        jnp.sum(robust_weighting * prod_im, axis=1),
        jnp.sum(robust_weighting * (pair_re * pair_re + pair_im * pair_im), axis=1),
    )


def weighted_sums(prod_re, prod_im, curvature, chan_weight, angular_frequency):
    weight_col = chan_weight[:, None]
    freq_col = angular_frequency[:, None]
    return jnp.stack(
        [
            jnp.sum(weight_col * prod_re, axis=0),
            jnp.sum(weight_col * prod_im, axis=0),
            jnp.sum(weight_col * freq_col * prod_im, axis=0),
            jnp.sum(weight_col * curvature, axis=0),
            jnp.sum(weight_col * freq_col * curvature, axis=0),
            jnp.sum(weight_col * freq_col * freq_col * curvature, axis=0),
        ]
    )


def solve_update(gain_parameters, sums):
    determinant = jnp.maximum(sums[3] * sums[5] - sums[4] * sums[4], 1.0)
    step_phase = (sums[5] * sums[1] - sums[4] * sums[2]) / determinant
    step_delay = (sums[3] * sums[2] - sums[4] * sums[1]) / determinant
    amplitude = gain_parameters[0] * (
        1.0 + damping * (sums[0] - sums[3]) / jnp.maximum(sums[3], 1.0)
    )
    return jnp.stack(
        [
            amplitude,
            gain_parameters[1] + damping * step_phase,
            gain_parameters[2] + damping * step_delay,
        ]
    )


def one_channel(channel_rows):
    half = channel_rows.shape[-1] // 2
    swapped = jnp.concatenate([channel_rows[:, half:], -channel_rows[:, :half]], axis=1)
    stacked = jnp.concatenate([channel_rows, swapped], axis=0)
    product = lax.dot_general(
        stacked, channel_rows, (((1,), (1,)), ((), ())), preferred_element_type=jnp.float32
    )
    return (product * (1.0 / half)).astype(jnp.bfloat16)


def correlate(arrived):
    channel_major = jnp.transpose(arrived[:, 0], (1, 0, 2))
    return lax.map(one_channel, channel_major)


def local(voltages, antenna_usable_mask, channel_flags):
    devices = lax.axis_size("chan")
    inputs_dev, channels, sample_cols = voltages.shape
    chan_dev = channels // devices
    blocks = voltages.reshape(inputs_dev, devices, chan_dev, sample_cols)
    turned = lax.all_to_all(blocks, "chan", split_axis=1, concat_axis=0, tiled=True)
    visibilities = correlate(turned)
    inputs = visibilities.shape[2]
    first_channel = lax.axis_index("chan") * chan_dev
    channel_ids = (first_channel + jnp.arange(chan_dev)).astype(jnp.float32)
    angular_frequency = 2.0 * math.pi * (channel_ids + 0.5) / (chan_dev * devices)
    chan_weight = channel_flags.astype(jnp.float32)
    antenna_weight = antenna_usable_mask.astype(jnp.float32)
    gain_parameters = jnp.concatenate(
        [jnp.ones((1, inputs), jnp.float32), jnp.zeros((2, inputs), jnp.float32)], axis=0
    )
    fitted = jnp.zeros((2, chan_dev, inputs), jnp.float32)
    for iteration in range(ITERS):

        def per_channel(solver_entry, gain_parameters=gain_parameters):
            return channel_normal_terms(
                solver_entry[0], solver_entry[1], gain_parameters, antenna_weight
            )

        prod_re, prod_im, curvature = lax.map(per_channel, (visibilities, angular_frequency))
        partial_sums = weighted_sums(prod_re, prod_im, curvature, chan_weight, angular_frequency)
        fitted = jnp.stack([prod_re, prod_im]) / jnp.maximum(curvature, 1.0)[None]
        totals = lax.psum(partial_sums, "chan")
        gain_parameters = solve_update(gain_parameters, totals)
    return (gain_parameters, fitted)


def solution(mesh):
    placed = (P(("groups", "chan"), None, None), P("groups"), P(("groups", "chan")))
    return jax.shard_map(
        local,
        mesh=mesh,
        in_specs=placed,
        out_specs=(P(None, "groups"), P(None, ("groups", "chan"), None)),
        check_vma=False,
    )
```

profile of v0, /device:TPU:0, one launch (start us, length us, event | category | flops | bytes accessed | tf_op | source)
XLA Modules:
  0.0 480.1 jit_solution(7814687942235623390)
XLA Ops:
  4.9 7.4 %all-to-all-start = ((bf16[64,16,8,128]{3,0,2,1:T(8,128)(2,1)}), bf16[64,16,8,128]{3,0,2,1:T(8,128)(2,1)S(1)}, u32[]{:S(2)}, u32[]{:S(2)}) async-start(bf16[64,16,8,128]{3,0,2,1:T(8,128)(2,1)} %bitcast.138), calls=%async_computation | async-start | bytes 4194304 | tf_op jit(solution)/shard_map/all_to_all | solution.py:98
  12.4 41.0 %all-to-all-done = bf16[64,16,8,128]{3,0,2,1:T(8,128)(2,1)S(1)} async-done(((bf16[64,16,8,128]{3,0,2,1:T(8,128)(2,1)}), bf16[64,16,8,128]{3,0,2,1:T(8,128)(2,1)S(1)}, u32[]{:S(2)}, u32[]{:S(2)}) %all-to-all-start) | async-done | bytes 2097184 | tf_op jit(solution)/shard_map/all_to_all | solution.py:98
  55.5 27.1 %while.52 = (s32[]{:T(128)}, bf16[8,2048,1024]{2,1,0:T(8,128)(2,1)}, bf16[8,1024,128]{2,1,0:T(8,128)(2,1)S(1)}, s32[]{:T(128)}) while((s32[]{:T(128)}, bf16[8,2048,1024]{2,1,0:T(8,128)(2,1)}, bf16[8,1024,128]{2,1,0:T(8,128)(2,1)S(1)}, s32[]{:T(128)}) %tuple.119), condition=%wide.region_1.2_spmd, body=%wide.region_0.1_spmd.sunk | while | flops 542703616 | bytes 6292025 | solution.py:90
  82.6 63.7 %while.53 = (s32[]{:T(128)}, f32[8,1024]{1,0:T(8,128)S(1)}, f32[8,1024]{1,0:T(8,128)S(1)}, f32[8,1024]{1,0:T(8,128)S(1)}, f32[1024]{0:T(1024)S(1)}, /*index=5*/b...) while((s32[]{:T(128)}, f32[8,1024]{1,0:T(8,128)S(1)}, ...), condition=%wide.region_6.7_spmd, body=%wide.region_2.6_spmd.sunk | while | flops 26211340 | bytes 4239649 | solution.py:117
  84.1 6.1 %fusion.65 = (f32[1024]{0:T(1024)S(1)}, f32[1024]{0:T(1024)S(1)}, f32[1024]{0:T(1024)S(1)}) fusion(f32[]{:T(128)} %bitcast.125, f32[]{:T(128)} %bitcast.126, bf16[8,2048,1024]{2,1,0:T(8,128)(2,1)} %get-tuple-element.555, s32[]{:T(128)} %get-tuple-element.539, s32[]{:T(128)S(6)} %add.294, f32[]{:T(128)S(6)} %add.295, f32[1024]{0:T(1024)S(1)} %get-tuple-element.554), kind=kLoop, calls=%fused_computation.29.clone.1 | loop fusion | flops 26211328 | bytes 4214804 | tf_op jit(solution)/shard_map/while/body/eval_jaxpr/reduce_sum | solution.py:42
  100.0 6.1 %fusion.65 = (f32[1024]{0:T(1024)S(1)}, f32[1024]{0:T(1024)S(1)}, f32[1024]{0:T(1024)S(1)}) fusion(f32[]{:T(128)} %bitcast.125, f32[]{:T(128)} %bitcast.126, bf16[8,2048,1024]{2,1,0:T(8,128)(2,1)} %get-tuple-element.555, s32[]{:T(128)} %get-tuple-element.539, s32[]{:T(128)S(6)} %add.294, f32[]{:T(128)S(6)} %add.295, f32[1024]{0:T(1024)S(1)} %get-tuple-element.554), kind=kLoop, calls=%fused_computation.29.clone.1 | loop fusion | flops 26211328 | bytes 4214804 | tf_op jit(solution)/shard_map/while/body/eval_jaxpr/reduce_sum | solution.py:42
  108.0 6.1 %fusion.65 = (f32[1024]{0:T(1024)S(1)}, f32[1024]{0:T(1024)S(1)}, f32[1024]{0:T(1024)S(1)}) fusion(f32[]{:T(128)} %bitcast.125, f32[]{:T(128)} %bitcast.126, bf16[8,2048,1024]{2,1,0:T(8,128)(2,1)} %get-tuple-element.555, s32[]{:T(128)} %get-tuple-element.539, s32[]{:T(128)S(6)} %add.294, f32[]{:T(128)S(6)} %add.295, f32[1024]{0:T(1024)S(1)} %get-tuple-element.554), kind=kLoop, calls=%fused_computation.29.clone.1 | loop fusion | flops 26211328 | bytes 4214804 | tf_op jit(solution)/shard_map/while/body/eval_jaxpr/reduce_sum | solution.py:42
  115.9 6.1 %fusion.65 = (f32[1024]{0:T(1024)S(1)}, f32[1024]{0:T(1024)S(1)}, f32[1024]{0:T(1024)S(1)}) fusion(f32[]{:T(128)} %bitcast.125, f32[]{:T(128)} %bitcast.126, bf16[8,2048,1024]{2,1,0:T(8,128)(2,1)} %get-tuple-element.555, s32[]{:T(128)} %get-tuple-element.539, s32[]{:T(128)S(6)} %add.294, f32[]{:T(128)S(6)} %add.295, f32[1024]{0:T(1024)S(1)} %get-tuple-element.554), kind=kLoop, calls=%fused_computation.29.clone.1 | loop fusion | flops 26211328 | bytes 4214804 | tf_op jit(solution)/shard_map/while/body/eval_jaxpr/reduce_sum | solution.py:42
  123.9 6.1 %fusion.65 = (f32[1024]{0:T(1024)S(1)}, f32[1024]{0:T(1024)S(1)}, f32[1024]{0:T(1024)S(1)}) fusion(f32[]{:T(128)} %bitcast.125, f32[]{:T(128)} %bitcast.126, bf16[8,2048,1024]{2,1,0:T(8,128)(2,1)} %get-tuple-element.555, s32[]{:T(128)} %get-tuple-element.539, s32[]{:T(128)S(6)} %add.294, f32[]{:T(128)S(6)} %add.295, f32[1024]{0:T(1024)S(1)} %get-tuple-element.554), kind=kLoop, calls=%fused_computation.29.clone.1 | loop fusion | flops 26211328 | bytes 4214804 | tf_op jit(solution)/shard_map/while/body/eval_jaxpr/reduce_sum | solution.py:42
  131.8 6.1 %fusion.65 = (f32[1024]{0:T(1024)S(1)}, f32[1024]{0:T(1024)S(1)}, f32[1024]{0:T(1024)S(1)}) fusion(f32[]{:T(128)} %bitcast.125, f32[]{:T(128)} %bitcast.126, bf16[8,2048,1024]{2,1,0:T(8,128)(2,1)} %get-tuple-element.555, s32[]{:T(128)} %get-tuple-element.539, s32[]{:T(128)S(6)} %add.294, f32[]{:T(128)S(6)} %add.295, f32[1024]{0:T(1024)S(1)} %get-tuple-element.554), kind=kLoop, calls=%fused_computation.29.clone.1 | loop fusion | flops 26211328 | bytes 4214804 | tf_op jit(solution)/shard_map/while/body/eval_jaxpr/reduce_sum | solution.py:42
  139.8 6.1 %fusion.65 = (f32[1024]{0:T(1024)S(1)}, f32[1024]{0:T(1024)S(1)}, f32[1024]{0:T(1024)S(1)}) fusion(f32[]{:T(128)} %bitcast.125, f32[]{:T(128)} %bitcast.126, bf16[8,2048,1024]{2,1,0:T(8,128)(2,1)} %get-tuple-element.555, s32[]{:T(128)} %get-tuple-element.539, s32[]{:T(128)S(6)} %add.294, f32[]{:T(128)S(6)} %add.295, f32[1024]{0:T(1024)S(1)} %get-tuple-element.554), kind=kLoop, calls=%fused_computation.29.clone.1 | loop fusion | flops 26211328 | bytes 4214804 | tf_op jit(solution)/shard_map/while/body/eval_jaxpr/reduce_sum | solution.py:42
  146.5 67.2 %psum.21 = f32[6,1024]{1,0:T(8,128)S(1)} all-reduce(f32[6,1024]{1,0:T(8,128)S(1)} %stack.84), channel_id=1, replica_groups=mesh['groups'=2,'chan'=16] {'chan'}, use_global_device_ids=true, to_apply=%region_13.14 | all-reduce | flops 6144 | bytes 49152 | tf_op jit(solution)/shard_map/psum | solution.py:120
  213.8 74.9 %while.54 = (s32[]{:T(128)}, f32[8,1024]{1,0:T(8,128)S(1)}, f32[8,1024]{1,0:T(8,128)S(1)}, f32[8,1024]{1,0:T(8,128)S(1)}, f32[1024]{0:T(1024)S(1)}, /*index=5*/b...) while((s32[]{:T(128)}, f32[8,1024]{1,0:T(8,128)S(1)}, ...), condition=%wide.region_18.19_spmd, body=%wide.region_14.18_spmd.sunk | while | flops 35652608 | bytes 4276397 | solution.py:117
  215.2 7.6 %fusion.66 = (f32[1024]{0:T(1024)S(1)}, f32[1024]{0:T(1024)S(1)}, f32[1024]{0:T(1024)S(1)}) fusion(f32[1024]{0:T(1024)S(1)} %get-tuple-element.496, f32[1024]{0:T(1024)S(1)} %get-tuple-element.497, bf16[8,2048,1024]{2,1,0:T(8,128)(2,1)} %get-tuple-element.592, s32[]{:T(128)} %get-tuple-element.574, s32[]{:T(128)S(6)} %add.298, ...), kind=kLoop, calls=%fused_computation.49.clone.1 | loop fusion | flops 35648512 | bytes 4231176 | tf_op jit(solution)/shard_map/while/body/eval_jaxpr/reduce_sum | solution.py:42
  224.5 7.6 %fusion.66 = (f32[1024]{0:T(1024)S(1)}, f32[1024]{0:T(1024)S(1)}, f32[1024]{0:T(1024)S(1)}) fusion(f32[1024]{0:T(1024)S(1)} %get-tuple-element.496, f32[1024]{0:T(1024)S(1)} %get-tuple-element.497, bf16[8,2048,1024]{2,1,0:T(8,128)(2,1)} %get-tuple-element.592, s32[]{:T(128)} %get-tuple-element.574, s32[]{:T(128)S(6)} %add.298, ...), kind=kLoop, calls=%fused_computation.49.clone.1 | loop fusion | flops 35648512 | bytes 4231176 | tf_op jit(solution)/shard_map/while/body/eval_jaxpr/reduce_sum | solution.py:42
  233.9 7.6 %fusion.66 = (f32[1024]{0:T(1024)S(1)}, f32[1024]{0:T(1024)S(1)}, f32[1024]{0:T(1024)S(1)}) fusion(f32[1024]{0:T(1024)S(1)} %get-tuple-element.496, f32[1024]{0:T(1024)S(1)} %get-tuple-element.497, bf16[8,2048,1024]{2,1,0:T(8,128)(2,1)} %get-tuple-element.592, s32[]{:T(128)} %get-tuple-element.574, s32[]{:T(128)S(6)} %add.298, ...), kind=kLoop, calls=%fused_computation.49.clone.1 | loop fusion | flops 35648512 | bytes 4231176 | tf_op jit(solution)/shard_map/while/body/eval_jaxpr/reduce_sum | solution.py:42
  243.2 7.6 %fusion.66 = (f32[1024]{0:T(1024)S(1)}, f32[1024]{0:T(1024)S(1)}, f32[1024]{0:T(1024)S(1)}) fusion(f32[1024]{0:T(1024)S(1)} %get-tuple-element.496, f32[1024]{0:T(1024)S(1)} %get-tuple-element.497, bf16[8,2048,1024]{2,1,0:T(8,128)(2,1)} %get-tuple-element.592, s32[]{:T(128)} %get-tuple-element.574, s32[]{:T(128)S(6)} %add.298, ...), kind=kLoop, calls=%fused_computation.49.clone.1 | loop fusion | flops 35648512 | bytes 4231176 | tf_op jit(solution)/shard_map/while/body/eval_jaxpr/reduce_sum | solution.py:42
  252.6 7.6 %fusion.66 = (f32[1024]{0:T(1024)S(1)}, f32[1024]{0:T(1024)S(1)}, f32[1024]{0:T(1024)S(1)}) fusion(f32[1024]{0:T(1024)S(1)} %get-tuple-element.496, f32[1024]{0:T(1024)S(1)} %get-tuple-element.497, bf16[8,2048,1024]{2,1,0:T(8,128)(2,1)} %get-tuple-element.592, s32[]{:T(128)} %get-tuple-element.574, s32[]{:T(128)S(6)} %add.298, ...), kind=kLoop, calls=%fused_computation.49.clone.1 | loop fusion | flops 35648512 | bytes 4231176 | tf_op jit(solution)/shard_map/while/body/eval_jaxpr/reduce_sum | solution.py:42
  262.0 7.6 %fusion.66 = (f32[1024]{0:T(1024)S(1)}, f32[1024]{0:T(1024)S(1)}, f32[1024]{0:T(1024)S(1)}) fusion(f32[1024]{0:T(1024)S(1)} %get-tuple-element.496, f32[1024]{0:T(1024)S(1)} %get-tuple-element.497, bf16[8,2048,1024]{2,1,0:T(8,128)(2,1)} %get-tuple-element.592, s32[]{:T(128)} %get-tuple-element.574, s32[]{:T(128)S(6)} %add.298, ...), kind=kLoop, calls=%fused_computation.49.clone.1 | loop fusion | flops 35648512 | bytes 4231176 | tf_op jit(solution)/shard_map/while/body/eval_jaxpr/reduce_sum | solution.py:42
  271.3 7.6 %fusion.66 = (f32[1024]{0:T(1024)S(1)}, f32[1024]{0:T(1024)S(1)}, f32[1024]{0:T(1024)S(1)}) fusion(f32[1024]{0:T(1024)S(1)} %get-tuple-element.496, f32[1024]{0:T(1024)S(1)} %get-tuple-element.497, bf16[8,2048,1024]{2,1,0:T(8,128)(2,1)} %get-tuple-element.592, s32[]{:T(128)} %get-tuple-element.574, s32[]{:T(128)S(6)} %add.298, ...), kind=kLoop, calls=%fused_computation.49.clone.1 | loop fusion | flops 35648512 | bytes 4231176 | tf_op jit(solution)/shard_map/while/body/eval_jaxpr/reduce_sum | solution.py:42
  280.7 7.6 %fusion.66 = (f32[1024]{0:T(1024)S(1)}, f32[1024]{0:T(1024)S(1)}, f32[1024]{0:T(1024)S(1)}) fusion(f32[1024]{0:T(1024)S(1)} %get-tuple-element.496, f32[1024]{0:T(1024)S(1)} %get-tuple-element.497, bf16[8,2048,1024]{2,1,0:T(8,128)(2,1)} %get-tuple-element.592, s32[]{:T(128)} %get-tuple-element.574, s32[]{:T(128)S(6)} %add.298, ...), kind=kLoop, calls=%fused_computation.49.clone.1 | loop fusion | flops 35648512 | bytes 4231176 | tf_op jit(solution)/shard_map/while/body/eval_jaxpr/reduce_sum | solution.py:42
  288.8 57.8 %psum.22 = f32[6,1024]{1,0:T(8,128)S(1)} all-reduce(f32[6,1024]{1,0:T(8,128)S(1)} %stack.91), channel_id=1, replica_groups=mesh['groups'=2,'chan'=16] {'chan'}, use_global_device_ids=true, to_apply=%region_25.26 | all-reduce | flops 6144 | bytes 49152 | tf_op jit(solution)/shard_map/psum | solution.py:120
  346.8 74.1 %while.55 = (s32[]{:T(128)}, f32[8,1024]{1,0:T(8,128)S(1)}, f32[8,1024]{1,0:T(8,128)S(1)}, f32[8,1024]{1,0:T(8,128)S(1)}, f32[1024]{0:T(1024)S(1)}, /*index=5*/b...) while((s32[]{:T(128)}, f32[8,1024]{1,0:T(8,128)S(1)}, ...), condition=%wide.region_30.31_spmd, body=%wide.region_26.30_spmd.sunk | while | flops 35652608 | bytes 4276397 | solution.py:117
  348.1 7.6 %fusion.67 = (f32[1024]{0:T(1024)S(1)}, f32[1024]{0:T(1024)S(1)}, f32[1024]{0:T(1024)S(1)}) fusion(f32[1024]{0:T(1024)S(1)} %get-tuple-element.511, f32[1024]{0:T(1024)S(1)} %get-tuple-element.512, bf16[8,2048,1024]{2,1,0:T(8,128)(2,1)} %get-tuple-element.631, s32[]{:T(128)} %get-tuple-element.613, s32[]{:T(128)S(6)} %add.301, ...), kind=kLoop, calls=%fused_computation.76.clone.1 | loop fusion | flops 35648512 | bytes 4231176 | tf_op jit(solution)/shard_map/while/body/eval_jaxpr/reduce_sum | solution.py:42
  357.3 7.6 %fusion.67 = (f32[1024]{0:T(1024)S(1)}, f32[1024]{0:T(1024)S(1)}, f32[1024]{0:T(1024)S(1)}) fusion(f32[1024]{0:T(1024)S(1)} %get-tuple-element.511, f32[1024]{0:T(1024)S(1)} %get-tuple-element.512, bf16[8,2048,1024]{2,1,0:T(8,128)(2,1)} %get-tuple-element.631, s32[]{:T(128)} %get-tuple-element.613, s32[]{:T(128)S(6)} %add.301, ...), kind=kLoop, calls=%fused_computation.76.clone.1 | loop fusion | flops 35648512 | bytes 4231176 | tf_op jit(solution)/shard_map/while/body/eval_jaxpr/reduce_sum | solution.py:42
  366.6 7.6 %fusion.67 = (f32[1024]{0:T(1024)S(1)}, f32[1024]{0:T(1024)S(1)}, f32[1024]{0:T(1024)S(1)}) fusion(f32[1024]{0:T(1024)S(1)} %get-tuple-element.511, f32[1024]{0:T(1024)S(1)} %get-tuple-element.512, bf16[8,2048,1024]{2,1,0:T(8,128)(2,1)} %get-tuple-element.631, s32[]{:T(128)} %get-tuple-element.613, s32[]{:T(128)S(6)} %add.301, ...), kind=kLoop, calls=%fused_computation.76.clone.1 | loop fusion | flops 35648512 | bytes 4231176 | tf_op jit(solution)/shard_map/while/body/eval_jaxpr/reduce_sum | solution.py:42
  375.9 7.6 %fusion.67 = (f32[1024]{0:T(1024)S(1)}, f32[1024]{0:T(1024)S(1)}, f32[1024]{0:T(1024)S(1)}) fusion(f32[1024]{0:T(1024)S(1)} %get-tuple-element.511, f32[1024]{0:T(1024)S(1)} %get-tuple-element.512, bf16[8,2048,1024]{2,1,0:T(8,128)(2,1)} %get-tuple-element.631, s32[]{:T(128)} %get-tuple-element.613, s32[]{:T(128)S(6)} %add.301, ...), kind=kLoop, calls=%fused_computation.76.clone.1 | loop fusion | flops 35648512 | bytes 4231176 | tf_op jit(solution)/shard_map/while/body/eval_jaxpr/reduce_sum | solution.py:42
  385.1 7.6 %fusion.67 = (f32[1024]{0:T(1024)S(1)}, f32[1024]{0:T(1024)S(1)}, f32[1024]{0:T(1024)S(1)}) fusion(f32[1024]{0:T(1024)S(1)} %get-tuple-element.511, f32[1024]{0:T(1024)S(1)} %get-tuple-element.512, bf16[8,2048,1024]{2,1,0:T(8,128)(2,1)} %get-tuple-element.631, s32[]{:T(128)} %get-tuple-element.613, s32[]{:T(128)S(6)} %add.301, ...), kind=kLoop, calls=%fused_computation.76.clone.1 | loop fusion | flops 35648512 | bytes 4231176 | tf_op jit(solution)/shard_map/while/body/eval_jaxpr/reduce_sum | solution.py:42
  394.4 7.6 %fusion.67 = (f32[1024]{0:T(1024)S(1)}, f32[1024]{0:T(1024)S(1)}, f32[1024]{0:T(1024)S(1)}) fusion(f32[1024]{0:T(1024)S(1)} %get-tuple-element.511, f32[1024]{0:T(1024)S(1)} %get-tuple-element.512, bf16[8,2048,1024]{2,1,0:T(8,128)(2,1)} %get-tuple-element.631, s32[]{:T(128)} %get-tuple-element.613, s32[]{:T(128)S(6)} %add.301, ...), kind=kLoop, calls=%fused_computation.76.clone.1 | loop fusion | flops 35648512 | bytes 4231176 | tf_op jit(solution)/shard_map/while/body/eval_jaxpr/reduce_sum | solution.py:42
  403.7 7.6 %fusion.67 = (f32[1024]{0:T(1024)S(1)}, f32[1024]{0:T(1024)S(1)}, f32[1024]{0:T(1024)S(1)}) fusion(f32[1024]{0:T(1024)S(1)} %get-tuple-element.511, f32[1024]{0:T(1024)S(1)} %get-tuple-element.512, bf16[8,2048,1024]{2,1,0:T(8,128)(2,1)} %get-tuple-element.631, s32[]{:T(128)} %get-tuple-element.613, s32[]{:T(128)S(6)} %add.301, ...), kind=kLoop, calls=%fused_computation.76.clone.1 | loop fusion | flops 35648512 | bytes 4231176 | tf_op jit(solution)/shard_map/while/body/eval_jaxpr/reduce_sum | solution.py:42
  412.9 7.6 %fusion.67 = (f32[1024]{0:T(1024)S(1)}, f32[1024]{0:T(1024)S(1)}, f32[1024]{0:T(1024)S(1)}) fusion(f32[1024]{0:T(1024)S(1)} %get-tuple-element.511, f32[1024]{0:T(1024)S(1)} %get-tuple-element.512, bf16[8,2048,1024]{2,1,0:T(8,128)(2,1)} %get-tuple-element.631, s32[]{:T(128)} %get-tuple-element.613, s32[]{:T(128)S(6)} %add.301, ...), kind=kLoop, calls=%fused_computation.76.clone.1 | loop fusion | flops 35648512 | bytes 4231176 | tf_op jit(solution)/shard_map/while/body/eval_jaxpr/reduce_sum | solution.py:42
  421.1 57.6 %psum.23 = f32[6,1024]{1,0:T(8,128)S(1)} all-reduce(f32[6,1024]{1,0:T(8,128)S(1)} %stack.98), channel_id=1, replica_groups=mesh['groups'=2,'chan'=16] {'chan'}, use_global_device_ids=true, to_apply=%region_37.38 | all-reduce | flops 6144 | bytes 49152 | tf_op jit(solution)/shard_map/psum | solution.py:120
  (171 shorter events, 75.5 us)
Async XLA Ops:
  0.6 11.7 %copy-start = (s32[1024]{0:T(1024)S(1)}, s32[1024]{0:T(1024)}, u32[]{:S(2)}) copy-start(s32[1024]{0:T(1024)} %param.12) | copy-start | bytes 12292
  0.6 11.7 %copy-start.1 = (s32[8]{0:T(128)S(1)}, s32[8]{0:T(128)}, u32[]{:S(2)}) copy-start(s32[8]{0:T(128)} %param.13) | copy-start | bytes 100
  4.9 48.5 %all-to-all-start = ((bf16[64,16,8,128]{3,0,2,1:T(8,128)(2,1)}), bf16[64,16,8,128]{3,0,2,1:T(8,128)(2,1)S(1)}, u32[]{:S(2)}, u32[]{:S(2)}) async-start(bf16[64,16,8,128]{3,0,2,1:T(8,128)(2,1)} %bitcast.138), calls=%async_computation | async-start | bytes 4194304 | tf_op jit(solution)/shard_map/all_to_all | solution.py:98
where the time goes:
time: 481 us; the launch traced here: 480 us
  other arithmetic  185 us (38%)
  blocking collectives  183 us (38%)
  waiting for transfers between devices  41 us (9%)
  local copies, waits for them, and re-layouts  29.6 us (6%)
  matrix products  25.7 us (5%)
  loops' own time  7.76 us (2%)
  starting transfers between devices  7.39 us (2%)
    psum x3, blocking collectives, local(): totals = lax.psum(partial_sums, 'chan')  183 us
    reduce_sum x24, other arithmetic, channel_normal_terms(): jnp.sum(robust_weighting * prod_im, axis=1)  171 us
    all_to_all x1, waiting for transfers between devices, local(): lax.all_to_all(blocks, 'chan', split_axis=1, concat_axis=0, tiled=True)  41 us
    dot_general x8, matrix products, one_channel(): lax.dot_general(stacked, channel_rows, (((1,), (1,)), ((), ())), preferre...  25.7 us
    dynamic_slice x24, local copies, waits for them, and re-layouts, local(): lax.map(per_channel, (visibilities, angular_frequency))  15.1 us
    mul x16, other arithmetic, channel_normal_terms(): model_re = gain_parameters[0] * jnp.cos(angles)  11.2 us
  transfers between devices with their start and end apart: 1, of which 1 were waited for; matrix products, arithmetic and copies ran while one was open for 0% of the time, Pallas kernels for 0%

commit v1 on v0

v1 whole, which is shorter than its diff:
```python
import math

import jax
import jax.numpy as jnp
from jax import lax
from jax.experimental import pallas as pl
from jax.experimental.pallas import tpu as pltpu
from jax.sharding import PartitionSpec as P

ITERS = 3
TILE = 128
VMEM_LIMIT = 48 * 1024 * 1024

huber_scale = 0.25
damping = 0.5


def solve_update(gains, sums):
    determinant = jnp.maximum(sums[3] * sums[5] - sums[4] * sums[4], 1.0)
    step_phase = (sums[5] * sums[1] - sums[4] * sums[2]) / determinant
    step_delay = (sums[3] * sums[2] - sums[4] * sums[1]) / determinant
    amplitude = gains[0] * (1.0 + damping * (sums[0] - sums[3]) / jnp.maximum(sums[3], 1.0))
    return jnp.concatenate(
        [amplitude, gains[1] + damping * step_phase, gains[2] + damping * step_delay], axis=0
    )


def rows_of(ref, count):
    return [ref[k : k + 1, :] for k in range(count)]


def group_rows(tile_row, tiles):
    return 32 if tiles - tile_row > 4 else (64 if tiles - tile_row > 2 else TILE)


def pair_sums(c, tiles, load_vis, row_terms, col_terms, terms, cols_ref, rows_ref):
    cols_ref[...] = jnp.zeros_like(cols_ref)
    for ti in range(tiles):
        group = group_rows(ti, tiles)

        def body(g, carry, ti=ti, group=group):
            first_row = pl.multiple_of(g * group, group)
            row = pl.multiple_of(ti * TILE + first_row, group)
            row_fac = row_terms(row, group)
            totals = None
            for tj in range(ti, tiles):
                vis_re, vis_im = load_vis(ti, tj, first_row, group)
                keep = None
                if tj == ti:
                    ids = lax.broadcasted_iota(jnp.int32, (group, TILE), 0) + first_row
                    keep = ids != lax.broadcasted_iota(jnp.int32, (group, TILE), 1)
                got = terms(vis_re, vis_im, row_fac, col_terms(tj), keep)
                totals = got if totals is None else [a + b for a, b in zip(totals, got)]
                if tj > ti:
                    for k in range(3):
                        part = got[k].reshape(group // 8, 8, TILE).sum(axis=0)
                        at = pl.ds(tj * TILE, TILE)
                        cols_ref[k, :, at] += part if k != 1 else -part
            lanes = lax.broadcasted_iota(jnp.int32, (group, TILE), 1)
            kept = rows_ref[pl.ds(row, group), :]
            for k in range(3):
                kept = jnp.where(lanes == 8 * k + c, jnp.sum(totals[k], axis=1, keepdims=True), kept)
            rows_ref[pl.ds(row, group), :] = kept
            return carry

        lax.fori_loop(0, TILE // group, body, 0)


def store_cols(c, cols_ref, colsum_ref):
    for k in range(3):
        colsum_ref[c, k : k + 1, :] = jnp.sum(cols_ref[k], axis=0, keepdims=True)


def channel_totals(tiles, rows_ref, colsum_ref):
    turned = [rows_ref[t * TILE : (t + 1) * TILE, :].T for t in range(tiles)]
    chans = colsum_ref.shape[0]
    return [
        jnp.concatenate([t[8 * k : 8 * k + chans] for t in turned], axis=1) + colsum_ref[:, k, :]
        for k in range(3)
    ]


def store_sums(totals, weight, freq, sums_ref):
    prod_re, prod_im, curvature = totals
    wim = weight * prod_im
    wcu = weight * curvature
    sums_ref[...] = jnp.concatenate(
        [
            jnp.sum(x, axis=0, keepdims=True)
            for x in (weight * prod_re, wim, freq * wim, wcu, freq * wcu, freq * freq * wcu)
        ],
        axis=0,
    )


def off_diagonal(ti, tj, tiles):
    return sum(tiles - t for t in range(ti)) + tj - ti


def first_kernel(mask_ref, weight_ref, freq_ref, x_ref, vis_ref, sums_ref,
                 wide_ref, chan_ref, swap_ref, maskrow_ref, cols_ref, rows_ref, colsum_ref):
    c = pl.program_id(0)
    inputs, chans, width = x_ref.shape
    tiles = inputs // TILE
    half = width // 2

    @pl.when(c == 0)
    def _():
        rows_ref[...] = jnp.zeros_like(rows_ref)
        for t in range(tiles):
            block = x_ref[t * TILE : (t + 1) * TILE].astype(jnp.float32)
            wide_ref[pl.ds(t * TILE * chans, TILE * chans), :] = block.reshape(TILE * chans, width)
            wide = jnp.broadcast_to(mask_ref[:, t * TILE : (t + 1) * TILE], (TILE, TILE))
            maskrow_ref[t * TILE : (t + 1) * TILE, :] = wide.T

    for t in range(tiles):
        rows = wide_ref[pl.ds(t * TILE * chans + c, TILE, stride=chans), :]
        chan_ref[t * TILE : (t + 1) * TILE, :] = rows.astype(jnp.bfloat16)
        turned = pltpu.roll(rows, half, 1)
        lanes = lax.broadcasted_iota(jnp.int32, rows.shape, 1)
        swap_ref[t * TILE : (t + 1) * TILE, :] = jnp.where(lanes < half, turned, -turned).astype(
            jnp.bfloat16
        )

    for ti in range(tiles):
        right = chan_ref[ti * TILE :, :]
        for part, left_ref in enumerate((chan_ref, swap_ref)):
            left = left_ref[ti * TILE : (ti + 1) * TILE, :]
            product = lax.dot_general(
                left, right, (((1,), (1,)), ((), ())), preferred_element_type=jnp.float32
            )
            scaled = (product * (1.0 / half)).astype(jnp.bfloat16)
            for tj in range(ti, tiles):
                at = (tj - ti) * TILE
                vis_ref[0, off_diagonal(ti, tj, tiles), part] = scaled[:, at : at + TILE]

    def load_vis(ti, tj, first_row, group):
        k = off_diagonal(ti, tj, tiles)
        return [vis_ref[0, k, p, pl.ds(first_row, group), :].astype(jnp.float32) for p in (0, 1)]

    def row_terms(row, group):
        return maskrow_ref[pl.ds(row, group), :]

    def col_terms(tj):
        return mask_ref[:, tj * TILE : (tj + 1) * TILE]

    def terms(vis_re, vis_im, row_mask, col_mask, keep):
        off = vis_re - 1.0
        weight = row_mask * col_mask
        if keep is not None:
            weight = jnp.where(keep, weight, 0.0)
        robust = weight / (1.0 + (off * off + vis_im * vis_im) * (1.0 / huber_scale))
        return [robust * vis_re, robust * vis_im, robust]

    pair_sums(c, tiles, load_vis, row_terms, col_terms, terms, cols_ref, rows_ref)
    store_cols(c, cols_ref, colsum_ref)

    @pl.when(c == pl.num_programs(0) - 1)
    def _():
        totals = channel_totals(tiles, rows_ref, colsum_ref)
        store_sums(totals, weight_ref[...], freq_ref[...], sums_ref)


def next_kernel(gains_ref, old_ref, mask_ref, weight_ref, freq_ref, vis_ref,
                sums_ref, new_ref, fit_ref,
                model_ref, rowfac_ref, cols_ref, rows_ref, colsum_ref):
    c = pl.program_id(0)
    inputs = mask_ref.shape[1]
    tiles = inputs // TILE

    @pl.when(c == 0)
    def _():
        rows_ref[...] = jnp.zeros_like(rows_ref)
        gains = solve_update(rows_of(gains_ref, 3), rows_of(old_ref, 6))
        new_ref[...] = gains
        angles = gains[1:2] + freq_ref[...] * gains[2:3]
        amplitude = gains[0:1] * mask_ref[...]
        model_ref[:, 0, :] = amplitude * jnp.cos(angles)
        model_ref[:, 1, :] = amplitude * jnp.sin(angles)
        model_ref[:, 2, :] = jnp.broadcast_to(amplitude * amplitude, angles.shape)

    for k in range(3):
        for t in range(tiles):
            fac = model_ref[c, k : k + 1, t * TILE : (t + 1) * TILE]
            rowfac_ref[k, t * TILE : (t + 1) * TILE, :] = jnp.broadcast_to(fac, (TILE, TILE)).T

    def load_vis(ti, tj, first_row, group):
        k = off_diagonal(ti, tj, tiles)
        return [vis_ref[0, k, p, pl.ds(first_row, group), :].astype(jnp.float32) for p in (0, 1)]

    def row_terms(row, group):
        return [rowfac_ref[k, pl.ds(row, group), :] for k in range(3)]

    def col_terms(tj):
        return [model_ref[c, k : k + 1, tj * TILE : (tj + 1) * TILE] for k in range(3)]

    def terms(vis_re, vis_im, row_fac, col_fac, keep):
        pair_re = row_fac[0] * col_fac[0] + row_fac[1] * col_fac[1]
        pair_im = row_fac[1] * col_fac[0] - row_fac[0] * col_fac[1]
        off_re = vis_re - pair_re
        off_im = vis_im - pair_im
        robust = 1.0 / (1.0 + (off_re * off_re + off_im * off_im) * (1.0 / huber_scale))
        if keep is not None:
            robust = jnp.where(keep, robust, 0.0)
        return [
            robust * (vis_re * pair_re + vis_im * pair_im),
            robust * (vis_im * pair_re - vis_re * pair_im),
            robust * (row_fac[2] * col_fac[2]),
        ]

    pair_sums(c, tiles, load_vis, row_terms, col_terms, terms, cols_ref, rows_ref)
    store_cols(c, cols_ref, colsum_ref)

    @pl.when(c == pl.num_programs(0) - 1)
    def _():
        totals = channel_totals(tiles, rows_ref, colsum_ref)
        store_sums(totals, weight_ref[...], freq_ref[...], sums_ref)
        bound = jnp.maximum(totals[2], 1.0)
        fit_ref[0] = totals[0] / bound
        fit_ref[1] = totals[1] / bound


def whole(shape):
    return pl.BlockSpec(shape, lambda c: (0,) * len(shape))


def first_iteration(x, mask, weight, freq):
    inputs, chans, width = x.shape
    tiles = inputs // TILE
    blocks = tiles * (tiles + 1) // 2
    return pl.pallas_call(
        first_kernel,
        grid=(chans,),
        in_specs=[whole(mask.shape), whole(weight.shape), whole(freq.shape), whole(x.shape)],
        out_specs=[
            pl.BlockSpec((1, blocks, 2, TILE, TILE), lambda c: (c, 0, 0, 0, 0)),
            whole((6, inputs)),
        ],
        out_shape=[
            jax.ShapeDtypeStruct((chans, blocks, 2, TILE, TILE), jnp.bfloat16),
            jax.ShapeDtypeStruct((6, inputs), jnp.float32),
        ],
        scratch_shapes=[
            pltpu.VMEM((inputs * chans, width), jnp.float32),
            pltpu.VMEM((inputs, width), jnp.bfloat16),
            pltpu.VMEM((inputs, width), jnp.bfloat16),
            pltpu.VMEM((inputs, TILE), jnp.float32),
            pltpu.VMEM((3, 8, inputs), jnp.float32),
            pltpu.VMEM((inputs, TILE), jnp.float32),
            pltpu.VMEM((chans, 8, inputs), jnp.float32),
        ],
        compiler_params=pltpu.CompilerParams(vmem_limit_bytes=VMEM_LIMIT),
        name="first_iteration",
    )(mask, weight, freq, x)


def next_iteration(gains, old_sums, mask, weight, freq, vis):
    chans, blocks = vis.shape[:2]
    inputs = mask.shape[1]
    return pl.pallas_call(
        next_kernel,
        grid=(chans,),
        in_specs=[
            whole(gains.shape), whole(old_sums.shape), whole(mask.shape), whole(weight.shape),
            whole(freq.shape),
            pl.BlockSpec((1, blocks, 2, TILE, TILE), lambda c: (c, 0, 0, 0, 0)),
        ],
        out_specs=[whole((6, inputs)), whole((3, inputs)), whole((2, chans, inputs))],
        out_shape=[
            jax.ShapeDtypeStruct((6, inputs), jnp.float32),
            jax.ShapeDtypeStruct((3, inputs), jnp.float32),
            jax.ShapeDtypeStruct((2, chans, inputs), jnp.float32),
        ],
        scratch_shapes=[
            pltpu.VMEM((chans, 8, inputs), jnp.float32),
            pltpu.VMEM((3, inputs, TILE), jnp.float32),
            pltpu.VMEM((3, 8, inputs), jnp.float32),
            pltpu.VMEM((inputs, TILE), jnp.float32),
            pltpu.VMEM((chans, 8, inputs), jnp.float32),
        ],
        compiler_params=pltpu.CompilerParams(vmem_limit_bytes=VMEM_LIMIT),
        name="next_iteration",
    )(gains, old_sums, mask, weight, freq, vis)


def all_sum(part, devices):
    if devices & (devices - 1):
        return lax.psum(part, "chan")
    reach = 1
    while reach < devices:
        ways = 4 if devices // reach >= 4 else 2
        got = [part] + [
            lax.ppermute(part, "chan", [(i, i ^ (k * reach)) for i in range(devices)])
            for k in range(1, ways)
        ]
        part = (got[0] + got[1]) + (got[2] + got[3]) if ways == 4 else got[0] + got[1]
        reach *= ways
    return part


def local(voltages, antenna_usable_mask, channel_flags):
    devices = lax.axis_size("chan")
    inputs_dev, channels, sample_cols = voltages.shape
    chan_dev = channels // devices
    blocks = voltages.reshape(inputs_dev, devices, chan_dev, sample_cols)
    turned = lax.all_to_all(blocks, "chan", split_axis=1, concat_axis=0, tiled=True)
    inputs = inputs_dev * devices
    arrived = turned.reshape(inputs, chan_dev, sample_cols)
    first_channel = lax.axis_index("chan") * chan_dev
    channel_ids = (first_channel + jnp.arange(chan_dev)).astype(jnp.float32)
    freq = (2.0 * math.pi * (channel_ids + 0.5) / (chan_dev * devices))[:, None]
    weight = channel_flags.astype(jnp.float32)[:, None]
    mask = antenna_usable_mask.astype(jnp.float32)[None, :]
    gains = jnp.concatenate(
        [jnp.ones((1, inputs), jnp.float32), jnp.zeros((2, inputs), jnp.float32)], axis=0
    )
    vis, sums = first_iteration(arrived, mask, weight, freq)
    fitted = None
    for iteration in range(1, ITERS):
        sums, gains, fitted = next_iteration(
            gains, all_sum(sums, devices), mask, weight, freq, vis
        )
    totals = all_sum(sums, devices)
    gains = solve_update([gains[k : k + 1] for k in range(3)], [totals[k : k + 1] for k in range(6)])
    return (gains, fitted)


def solution(mesh):
    placed = (P(("groups", "chan"), None, None), P("groups"), P(("groups", "chan")))
    return jax.shard_map(
        local,
        mesh=mesh,
        in_specs=placed,
        out_specs=(P(None, "groups"), P(None, ("groups", "chan"), None)),
        check_vma=False,
    )
```

time: 481 us -> 212 us (0.44)
  other arithmetic: 185 us -> 0.74 us
  blocking collectives: 183 us -> 0 us
  Pallas kernels: 0 us -> 117 us
  local copies, waits for them, and re-layouts: 29.6 us -> 3.56 us
  matrix products: 25.7 us -> 0 us
  starting transfers between devices: 7.39 us -> 31.3 us
  waiting for transfers between devices: 41 us -> 58.8 us
  loops' own time: 7.76 us -> 0 us
    psum x3 -> x0, blocking collectives: 183 us -> none  [local(): totals = lax.psum(partial_sums, 'chan')]
    reduce_sum x27 -> x0, other arithmetic: 171 us -> none  [the longest x24 171 us: channel_normal_terms(): jnp.sum(robust_weighting * prod_im, axis=1)]
    pallas_call x0 -> x3, Pallas kernels: none -> 117 us  [the longest x2 80 us: next_iteration(): pl.pallas_call(next_kernel, grid=(chans,), in_specs=[whole(gains.shape),...]
    dot_general x8 -> x0, matrix products: 25.7 us -> none  [one_channel(): lax.dot_general(stacked, channel_rows, (((1,), (1,)), ((), ())), preferre...]
    ppermute x0 -> x18, starting transfers between devices: none -> 23.8 us  [all_sum(): lax.ppermute(part, 'chan', [(i, i ^ k * reach) for i in range(devices)])]
    ppermute x0 -> x18, waiting for transfers between devices: none -> 17.9 us  [all_sum(): lax.ppermute(part, 'chan', [(i, i ^ k * reach) for i in range(devices)])]
    dynamic_slice x24 -> x0, local copies, waits for them, and re-layouts: 15.1 us -> none  [local(): lax.map(per_channel, (visibilities, angular_frequency))]
    mul x21 -> x1, other arithmetic: 11.3 us -> 0.05 us  [solve_update(): gains[0] * (1.0 + damping * (sums[0] - sums[3]) / jnp.maximum(sums[3], 1.0))]
  transfers between devices with their start and end apart: 1 -> 19, of which waited for: 1 -> 14; matrix products, arithmetic and copies ran while one was open for 0% -> 0% of each run, Pallas kernels for 0% -> 0%
where the time goes in v1:
time: 212 us
  Pallas kernels  117 us (55%)
  waiting for transfers between devices  58.8 us (28%)
  starting transfers between devices  31.3 us (15%)
  local copies, waits for them, and re-layouts  3.56 us (2%)
    pallas_call x2, Pallas kernels, next_iteration(): pl.pallas_call(next_kernel, grid=(chans,), in_specs=[whole(gains.shape),...  80 us
    all_to_all x1, waiting for transfers between devices, local(): lax.all_to_all(blocks, 'chan', split_axis=1, concat_axis=0, tiled=True)  41 us
    pallas_call x1, Pallas kernels, first_iteration(): pl.pallas_call(first_kernel, grid=(chans,), in_specs=[whole(mask.shape),...  36.5 us
    ppermute x18, starting transfers between devices, all_sum(): lax.ppermute(part, 'chan', [(i, i ^ k * reach) for i in range(devices)])  23.8 us
    ppermute x18, waiting for transfers between devices, all_sum(): lax.ppermute(part, 'chan', [(i, i ^ k * reach) for i in range(devices)])  17.9 us
    all_to_all x1, starting transfers between devices, local(): lax.all_to_all(blocks, 'chan', split_axis=1, concat_axis=0, tiled=True)  7.52 us
  transfers between devices with their start and end apart: 19, of which 14 were waited for; matrix products, arithmetic and copies ran while one was open for 0% of the time, Pallas kernels for 0%

profile of v1, /device:TPU:0, one launch (start us, length us, event | category | flops | bytes accessed | tf_op | source)
XLA Modules:
  0.0 211.7 jit_solution(15014995559918901164)
XLA Ops:
  0.6 3.5 %copy.5 = bf16[64,16,8,128]{3,2,0,1:T(8,128)(2,1)} copy(bf16[64,16,8,128]{3,2,1,0:T(8,128)(2,1)} %bitcast.13) | data formatting | bytes 4194304 | tf_op jit(solution)/shard_map/reshape | solution.py:305
  4.1 7.5 %all-to-all-start = ((bf16[64,16,8,128]{3,2,0,1:T(8,128)(2,1)}), bf16[64,16,8,128]{3,2,0,1:T(8,128)(2,1)S(1)}, u32[]{:S(2)}, u32[]{:S(2)}) async-start(bf16[64,16,8,128]{3,2,0,1:T(8,128)(2,1)} %copy.5), calls=%async_computation | async-start | bytes 4194304 | tf_op jit(solution)/shard_map/all_to_all | solution.py:306
  11.8 41.0 %all-to-all-done = bf16[64,16,8,128]{3,2,0,1:T(8,128)(2,1)S(1)} async-done(((bf16[64,16,8,128]{3,2,0,1:T(8,128)(2,1)}), bf16[64,16,8,128]{3,2,0,1:T(8,128)(2,1)S(1)}, u32[]{:S(2)}, u32[]{:S(2)}) %all-to-all-start) | async-done | bytes 2097184 | tf_op jit(solution)/shard_map/all_to_all | solution.py:306
  52.7 36.5 %first_iteration.1 = (bf16[8,36,2,128,128]{4,3,2,1,0:T(8,128)(2,1)}, f32[6,1024]{1,0:T(8,128)S(1)}) custom-call(f32[1,1024]{1,0:T(1,128)S(1)} %bitcast.10, f32[8,1]{1,0:T(8,128)S(1)} %copy.6.weight_ref, f32[8,1]{1,0:T(8,128)S(1)} %add_multiply_fusion.1.freq_ref, bf16[1024,8,128]{2,1,0:T(8,128)(2,1)S(1)} %bitcast.9), custom_call_target="tpu_custom_call" | custom-call | tf_op jit(solution)/shard_map/first_iteration/pallas_call | solution.py:231
  89.2 3.7 %collective-permute-start.2 = (f32[6,1024]{1,0:T(8,128)S(1)}, f32[6,1024]{1,0:T(8,128)S(1)}, u32[]{:S(2)}, u32[]{:S(2)}) collective-permute-start(f32[6,1024]{1,0:T(8,128)S(1)} %get-tuple-element.9), channel_id=1, source_target_pairs={{0,3},{1,2},{2,1},{3,0},{4,7},{5,6},{6,5},{7,4},{8,11},{9,10},{10,... | collective-permute-start | bytes 73736 | tf_op jit(solution)/shard_map/ppermute | solution.py:293
  93.1 1.7 collective-permute-done.2
  94.9 2.0 collective-permute-done.1
  96.9 6.6 %collective-permute-start.5 = (f32[6,1024]{1,0:T(8,128)S(1)}, f32[6,1024]{1,0:T(8,128)S(1)}, u32[]{:S(2)}, u32[]{:S(2)}) collective-permute-start(f32[6,1024]{1,0:T(8,128)S(1)} %add_add_fusion.5), channel_id=1, source_target_pairs={{0,12},{1,13},{2,14},{3,15},{4,8},{5,9},{6,10},{7,11},{8,4},{9,5},... | collective-permute-start | bytes 73736 | tf_op jit(solution)/shard_map/ppermute | solution.py:293
  103.5 0.6 collective-permute-start.4
  104.2 1.3 collective-permute-done.5
  105.4 3.0 %collective-permute-done.4 = f32[6,1024]{1,0:T(8,128)S(1)} collective-permute-done((f32[6,1024]{1,0:T(8,128)S(1)}, f32[6,1024]{1,0:T(8,128)S(1)}, u32[]{:S(2)}, u32[]{:S(2)}) %collective-permute-start.4) | collective-permute-done | bytes 24608 | tf_op jit(solution)/shard_map/ppermute | solution.py:293
  108.5 40.0 %next_iteration.2 = (f32[6,1024]{1,0:T(8,128)S(1)}, f32[3,1024]{1,0:T(4,128)S(1)}, f32[2,8,1024]{2,1,0:T(8,128)}) custom-call(f32[3,1024]{1,0:T(4,128)S(1)} %copy-done, f32[6,1024]{1,0:T(8,128)S(1)} %add_add_fusion.4.old_ref, f32[1,1024]{1,0:T(1,128)S(1)} %bitcast.11, f32[8,1]{1,0:T(8,128)S(1)} %copy.6.weight_ref, f32[8,1]{1,0:T(8,128)S(1)} %add_multiply_fusion.1.freq_ref, ...), custom_call_target="tpu_custom_call" | custom-call | tf_op jit(solution)/shard_map/next_iteration/pallas_call | solution.py:260
  148.5 0.9 collective-permute-start.7
  149.4 1.0 collective-permute-start.6
  150.3 1.5 collective-permute-done.8
  151.8 0.9 collective-permute-done.7
  152.7 1.2 collective-permute-start.11
  154.0 0.6 collective-permute-start.10
  154.6 2.6 %collective-permute-start.9 = (f32[6,1024]{1,0:T(8,128)S(1)}, f32[6,1024]{1,0:T(8,128)S(1)}, u32[]{:S(2)}, u32[]{:S(2)}) collective-permute-start(f32[6,1024]{1,0:T(8,128)S(1)} %add_add_fusion.3), channel_id=1, source_target_pairs={{0,4},{1,5},{2,6},{3,7},{4,0},{5,1},{6,2},{7,3},{8,12},{9,13},{10,... | collective-permute-start | bytes 73736 | tf_op jit(solution)/shard_map/ppermute | solution.py:293
  157.2 1.4 collective-permute-done.11
  158.6 0.8 collective-permute-done.10
  159.4 40.0 %next_iteration.3 = (f32[6,1024]{1,0:T(8,128)S(1)}, f32[3,1024]{1,0:T(4,128)S(1)}, f32[2,8,1024]{2,1,0:T(8,128)}) custom-call(f32[3,1024]{1,0:T(4,128)S(1)} %get-tuple-element.11.gains_ref, f32[6,1024]{1,0:T(8,128)S(1)} %add_add_fusion.2.old_ref, f32[1,1024]{1,0:T(1,128)S(1)} %bitcast.12, f32[8,1]{1,0:T(8,128)S(1)} %copy.6.weight_ref, ...), custom_call_target="tpu_custom_call" | custom-call | tf_op jit(solution)/shard_map/next_iteration/pallas_call | solution.py:260
  199.8 0.8 collective-permute-start.13
  200.6 0.7 collective-permute-start.12
  201.3 1.6 collective-permute-done.14
  202.9 0.9 collective-permute-done.13
  203.8 2.1 collective-permute-start.17
  205.9 0.8 collective-permute-start.16
  206.7 1.6 collective-permute-start.15
  208.3 1.3 collective-permute-done.17
  209.6 1.2 collective-permute-done.16
  211.1 0.6 pad_maximum_fusion
  (28 shorter events, 1.0 us)
Async XLA Ops:
  4.1 7.5 %copy-start.2 = (s32[8]{0:T(128)S(1)}, s32[8]{0:T(128)}, u32[]{:S(2)}) copy-start(s32[8]{0:T(128)} %param.5) | copy-start | bytes 100
  4.1 7.6 %copy-start.1 = (s32[1024]{0:T(1024)S(1)}, s32[1024]{0:T(1024)}, u32[]{:S(2)}) copy-start(s32[1024]{0:T(1024)} %param.4) | copy-start | bytes 12292
  4.1 48.6 %all-to-all-start = ((bf16[64,16,8,128]{3,2,0,1:T(8,128)(2,1)}), bf16[64,16,8,128]{3,2,0,1:T(8,128)(2,1)S(1)}, u32[]{:S(2)}, u32[]{:S(2)}) async-start(bf16[64,16,8,128]{3,2,0,1:T(8,128)(2,1)} %copy.5), calls=%async_computation | async-start | bytes 4194304 | tf_op jit(solution)/shard_map/all_to_all | solution.py:306
  11.6 96.8 %copy-start = (f32[3,1024]{1,0:T(4,128)S(1)}, f32[3,1024]{1,0:T(4,128)}, u32[]{:S(2)}) copy-start(f32[3,1024]{1,0:T(4,128)} %constant.6.clone.1.gains_ref) | copy-start | bytes 36868
  89.2 5.6 %collective-permute-start.2 = (f32[6,1024]{1,0:T(8,128)S(1)}, f32[6,1024]{1,0:T(8,128)S(1)}, u32[]{:S(2)}, u32[]{:S(2)}) collective-permute-start(f32[6,1024]{1,0:T(8,128)S(1)} %get-tuple-element.9), channel_id=1, source_target_pairs={{0,3},{1,2},{2,1},{3,0},{4,7},{5,6},{6,5},{7,4},{8,11},{9,10},{10,... | collective-permute-start | bytes 73736 | tf_op jit(solution)/shard_map/ppermute | solution.py:293
  93.0 3.9 %collective-permute-start.1 = (f32[6,1024]{1,0:T(8,128)S(1)}, f32[6,1024]{1,0:T(8,128)S(1)}, u32[]{:S(2)}, u32[]{:S(2)}) collective-permute-start(f32[6,1024]{1,0:T(8,128)S(1)} %get-tuple-element.9), channel_id=1, source_target_pairs={{0,2},{1,3},{2,0},{3,1},{4,6},{5,7},{6,4},{7,5},{8,10},{9,11},{10,... | collective-permute-start | bytes 73736 | tf_op jit(solution)/shard_map/ppermute | solution.py:293
  93.0 3.9 %collective-permute-start = (f32[6,1024]{1,0:T(8,128)S(1)}, f32[6,1024]{1,0:T(8,128)S(1)}, u32[]{:S(2)}, u32[]{:S(2)}) collective-permute-start(f32[6,1024]{1,0:T(8,128)S(1)} %get-tuple-element.9), channel_id=1, source_target_pairs={{0,1},{1,0},{2,3},{3,2},{4,5},{5,4},{6,7},{7,6},{8,9},{9,8},{10,11... | collective-permute-start | bytes 73736 | tf_op jit(solution)/shard_map/ppermute | solution.py:293
  96.9 8.5 %collective-permute-start.5 = (f32[6,1024]{1,0:T(8,128)S(1)}, f32[6,1024]{1,0:T(8,128)S(1)}, u32[]{:S(2)}, u32[]{:S(2)}) collective-permute-start(f32[6,1024]{1,0:T(8,128)S(1)} %add_add_fusion.5), channel_id=1, source_target_pairs={{0,12},{1,13},{2,14},{3,15},{4,8},{5,9},{6,10},{7,11},{8,4},{9,5},... | collective-permute-start | bytes 73736 | tf_op jit(solution)/shard_map/ppermute | solution.py:293
  103.5 4.9 %collective-permute-start.4 = (f32[6,1024]{1,0:T(8,128)S(1)}, f32[6,1024]{1,0:T(8,128)S(1)}, u32[]{:S(2)}, u32[]{:S(2)}) collective-permute-start(f32[6,1024]{1,0:T(8,128)S(1)} %add_add_fusion.5), channel_id=1, source_target_pairs={{0,8},{1,9},{2,10},{3,11},{4,12},{5,13},{6,14},{7,15},{8,0},{9,1},... | collective-permute-start | bytes 73736 | tf_op jit(solution)/shard_map/ppermute | solution.py:293
  104.2 4.3 %collective-permute-start.3 = (f32[6,1024]{1,0:T(8,128)S(1)}, f32[6,1024]{1,0:T(8,128)S(1)}, u32[]{:S(2)}, u32[]{:S(2)}) collective-permute-start(f32[6,1024]{1,0:T(8,128)S(1)} %add_add_fusion.5), channel_id=1, source_target_pairs={{0,4},{1,5},{2,6},{3,7},{4,0},{5,1},{6,2},{7,3},{8,12},{9,13},{10,... | collective-permute-start | bytes 73736 | tf_op jit(solution)/shard_map/ppermute | solution.py:293
  148.5 3.3 %collective-permute-start.8 = (f32[6,1024]{1,0:T(8,128)S(1)}, f32[6,1024]{1,0:T(8,128)S(1)}, u32[]{:S(2)}, u32[]{:S(2)}) collective-permute-start(f32[6,1024]{1,0:T(8,128)S(1)} %get-tuple-element.12), channel_id=1, source_target_pairs={{0,3},{1,2},{2,1},{3,0},{4,7},{5,6},{6,5},{7,4},{8,11},{9,10},{10,... | collective-permute-start | bytes 73736 | tf_op jit(solution)/shard_map/ppermute | solution.py:293
  148.5 4.3 %collective-permute-start.7 = (f32[6,1024]{1,0:T(8,128)S(1)}, f32[6,1024]{1,0:T(8,128)S(1)}, u32[]{:S(2)}, u32[]{:S(2)}) collective-permute-start(f32[6,1024]{1,0:T(8,128)S(1)} %get-tuple-element.12), channel_id=1, source_target_pairs={{0,2},{1,3},{2,0},{3,1},{4,6},{5,7},{6,4},{7,5},{8,10},{9,11},{10,... | collective-permute-start | bytes 73736 | tf_op jit(solution)/shard_map/ppermute | solution.py:293
  149.4 3.4 %collective-permute-start.6 = (f32[6,1024]{1,0:T(8,128)S(1)}, f32[6,1024]{1,0:T(8,128)S(1)}, u32[]{:S(2)}, u32[]{:S(2)}) collective-permute-start(f32[6,1024]{1,0:T(8,128)S(1)} %get-tuple-element.12), channel_id=1, source_target_pairs={{0,1},{1,0},{2,3},{3,2},{4,5},{5,4},{6,7},{7,6},{8,9},{9,8},{10,11... | collective-permute-start | bytes 73736 | tf_op jit(solution)/shard_map/ppermute | solution.py:293
  152.7 5.8 %collective-permute-start.11 = (f32[6,1024]{1,0:T(8,128)S(1)}, f32[6,1024]{1,0:T(8,128)S(1)}, u32[]{:S(2)}, u32[]{:S(2)}) collective-permute-start(f32[6,1024]{1,0:T(8,128)S(1)} %add_add_fusion.3), channel_id=1, source_target_pairs={{0,12},{1,13},{2,14},{3,15},{4,8},{5,9},{6,10},{7,11},{8,4},{9,5},... | collective-permute-start | bytes 73736 | tf_op jit(solution)/shard_map/ppermute | solution.py:293
  154.0 5.4 %collective-permute-start.10 = (f32[6,1024]{1,0:T(8,128)S(1)}, f32[6,1024]{1,0:T(8,128)S(1)}, u32[]{:S(2)}, u32[]{:S(2)}) collective-permute-start(f32[6,1024]{1,0:T(8,128)S(1)} %add_add_fusion.3), channel_id=1, source_target_pairs={{0,8},{1,9},{2,10},{3,11},{4,12},{5,13},{6,14},{7,15},{8,0},{9,1},... | collective-permute-start | bytes 73736 | tf_op jit(solution)/shard_map/ppermute | solution.py:293
  154.6 4.8 %collective-permute-start.9 = (f32[6,1024]{1,0:T(8,128)S(1)}, f32[6,1024]{1,0:T(8,128)S(1)}, u32[]{:S(2)}, u32[]{:S(2)}) collective-permute-start(f32[6,1024]{1,0:T(8,128)S(1)} %add_add_fusion.3), channel_id=1, source_target_pairs={{0,4},{1,5},{2,6},{3,7},{4,0},{5,1},{6,2},{7,3},{8,12},{9,13},{10,... | collective-permute-start | bytes 73736 | tf_op jit(solution)/shard_map/ppermute | solution.py:293
  199.4 3.4 %collective-permute-start.14 = (f32[6,1024]{1,0:T(8,128)S(1)}, f32[6,1024]{1,0:T(8,128)S(1)}, u32[]{:S(2)}, u32[]{:S(2)}) collective-permute-start(f32[6,1024]{1,0:T(8,128)S(1)} %get-tuple-element.14), channel_id=1, source_target_pairs={{0,3},{1,2},{2,1},{3,0},{4,7},{5,6},{6,5},{7,4},{8,11},{9,10},{10,... | collective-permute-start | bytes 73736 | tf_op jit(solution)/shard_map/ppermute | solution.py:293
  199.8 4.0 %collective-permute-start.13 = (f32[6,1024]{1,0:T(8,128)S(1)}, f32[6,1024]{1,0:T(8,128)S(1)}, u32[]{:S(2)}, u32[]{:S(2)}) collective-permute-start(f32[6,1024]{1,0:T(8,128)S(1)} %get-tuple-element.14), channel_id=1, source_target_pairs={{0,2},{1,3},{2,0},{3,1},{4,6},{5,7},{6,4},{7,5},{8,10},{9,11},{10,... | collective-permute-start | bytes 73736 | tf_op jit(solution)/shard_map/ppermute | solution.py:293
  200.6 3.2 %collective-permute-start.12 = (f32[6,1024]{1,0:T(8,128)S(1)}, f32[6,1024]{1,0:T(8,128)S(1)}, u32[]{:S(2)}, u32[]{:S(2)}) collective-permute-start(f32[6,1024]{1,0:T(8,128)S(1)} %get-tuple-element.14), channel_id=1, source_target_pairs={{0,1},{1,0},{2,3},{3,2},{4,5},{5,4},{6,7},{7,6},{8,9},{9,8},{10,11... | collective-permute-start | bytes 73736 | tf_op jit(solution)/shard_map/ppermute | solution.py:293
  203.8 5.8 %collective-permute-start.17 = (f32[6,1024]{1,0:T(8,128)S(1)}, f32[6,1024]{1,0:T(8,128)S(1)}, u32[]{:S(2)}, u32[]{:S(2)}) collective-permute-start(f32[6,1024]{1,0:T(8,128)S(1)} %add_add_fusion.1), channel_id=1, source_target_pairs={{0,12},{1,13},{2,14},{3,15},{4,8},{5,9},{6,10},{7,11},{8,4},{9,5},... | collective-permute-start | bytes 73736 | tf_op jit(solution)/shard_map/ppermute | solution.py:293
  205.9 4.9 %collective-permute-start.16 = (f32[6,1024]{1,0:T(8,128)S(1)}, f32[6,1024]{1,0:T(8,128)S(1)}, u32[]{:S(2)}, u32[]{:S(2)}) collective-permute-start(f32[6,1024]{1,0:T(8,128)S(1)} %add_add_fusion.1), channel_id=1, source_target_pairs={{0,8},{1,9},{2,10},{3,11},{4,12},{5,13},{6,14},{7,15},{8,0},{9,1},... | collective-permute-start | bytes 73736 | tf_op jit(solution)/shard_map/ppermute | solution.py:293
  206.7 4.3 %collective-permute-start.15 = (f32[6,1024]{1,0:T(8,128)S(1)}, f32[6,1024]{1,0:T(8,128)S(1)}, u32[]{:S(2)}, u32[]{:S(2)}) collective-permute-start(f32[6,1024]{1,0:T(8,128)S(1)} %add_add_fusion.1), channel_id=1, source_target_pairs={{0,4},{1,5},{2,6},{3,7},{4,0},{5,1},{6,2},{7,3},{8,12},{9,13},{10,... | collective-permute-start | bytes 73736 | tf_op jit(solution)/shard_map/ppermute | solution.py:293

commit v2 on v1

v2 whole, which is shorter than its diff:
```python
import math

import jax
import jax.numpy as jnp
from jax import lax
from jax.experimental import pallas as pl
from jax.experimental.pallas import tpu as pltpu
from jax.sharding import PartitionSpec as P

ITERS = 3
TILE = 128
GROUP = 16
UNIT = 16
PARTS = 2
AHEAD = 1
HUGE = 1e38
VMEM_LIMIT = 20 * 1024 * 1024

huber_scale = 0.25
damping = 0.5


def solve_update(gains, sums):
    determinant = jnp.maximum(sums[3] * sums[5] - sums[4] * sums[4], 1.0)
    step_phase = (sums[5] * sums[1] - sums[4] * sums[2]) / determinant
    step_delay = (sums[3] * sums[2] - sums[4] * sums[1]) / determinant
    amplitude = gains[0] * (1.0 + damping * (sums[0] - sums[3]) / jnp.maximum(sums[3], 1.0))
    return jnp.concatenate(
        [amplitude, gains[1] + damping * step_phase, gains[2] + damping * step_delay], axis=0
    )


def rows_of(ref, count):
    return [ref[k : k + 1, :] for k in range(count)]


def places(tiles):
    out = {}
    for part, rows in enumerate(tile_parts(tiles)):
        pairs = [(ti, tj) for ti in rows for tj in range(ti, tiles)]
        out.update({pair: (part, k) for k, pair in enumerate(pairs)})
    return out


def part_size(tiles):
    return max(k for _, k in places(tiles).values()) + 1


def drain(jobs):
    for _ in jobs:
        pass


def pair_sums(c, rows, tiles, terms, ahead, cols_ref, acc_ref, rows_ref):
    for ti in rows:
        for first in range(0, TILE, GROUP):
            for _ in range(AHEAD):
                next(ahead, None)
            row = ti * TILE + first
            totals = [None] * (GROUP // UNIT)
            for tj in range(ti, tiles):
                parts = None
                for unit in range(GROUP // UNIT):
                    at = first + unit * UNIT
                    keep = None
                    if tj == ti:
                        ids = lax.broadcasted_iota(jnp.int32, (UNIT, TILE), 0) + at
                        keep = ids != lax.broadcasted_iota(jnp.int32, (UNIT, TILE), 1)
                    got = terms(ti, tj, at, keep)
                    if totals[unit] is None:
                        totals[unit] = got
                    else:
                        totals[unit] = [a + b for a, b in zip(totals[unit], got)]
                    if tj > ti:
                        part = [x.reshape(UNIT // 8, 8, TILE).sum(axis=0) for x in got]
                        parts = part if parts is None else [a + b for a, b in zip(parts, part)]
                if tj > ti:
                    lanes = slice(tj * TILE, (tj + 1) * TILE)
                    for k in range(3):
                        cols_ref[k, :, lanes] += parts[k] if k != 1 else -parts[k]
            fold_rows(c - 1, row, GROUP, acc_ref, rows_ref)
            for unit in range(GROUP // UNIT):
                for k in range(3):
                    acc_ref[k, row + unit * UNIT : row + (unit + 1) * UNIT, :] = totals[unit][k]
    drain(ahead)


def tile_parts(tiles):
    order = [r for p in range((tiles + 1) // 2) for r in sorted({p, tiles - 1 - p})]
    size = -(-len(order) // PARTS)
    return [order[k : k + size] for k in range(0, len(order), size)]


def fold_rows(c, row, count, acc_ref, rows_ref):
    lanes = lax.broadcasted_iota(jnp.int32, (count, TILE), 1)
    kept = rows_ref[row : row + count, :]
    for k in range(3):
        total = jnp.sum(acc_ref[k, row : row + count, :], axis=1, keepdims=True)
        kept = jnp.where(lanes == 8 * k + c, total, kept)
    rows_ref[row : row + count, :] = kept


def store_cols(c, cols_ref, colsum_ref):
    for k in range(3):
        colsum_ref[c, k : k + 1, :] = jnp.sum(cols_ref[k], axis=0, keepdims=True)


def channel_totals(tiles, rows_ref, colsum_ref, scales):
    turned = [rows_ref[t * TILE : (t + 1) * TILE, :].T for t in range(tiles)]
    chans = colsum_ref.shape[0]
    return [
        scales[k]
        * (jnp.concatenate([t[8 * k : 8 * k + chans] for t in turned], axis=1) + colsum_ref[:, k, :])
        for k in range(3)
    ]


def store_sums(totals, weight, freq, sums_ref):
    prod_re, prod_im, curvature = totals
    wim = weight * prod_im
    wcu = weight * curvature
    sums_ref[...] = jnp.concatenate(
        [
            jnp.sum(x, axis=0, keepdims=True)
            for x in (weight * prod_re, wim, freq * wim, wcu, freq * wcu, freq * freq * wcu)
        ],
        axis=0,
    )


def first_kernel(mask_ref, weight_ref, freq_ref, x_ref, vis_ref, size_ref, sums_ref,
                 wide_ref, right_ref, left_ref, maskrow_ref, base_ref, cols_ref, acc_ref,
                 rows_ref, colsum_ref):
    c = pl.program_id(0)
    inputs, chans, width = x_ref.shape
    tiles = inputs // TILE
    half = width // 2
    parts, place = tile_parts(tiles), places(tiles)
    last = chans - 1

    def load_channel(c):
        lanes = lax.broadcasted_iota(jnp.int32, (TILE, width), 1)
        slot = lax.rem(c, 2)
        for t in range(tiles):
            at = slice(t * TILE, (t + 1) * TILE)
            rows = wide_ref[pl.ds(t * TILE * chans + c, TILE, stride=chans), :]
            rows = rows * maskrow_ref[at, :]
            right_ref[slot, at, :] = rows.astype(jnp.bfloat16)
            rows = rows + rows
            turned = pltpu.roll(rows, half, 1)
            left_ref[slot, t, :TILE, :] = rows.astype(jnp.bfloat16)
            left_ref[slot, t, TILE:, :] = jnp.where(lanes < half, turned, -turned).astype(jnp.bfloat16)

    def correlate(c, part):
        slot = lax.rem(c, 2)
        for ti in parts[part]:
            yield
            twice = lax.dot_general(
                left_ref[slot, ti], right_ref[slot, ti * TILE :, :], (((1,), (1,)), ((), ())),
                preferred_element_type=jnp.float32,
            ).astype(jnp.bfloat16)
            for tj in range(ti, tiles):
                at = slice((tj - ti) * TILE, (tj - ti + 1) * TILE)
                for p in (0, 1):
                    vis_ref[(c,) + place[ti, tj] + (p,)] = twice[p * TILE : (p + 1) * TILE, at]

    @pl.when(c == 0)
    def _():
        rows_ref[...] = jnp.zeros_like(rows_ref)
        acc_ref[...] = jnp.zeros_like(acc_ref)
        for t in range(tiles):
            at = slice(t * TILE, (t + 1) * TILE)
            block = x_ref[at].astype(jnp.float32)
            wide_ref[pl.ds(t * TILE * chans, TILE * chans), :] = block.reshape(TILE * chans, width)
            maskrow_ref[at, :] = jnp.broadcast_to(mask_ref[:, at] * 0.125, (TILE, TILE)).T
        flagged = (1.0 - mask_ref[...]) * HUGE
        ones = jnp.ones_like(flagged)
        sub = lax.broadcasted_iota(jnp.int32, (16, inputs), 0)
        near = jnp.where(sub == 0, 5.0 * ones, jnp.where(sub == 1, flagged, jnp.where(sub == 2, ones, 0.0)))
        far = jnp.where(sub < 2, ones, jnp.where(sub == 2, flagged, 0.0))
        near, far = near.astype(jnp.bfloat16), far.astype(jnp.bfloat16)
        for ti in range(tiles):
            base = lax.dot_general(
                near[:, ti * TILE : (ti + 1) * TILE], far[:, ti * TILE :], (((0,), (0,)), ((), ())),
                preferred_element_type=jnp.float32,
            )
            for tj in range(ti, tiles):
                base_ref[place[ti, tj]] = base[:, (tj - ti) * TILE : (tj - ti + 1) * TILE]

    @pl.when(c == 0)
    def _():
        load_channel(c)

    @pl.when(c == 0)
    def _():
        drain(correlate(c, 0))

    def terms(ti, tj, first, keep):
        rows = slice(first, first + UNIT)
        part, k = place[ti, tj]
        vis = []
        for p in (0, 1):
            vis.append(vis_ref[c, part, k, p, rows, :].astype(jnp.float32))
        size = vis[0] * vis[0] + vis[1] * vis[1]
        size_ref[c, part, k, rows, :] = size + 1.0
        robust = 1.0 / (size + (base_ref[part, k, rows, :] - 4.0 * vis[0]))
        if keep is not None:
            robust = jnp.where(keep, robust, 0.0)
        return [robust * vis[0], robust * vis[1], robust]

    for part in range(len(parts)):
        @pl.when(c >= -part)
        def _(part=part):
            if part == 0:
                cols_ref[...] = jnp.zeros_like(cols_ref)
            if part + 1 < len(parts):
                ahead = correlate(c, part + 1)
            else:
                ahead = correlate(jnp.minimum(c + 1, last), 0)
            if part == 0:
                load_channel(jnp.minimum(c + 1, last))
            pair_sums(c, parts[part], tiles, terms, ahead, cols_ref, acc_ref, rows_ref)
            if part + 1 == len(parts):
                store_cols(c, cols_ref, colsum_ref)

    @pl.when(c == last)
    def _():
        fold_rows(c, 0, inputs, acc_ref, rows_ref)
        totals = channel_totals(tiles, rows_ref, colsum_ref, (0.5, 0.5, 1.0))
        store_sums(totals, weight_ref[...], freq_ref[...], sums_ref)


def pieces(value):
    out = []
    for _ in range(3):
        out.append(value.astype(jnp.bfloat16).astype(jnp.float32))
        value = value - out[-1]
    return out


def next_kernel(gains_ref, old_ref, mask_ref, weight_ref, freq_ref, vis_ref, size_ref,
                sums_ref, new_ref, fit_ref,
                model_ref, pair_ref, square_ref, left_ref, right_ref, cols_ref, acc_ref, rows_ref,
                colsum_ref):
    c = pl.program_id(0)
    last = pl.num_programs(0) - 1
    inputs = mask_ref.shape[1]
    tiles = inputs // TILE
    parts, place = tile_parts(tiles), places(tiles)
    sub = lax.broadcasted_iota(jnp.int32, (8, inputs), 0)
    zero = jnp.zeros((8, inputs), jnp.float32)

    def spread(piece, count):
        return jnp.broadcast_to(piece, (count, inputs))

    def load_channel(c):
        slot = lax.rem(c, 2)
        for p in (0, 1):
            own = model_ref[c, 8 * p : 8 * p + 8, :]
            left_ref[slot, p] = jnp.concatenate([own] * 3 + [zero], axis=0).astype(jnp.bfloat16)
        right = [
            jnp.where(sub < 3, spread(model_ref[c, k : k + 1, :], 8), spread(model_ref[c, 3 + k : 4 + k, :], 8))
            for k in range(3)
        ]
        right_ref[slot] = jnp.concatenate(right + [zero], axis=0).astype(jnp.bfloat16)

    def model(c, part):
        slot = lax.rem(c, 2)
        for ti in parts[part]:
            for p in (0, 1):
                yield
                pair = lax.dot_general(
                    left_ref[slot, p, :, ti * TILE : (ti + 1) * TILE],
                    right_ref[slot, :, ti * TILE :],
                    (((0,), (0,)), ((), ())),
                    preferred_element_type=jnp.float32,
                )
                for tj in range(ti, tiles):
                    at = slice((tj - ti) * TILE, (tj - ti + 1) * TILE)
                    pair_ref[place[ti, tj] + (p,)] = pair[:, at]

    @pl.when(c == 0)
    def _():
        rows_ref[...] = jnp.zeros_like(rows_ref)
        acc_ref[...] = jnp.zeros_like(acc_ref)
        gains = solve_update(rows_of(gains_ref, 3), rows_of(old_ref, 6))
        new_ref[...] = gains
        angles = gains[1:2] + freq_ref[...] * gains[2:3]
        amplitude = gains[0:1] * mask_ref[...]
        double = amplitude + amplitude
        model_re = pieces(double * jnp.cos(angles))
        model_im = pieces(double * jnp.sin(angles))
        for k in range(3):
            model_ref[:, k, :] = model_re[k]
            model_ref[:, 3 + k, :] = model_im[k]
            model_ref[:, 8 + k, :] = model_im[k]
            model_ref[:, 11 + k, :] = -model_re[k]
        for k in (6, 7, 14, 15):
            model_ref[:, k, :] = jnp.zeros_like(angles)
        b = pieces(double * amplitude)
        b = [jnp.broadcast_to(x, (8, inputs)) for x in b]
        left = jnp.where(sub < 3, b[0], jnp.where(sub < 5, b[1], jnp.where(sub < 6, b[2], 0.0)))
        right = jnp.where(
            (sub == 0) | (sub == 3) | (sub == 5), b[0], jnp.where((sub == 1) | (sub == 4), b[1], b[2])
        )
        left = jnp.concatenate([left, zero], axis=0).astype(jnp.bfloat16)
        right = jnp.concatenate([right, zero], axis=0).astype(jnp.bfloat16)
        for ti in range(tiles):
            square = lax.dot_general(
                left[:, ti * TILE : (ti + 1) * TILE], right[:, ti * TILE :], (((0,), (0,)), ((), ())),
                preferred_element_type=jnp.float32,
            )
            for tj in range(ti, tiles):
                square_ref[place[ti, tj]] = square[:, (tj - ti) * TILE : (tj - ti + 1) * TILE]

    @pl.when(c == 0)
    def _():
        load_channel(c)
        drain(model(c, 0))

    def terms(ti, tj, first, keep):
        part, k = place[ti, tj]
        rows = slice(first, first + UNIT)
        vis_re, vis_im = [vis_ref[c, part, k, p, rows, :].astype(jnp.float32) for p in (0, 1)]
        pair_re, pair_im = [pair_ref[part, k, p, rows, :] for p in (0, 1)]
        square = square_ref[part, k, rows, :]
        prod_re = vis_re * pair_re + vis_im * pair_im
        prod_im = vis_im * pair_re - vis_re * pair_im
        robust = 1.0 / (size_ref[c, part, k, rows, :] - prod_re + square)
        if keep is not None:
            robust = jnp.where(keep, robust, 0.0)
        return [robust * prod_re, robust * prod_im, robust * square]

    for part in range(len(parts)):
        @pl.when(c >= -part)
        def _(part=part):
            if part == 0:
                cols_ref[...] = jnp.zeros_like(cols_ref)
            if part + 1 < len(parts):
                ahead = model(c, part + 1)
            else:
                ahead = model(jnp.minimum(c + 1, last), 0)
            if part == 0:
                load_channel(jnp.minimum(c + 1, last))
            pair_sums(c, parts[part], tiles, terms, ahead, cols_ref, acc_ref, rows_ref)
            if part + 1 == len(parts):
                store_cols(c, cols_ref, colsum_ref)

    @pl.when(c == last)
    def _():
        fold_rows(c, 0, inputs, acc_ref, rows_ref)
        totals = channel_totals(tiles, rows_ref, colsum_ref, (0.125, 0.125, 0.25))
        store_sums(totals, weight_ref[...], freq_ref[...], sums_ref)
        bound = jnp.maximum(totals[2], 1.0)
        fit_ref[0] = totals[0] / bound
        fit_ref[1] = totals[1] / bound


def whole(shape):
    return pl.BlockSpec(shape, lambda c: (0,) * len(shape))


RESIDENT = pl.BlockSpec(memory_space=pltpu.VMEM)


def first_iteration(x, mask, weight, freq):
    inputs, chans, width = x.shape
    tiles = inputs // TILE
    steps, size = len(tile_parts(tiles)), part_size(tiles)
    return pl.pallas_call(
        first_kernel,
        grid=(chans,),
        in_specs=[whole(mask.shape), whole(weight.shape), whole(freq.shape), whole(x.shape)],
        out_specs=[RESIDENT, RESIDENT, whole((6, inputs))],
        out_shape=[
            pltpu.VMEM((chans, steps, size, 2, TILE, TILE), jnp.bfloat16),
            pltpu.VMEM((chans, steps, size, TILE, TILE), jnp.float32),
            jax.ShapeDtypeStruct((6, inputs), jnp.float32),
        ],
        scratch_shapes=[
            pltpu.VMEM((inputs * chans, width), jnp.float32),
            pltpu.VMEM((2, inputs, width), jnp.bfloat16),
            pltpu.VMEM((2, tiles, 2 * TILE, width), jnp.bfloat16),
            pltpu.VMEM((inputs, TILE), jnp.float32),
            pltpu.VMEM((steps, size, TILE, TILE), jnp.float32),
            pltpu.VMEM((3, 8, inputs), jnp.float32),
            pltpu.VMEM((3, inputs, TILE), jnp.float32),
            pltpu.VMEM((inputs, TILE), jnp.float32),
            pltpu.VMEM((chans, 8, inputs), jnp.float32),
        ],
        compiler_params=pltpu.CompilerParams(vmem_limit_bytes=VMEM_LIMIT),
        name="first_iteration",
    )(mask, weight, freq, x)


def held(x):
    return pltpu.with_memory_space_constraint(x, pltpu.VMEM)


def next_iteration(gains, old_sums, mask, weight, freq, vis, size):
    chans, steps, count = size.shape[:3]
    inputs = mask.shape[1]
    tiles = inputs // TILE
    return pl.pallas_call(
        next_kernel,
        grid=(chans,),
        in_specs=[
            whole(gains.shape), whole(old_sums.shape), whole(mask.shape), whole(weight.shape),
            whole(freq.shape),
        ] + [RESIDENT, RESIDENT],
        out_specs=[whole((6, inputs)), whole((3, inputs)), whole((2, chans, inputs))],
        out_shape=[
            jax.ShapeDtypeStruct((6, inputs), jnp.float32),
            jax.ShapeDtypeStruct((3, inputs), jnp.float32),
            jax.ShapeDtypeStruct((2, chans, inputs), jnp.float32),
        ],
        scratch_shapes=[
            pltpu.VMEM((chans, 16, inputs), jnp.float32),
            pltpu.VMEM((steps, count, 2, TILE, TILE), jnp.float32),
            pltpu.VMEM((steps, count, TILE, TILE), jnp.float32),
            pltpu.VMEM((2, 2, 32, inputs), jnp.bfloat16),
            pltpu.VMEM((2, 32, inputs), jnp.bfloat16),
            pltpu.VMEM((3, 8, inputs), jnp.float32),
            pltpu.VMEM((3, inputs, TILE), jnp.float32),
            pltpu.VMEM((inputs, TILE), jnp.float32),
            pltpu.VMEM((chans, 8, inputs), jnp.float32),
        ],
        compiler_params=pltpu.CompilerParams(vmem_limit_bytes=VMEM_LIMIT),
        name="next_iteration",
    )(gains, old_sums, mask, weight, freq, held(vis), held(size))


def all_sum(part, devices):
    if devices & (devices - 1):
        return lax.psum(part, "chan")
    reach = 1
    while reach < devices:
        ways = 4 if devices // reach >= 4 else 2
        got = [part] + [
            lax.ppermute(part, "chan", [(i, i ^ (k * reach)) for i in range(devices)])
            for k in range(1, ways)
        ]
        part = (got[0] + got[1]) + (got[2] + got[3]) if ways == 4 else got[0] + got[1]
        reach *= ways
    return part


def local(voltages, antenna_usable_mask, channel_flags):
    devices = lax.axis_size("chan")
    inputs_dev, channels, sample_cols = voltages.shape
    chan_dev = channels // devices
    blocks = voltages.reshape(inputs_dev, devices, chan_dev, sample_cols)
    turned = lax.all_to_all(blocks, "chan", split_axis=1, concat_axis=0, tiled=True)
    inputs = inputs_dev * devices
    arrived = turned.reshape(inputs, chan_dev, sample_cols)
    first_channel = lax.axis_index("chan") * chan_dev
    channel_ids = (first_channel + jnp.arange(chan_dev)).astype(jnp.float32)
    freq = (2.0 * math.pi * (channel_ids + 0.5) / (chan_dev * devices))[:, None]
    weight = channel_flags.astype(jnp.float32)[:, None]
    mask = antenna_usable_mask.astype(jnp.float32)[None, :]
    gains = jnp.concatenate(
        [jnp.ones((1, inputs), jnp.float32), jnp.zeros((2, inputs), jnp.float32)], axis=0
    )
    vis, size, sums = first_iteration(arrived, mask, weight, freq)
    fitted = None
    for iteration in range(1, ITERS):
        sums, gains, fitted = next_iteration(
            gains, all_sum(sums, devices), mask, weight, freq, vis, size
        )
    totals = all_sum(sums, devices)
    gains = solve_update([gains[k : k + 1] for k in range(3)], [totals[k : k + 1] for k in range(6)])
    return (gains, fitted)


def solution(mesh):
    placed = (P(("groups", "chan"), None, None), P("groups"), P(("groups", "chan")))
    return jax.shard_map(
        local,
        mesh=mesh,
        in_specs=placed,
        out_specs=(P(None, "groups"), P(None, ("groups", "chan"), None)),
        check_vma=False,
    )
```

time: 212 us -> 169 us (0.80)
  Pallas kernels: 117 us -> 66.5 us
  other arithmetic: 0.74 us -> 6.25 us
    pallas_call x2, Pallas kernels: 80 us -> 43.9 us  [next_iteration(): pl.pallas_call(next_kernel, grid=(chans,), in_specs=[whole(gains.shape),...]
    pallas_call x1, Pallas kernels: 36.5 us -> 22.5 us  [first_iteration(): pl.pallas_call(first_kernel, grid=(chans,), in_specs=[whole(mask.shape),...]
    add x6, other arithmetic: 0.06 us -> 3.57 us  [all_sum(): part = got[0] + got[1] + (got[2] + got[3]) if ways == 4 else got[0] + got[1]]
  transfers between devices with their start and end apart: 19 -> 19, of which waited for: 14 -> 14; matrix products, arithmetic and copies ran while one was open for 0% -> 1% of each run, Pallas kernels for 0% -> 0%
where the time goes in v2:
time: 169 us; the launch traced here: 168 us
  Pallas kernels  66.5 us (39%)
  waiting for transfers between devices  57.7 us (34%)
  starting transfers between devices  31.3 us (19%)
  other arithmetic  6.25 us (4%)
  local copies, waits for them, and re-layouts  5.46 us (3%)
    pallas_call x2, Pallas kernels, next_iteration(): pl.pallas_call(next_kernel, grid=(chans,), in_specs=[whole(gains.shape),...  43.9 us
    all_to_all x1, waiting for transfers between devices, local(): lax.all_to_all(blocks, 'chan', split_axis=1, concat_axis=0, tiled=True)  39.2 us
    ppermute x18, starting transfers between devices, all_sum(): lax.ppermute(part, 'chan', [(i, i ^ k * reach) for i in range(devices)])  23.8 us
    pallas_call x1, Pallas kernels, first_iteration(): pl.pallas_call(first_kernel, grid=(chans,), in_specs=[whole(mask.shape),...  22.5 us
    ppermute x18, waiting for transfers between devices, all_sum(): lax.ppermute(part, 'chan', [(i, i ^ k * reach) for i in range(devices)])  18.5 us
    all_to_all x1, starting transfers between devices, local(): lax.all_to_all(blocks, 'chan', split_axis=1, concat_axis=0, tiled=True)  7.52 us
    add x6, other arithmetic, all_sum(): part = got[0] + got[1] + (got[2] + got[3]) if ways == 4 else got[0] + got[1]  3.57 us
    reshape x1, local copies, waits for them, and re-layouts, local(): blocks = voltages.reshape(inputs_dev, devices, chan_dev, sample_cols)  3.46 us
  transfers between devices with their start and end apart: 19, of which 14 were waited for; matrix products, arithmetic and copies ran while one was open for 1% of the time, Pallas kernels for 0%

profile of v2, /device:TPU:0, one launch (start us, length us, event | category | flops | bytes accessed | tf_op | source)
XLA Modules:
  0.0 167.9 jit_solution(16041560683829567920)
XLA Ops:
  0.6 3.5 %copy.5 = bf16[64,16,8,128]{3,2,0,1:T(8,128)(2,1)} copy(bf16[64,16,8,128]{3,2,1,0:T(8,128)(2,1)} %bitcast.10) | data formatting | bytes 4194304 | tf_op jit(solution)/shard_map/reshape | solution.py:452
  4.1 7.5 %all-to-all-start = ((bf16[64,16,8,128]{3,2,0,1:T(8,128)(2,1)}), bf16[64,16,8,128]{3,2,0,1:T(8,128)(2,1)S(1)}, u32[]{:S(2)}, u32[]{:S(2)}) async-start(bf16[64,16,8,128]{3,2,0,1:T(8,128)(2,1)} %copy.5), calls=%async_computation | async-start | bytes 4194304 | tf_op jit(solution)/shard_map/all_to_all | solution.py:453
  13.5 39.2 %all-to-all-done = bf16[64,16,8,128]{3,2,0,1:T(8,128)(2,1)S(1)} async-done(((bf16[64,16,8,128]{3,2,0,1:T(8,128)(2,1)}), bf16[64,16,8,128]{3,2,0,1:T(8,128)(2,1)S(1)}, u32[]{:S(2)}, u32[]{:S(2)}) %all-to-all-start) | async-done | bytes 2097184 | tf_op jit(solution)/shard_map/all_to_all | solution.py:453
  52.7 1.3 copy-done
  54.1 22.5 %first_iteration.1 = (bf16[8,2,18,2,128,128]{5,4,3,2,1,0:T(8,128)(2,1)S(1)}, f32[8,2,18,128,128]{4,3,2,1,0:T(8,128)S(1)}, f32[6,1024]{1,0:T(8,128)}) custom-call(f32[1,1024]{1,0:T(1,128)} %bitcast.11, f32[8,1]{1,0:T(8,128)} %copy.6.weight_ref, f32[8,1]{1,0:T(8,128)} %add_multiply_fusion.1.freq_ref, bf16[1024,8,128]{2,1,0:T(8,128)(2,1)} %bitcast.9), custom_call_target="tpu_custom_call" | custom-call | tf_op jit(solution)/shard_map/first_iteration/pallas_call | solution.py:370
  76.6 3.7 %collective-permute-start.2 = (f32[6,1024]{1,0:T(8,128)}, f32[6,1024]{1,0:T(8,128)S(1)}, u32[]{:S(2)}, u32[]{:S(2)}) collective-permute-start(f32[6,1024]{1,0:T(8,128)} %get-tuple-element.10), channel_id=1, source_target_pairs={{0,3},{1,2},{2,1},{3,0},{4,7},{5,6},{6,5},{7,4},{8,11},{9,10},{10,... | collective-permute-start | bytes 73736 | tf_op jit(solution)/shard_map/ppermute | solution.py:440
  80.5 1.9 %collective-permute-done.2 = f32[6,1024]{1,0:T(8,128)S(1)} collective-permute-done((f32[6,1024]{1,0:T(8,128)}, f32[6,1024]{1,0:T(8,128)S(1)}, u32[]{:S(2)}, u32[]{:S(2)}) %collective-permute-start.2) | collective-permute-done | bytes 24608 | tf_op jit(solution)/shard_map/ppermute | solution.py:440
  82.4 2.0 %collective-permute-done.1 = f32[6,1024]{1,0:T(8,128)S(1)} collective-permute-done((f32[6,1024]{1,0:T(8,128)}, f32[6,1024]{1,0:T(8,128)S(1)}, u32[]{:S(2)}, u32[]{:S(2)}) %collective-permute-start.1) | collective-permute-done | bytes 24608 | tf_op jit(solution)/shard_map/ppermute | solution.py:440
  84.5 0.8 add_add_fusion.5
  85.2 6.6 %collective-permute-start.5 = (f32[6,1024]{1,0:T(8,128)S(1)}, f32[6,1024]{1,0:T(8,128)S(1)}, u32[]{:S(2)}, u32[]{:S(2)}) collective-permute-start(f32[6,1024]{1,0:T(8,128)S(1)} %add_add_fusion.5), channel_id=1, source_target_pairs={{0,12},{1,13},{2,14},{3,15},{4,8},{5,9},{6,10},{7,11},{8,4},{9,5},... | collective-permute-start | bytes 73736 | tf_op jit(solution)/shard_map/ppermute | solution.py:440
  92.5 1.3 collective-permute-done.5
  93.7 3.0 %collective-permute-done.4 = f32[6,1024]{1,0:T(8,128)S(1)} collective-permute-done((f32[6,1024]{1,0:T(8,128)S(1)}, f32[6,1024]{1,0:T(8,128)S(1)}, u32[]{:S(2)}, u32[]{:S(2)}) %collective-permute-start.4) | collective-permute-done | bytes 24608 | tf_op jit(solution)/shard_map/ppermute | solution.py:440
  97.4 22.0 %next_iteration.2 = (f32[6,1024]{1,0:T(8,128)}, f32[3,1024]{1,0:T(4,128)}, f32[2,8,1024]{2,1,0:T(8,128)}) custom-call(f32[3,1024]{1,0:T(4,128)} %constant.6.clone.1.gains_ref, f32[6,1024]{1,0:T(8,128)} %add_add_fusion.4.old_ref, f32[1,1024]{1,0:T(1,128)} %bitcast.12, f32[8,1]{1,0:T(8,128)} %copy.6.weight_ref, f32[8,1]{1,0:T(8,128)} %add_multiply_fusion.1.freq_ref, ...), custom_call_target="tpu_custom_call" | custom-call | tf_op jit(solution)/shard_map/next_iteration/pallas_call | solution.py:404
  119.3 0.9 collective-permute-start.7
  120.2 1.0 collective-permute-start.6
  121.2 1.7 %collective-permute-done.8 = f32[6,1024]{1,0:T(8,128)S(1)} collective-permute-done((f32[6,1024]{1,0:T(8,128)}, f32[6,1024]{1,0:T(8,128)S(1)}, u32[]{:S(2)}, u32[]{:S(2)}) %collective-permute-start.8) | collective-permute-done | bytes 24608 | tf_op jit(solution)/shard_map/ppermute | solution.py:440
  122.9 0.9 collective-permute-done.7
  123.8 0.8 add_add_fusion.3
  124.6 1.2 collective-permute-start.11
  126.4 2.6 %collective-permute-start.9 = (f32[6,1024]{1,0:T(8,128)S(1)}, f32[6,1024]{1,0:T(8,128)S(1)}, u32[]{:S(2)}, u32[]{:S(2)}) collective-permute-start(f32[6,1024]{1,0:T(8,128)S(1)} %add_add_fusion.3), channel_id=1, source_target_pairs={{0,4},{1,5},{2,6},{3,7},{4,0},{5,1},{6,2},{7,3},{8,12},{9,13},{10,... | collective-permute-start | bytes 73736 | tf_op jit(solution)/shard_map/ppermute | solution.py:440
  129.0 1.4 collective-permute-done.11
  130.4 0.8 collective-permute-done.10
  131.8 22.0 %next_iteration.3 = (f32[6,1024]{1,0:T(8,128)}, f32[3,1024]{1,0:T(4,128)}, f32[2,8,1024]{2,1,0:T(8,128)}) custom-call(f32[3,1024]{1,0:T(4,128)} %get-tuple-element.13.gains_ref, f32[6,1024]{1,0:T(8,128)} %add_add_fusion.2.old_ref, f32[1,1024]{1,0:T(1,128)} %bitcast.13, f32[8,1]{1,0:T(8,128)} %copy.6.weight_ref, f32[8,1]{1,0:T(8,128)} %add_multiply_fusion.1.freq_ref, ...), custom_call_target="tpu_custom_call" | custom-call | tf_op jit(solution)/shard_map/next_iteration/pallas_call | solution.py:404
  155.7 1.8 %collective-permute-done.14 = f32[6,1024]{1,0:T(8,128)S(1)} collective-permute-done((f32[6,1024]{1,0:T(8,128)}, f32[6,1024]{1,0:T(8,128)S(1)}, u32[]{:S(2)}, u32[]{:S(2)}) %collective-permute-start.14) | collective-permute-done | bytes 24608 | tf_op jit(solution)/shard_map/ppermute | solution.py:440
  157.4 1.0 collective-permute-done.13
  158.4 0.8 add_add_fusion.1
  159.2 2.1 %collective-permute-start.17 = (f32[6,1024]{1,0:T(8,128)S(1)}, f32[6,1024]{1,0:T(8,128)S(1)}, u32[]{:S(2)}, u32[]{:S(2)}) collective-permute-start(f32[6,1024]{1,0:T(8,128)S(1)} %add_add_fusion.1), channel_id=1, source_target_pairs={{0,12},{1,13},{2,14},{3,15},{4,8},{5,9},{6,10},{7,11},{8,4},{9,5},... | collective-permute-start | bytes 73736 | tf_op jit(solution)/shard_map/ppermute | solution.py:440
  161.3 0.8 collective-permute-start.16
  162.1 1.5 collective-permute-start.15
  163.6 1.3 collective-permute-done.17
  164.9 1.2 collective-permute-done.16
  166.4 0.9 add_multiply_fusion
  (28 shorter events, 7.2 us)
Async XLA Ops:
  4.1 7.5 %copy-start.2 = (s32[8]{0:T(128)S(1)}, s32[8]{0:T(128)}, u32[]{:S(2)}) copy-start(s32[8]{0:T(128)} %param.5) | copy-start | bytes 100
  4.1 8.2 %copy-start.1 = (s32[1024]{0:T(1024)S(1)}, s32[1024]{0:T(1024)}, u32[]{:S(2)}) copy-start(s32[1024]{0:T(1024)} %param.4) | copy-start | bytes 12292
  4.1 48.6 %all-to-all-start = ((bf16[64,16,8,128]{3,2,0,1:T(8,128)(2,1)}), bf16[64,16,8,128]{3,2,0,1:T(8,128)(2,1)S(1)}, u32[]{:S(2)}, u32[]{:S(2)}) async-start(bf16[64,16,8,128]{3,2,0,1:T(8,128)(2,1)} %copy.5), calls=%async_computation | async-start | bytes 4194304 | tf_op jit(solution)/shard_map/all_to_all | solution.py:453
  52.7 1.3 copy-start
  76.6 5.8 %collective-permute-start.2 = (f32[6,1024]{1,0:T(8,128)}, f32[6,1024]{1,0:T(8,128)S(1)}, u32[]{:S(2)}, u32[]{:S(2)}) collective-permute-start(f32[6,1024]{1,0:T(8,128)} %get-tuple-element.10), channel_id=1, source_target_pairs={{0,3},{1,2},{2,1},{3,0},{4,7},{5,6},{6,5},{7,4},{8,11},{9,10},{10,... | collective-permute-start | bytes 73736 | tf_op jit(solution)/shard_map/ppermute | solution.py:440
  80.3 4.1 %collective-permute-start.1 = (f32[6,1024]{1,0:T(8,128)}, f32[6,1024]{1,0:T(8,128)S(1)}, u32[]{:S(2)}, u32[]{:S(2)}) collective-permute-start(f32[6,1024]{1,0:T(8,128)} %get-tuple-element.10), channel_id=1, source_target_pairs={{0,2},{1,3},{2,0},{3,1},{4,6},{5,7},{6,4},{7,5},{8,10},{9,11},{10,... | collective-permute-start | bytes 73736 | tf_op jit(solution)/shard_map/ppermute | solution.py:440
  80.3 4.1 %collective-permute-start = (f32[6,1024]{1,0:T(8,128)}, f32[6,1024]{1,0:T(8,128)S(1)}, u32[]{:S(2)}, u32[]{:S(2)}) collective-permute-start(f32[6,1024]{1,0:T(8,128)} %get-tuple-element.10), channel_id=1, source_target_pairs={{0,1},{1,0},{2,3},{3,2},{4,5},{5,4},{6,7},{7,6},{8,9},{9,8},{10,11... | collective-permute-start | bytes 73736 | tf_op jit(solution)/shard_map/ppermute | solution.py:440
  85.2 8.5 %collective-permute-start.5 = (f32[6,1024]{1,0:T(8,128)S(1)}, f32[6,1024]{1,0:T(8,128)S(1)}, u32[]{:S(2)}, u32[]{:S(2)}) collective-permute-start(f32[6,1024]{1,0:T(8,128)S(1)} %add_add_fusion.5), channel_id=1, source_target_pairs={{0,12},{1,13},{2,14},{3,15},{4,8},{5,9},{6,10},{7,11},{8,4},{9,5},... | collective-permute-start | bytes 73736 | tf_op jit(solution)/shard_map/ppermute | solution.py:440
  91.9 4.9 %collective-permute-start.4 = (f32[6,1024]{1,0:T(8,128)S(1)}, f32[6,1024]{1,0:T(8,128)S(1)}, u32[]{:S(2)}, u32[]{:S(2)}) collective-permute-start(f32[6,1024]{1,0:T(8,128)S(1)} %add_add_fusion.5), channel_id=1, source_target_pairs={{0,8},{1,9},{2,10},{3,11},{4,12},{5,13},{6,14},{7,15},{8,0},{9,1},... | collective-permute-start | bytes 73736 | tf_op jit(solution)/shard_map/ppermute | solution.py:440
  92.5 4.3 %collective-permute-start.3 = (f32[6,1024]{1,0:T(8,128)S(1)}, f32[6,1024]{1,0:T(8,128)S(1)}, u32[]{:S(2)}, u32[]{:S(2)}) collective-permute-start(f32[6,1024]{1,0:T(8,128)S(1)} %add_add_fusion.5), channel_id=1, source_target_pairs={{0,4},{1,5},{2,6},{3,7},{4,0},{5,1},{6,2},{7,3},{8,12},{9,13},{10,... | collective-permute-start | bytes 73736 | tf_op jit(solution)/shard_map/ppermute | solution.py:440
  119.3 3.6 %collective-permute-start.8 = (f32[6,1024]{1,0:T(8,128)}, f32[6,1024]{1,0:T(8,128)S(1)}, u32[]{:S(2)}, u32[]{:S(2)}) collective-permute-start(f32[6,1024]{1,0:T(8,128)} %get-tuple-element.14), channel_id=1, source_target_pairs={{0,3},{1,2},{2,1},{3,0},{4,7},{5,6},{6,5},{7,4},{8,11},{9,10},{10,... | collective-permute-start | bytes 73736 | tf_op jit(solution)/shard_map/ppermute | solution.py:440
  119.3 4.5 %collective-permute-start.7 = (f32[6,1024]{1,0:T(8,128)}, f32[6,1024]{1,0:T(8,128)S(1)}, u32[]{:S(2)}, u32[]{:S(2)}) collective-permute-start(f32[6,1024]{1,0:T(8,128)} %get-tuple-element.14), channel_id=1, source_target_pairs={{0,2},{1,3},{2,0},{3,1},{4,6},{5,7},{6,4},{7,5},{8,10},{9,11},{10,... | collective-permute-start | bytes 73736 | tf_op jit(solution)/shard_map/ppermute | solution.py:440
  120.2 3.6 %collective-permute-start.6 = (f32[6,1024]{1,0:T(8,128)}, f32[6,1024]{1,0:T(8,128)S(1)}, u32[]{:S(2)}, u32[]{:S(2)}) collective-permute-start(f32[6,1024]{1,0:T(8,128)} %get-tuple-element.14), channel_id=1, source_target_pairs={{0,1},{1,0},{2,3},{3,2},{4,5},{5,4},{6,7},{7,6},{8,9},{9,8},{10,11... | collective-permute-start | bytes 73736 | tf_op jit(solution)/shard_map/ppermute | solution.py:440
  124.6 5.8 %collective-permute-start.11 = (f32[6,1024]{1,0:T(8,128)S(1)}, f32[6,1024]{1,0:T(8,128)S(1)}, u32[]{:S(2)}, u32[]{:S(2)}) collective-permute-start(f32[6,1024]{1,0:T(8,128)S(1)} %add_add_fusion.3), channel_id=1, source_target_pairs={{0,12},{1,13},{2,14},{3,15},{4,8},{5,9},{6,10},{7,11},{8,4},{9,5},... | collective-permute-start | bytes 73736 | tf_op jit(solution)/shard_map/ppermute | solution.py:440
  125.8 5.4 %collective-permute-start.10 = (f32[6,1024]{1,0:T(8,128)S(1)}, f32[6,1024]{1,0:T(8,128)S(1)}, u32[]{:S(2)}, u32[]{:S(2)}) collective-permute-start(f32[6,1024]{1,0:T(8,128)S(1)} %add_add_fusion.3), channel_id=1, source_target_pairs={{0,8},{1,9},{2,10},{3,11},{4,12},{5,13},{6,14},{7,15},{8,0},{9,1},... | collective-permute-start | bytes 73736 | tf_op jit(solution)/shard_map/ppermute | solution.py:440
  126.4 4.8 %collective-permute-start.9 = (f32[6,1024]{1,0:T(8,128)S(1)}, f32[6,1024]{1,0:T(8,128)S(1)}, u32[]{:S(2)}, u32[]{:S(2)}) collective-permute-start(f32[6,1024]{1,0:T(8,128)S(1)} %add_add_fusion.3), channel_id=1, source_target_pairs={{0,4},{1,5},{2,6},{3,7},{4,0},{5,1},{6,2},{7,3},{8,12},{9,13},{10,... | collective-permute-start | bytes 73736 | tf_op jit(solution)/shard_map/ppermute | solution.py:440
  153.8 3.6 %collective-permute-start.14 = (f32[6,1024]{1,0:T(8,128)}, f32[6,1024]{1,0:T(8,128)S(1)}, u32[]{:S(2)}, u32[]{:S(2)}) collective-permute-start(f32[6,1024]{1,0:T(8,128)} %get-tuple-element.16), channel_id=1, source_target_pairs={{0,3},{1,2},{2,1},{3,0},{4,7},{5,6},{6,5},{7,4},{8,11},{9,10},{10,... | collective-permute-start | bytes 73736 | tf_op jit(solution)/shard_map/ppermute | solution.py:440
  154.2 4.2 %collective-permute-start.13 = (f32[6,1024]{1,0:T(8,128)}, f32[6,1024]{1,0:T(8,128)S(1)}, u32[]{:S(2)}, u32[]{:S(2)}) collective-permute-start(f32[6,1024]{1,0:T(8,128)} %get-tuple-element.16), channel_id=1, source_target_pairs={{0,2},{1,3},{2,0},{3,1},{4,6},{5,7},{6,4},{7,5},{8,10},{9,11},{10,... | collective-permute-start | bytes 73736 | tf_op jit(solution)/shard_map/ppermute | solution.py:440
  155.0 3.4 %collective-permute-start.12 = (f32[6,1024]{1,0:T(8,128)}, f32[6,1024]{1,0:T(8,128)S(1)}, u32[]{:S(2)}, u32[]{:S(2)}) collective-permute-start(f32[6,1024]{1,0:T(8,128)} %get-tuple-element.16), channel_id=1, source_target_pairs={{0,1},{1,0},{2,3},{3,2},{4,5},{5,4},{6,7},{7,6},{8,9},{9,8},{10,11... | collective-permute-start | bytes 73736 | tf_op jit(solution)/shard_map/ppermute | solution.py:440
  159.2 5.8 %collective-permute-start.17 = (f32[6,1024]{1,0:T(8,128)S(1)}, f32[6,1024]{1,0:T(8,128)S(1)}, u32[]{:S(2)}, u32[]{:S(2)}) collective-permute-start(f32[6,1024]{1,0:T(8,128)S(1)} %add_add_fusion.1), channel_id=1, source_target_pairs={{0,12},{1,13},{2,14},{3,15},{4,8},{5,9},{6,10},{7,11},{8,4},{9,5},... | collective-permute-start | bytes 73736 | tf_op jit(solution)/shard_map/ppermute | solution.py:440
  161.3 4.9 %collective-permute-start.16 = (f32[6,1024]{1,0:T(8,128)S(1)}, f32[6,1024]{1,0:T(8,128)S(1)}, u32[]{:S(2)}, u32[]{:S(2)}) collective-permute-start(f32[6,1024]{1,0:T(8,128)S(1)} %add_add_fusion.1), channel_id=1, source_target_pairs={{0,8},{1,9},{2,10},{3,11},{4,12},{5,13},{6,14},{7,15},{8,0},{9,1},... | collective-permute-start | bytes 73736 | tf_op jit(solution)/shard_map/ppermute | solution.py:440
  162.1 4.3 %collective-permute-start.15 = (f32[6,1024]{1,0:T(8,128)S(1)}, f32[6,1024]{1,0:T(8,128)S(1)}, u32[]{:S(2)}, u32[]{:S(2)}) collective-permute-start(f32[6,1024]{1,0:T(8,128)S(1)} %add_add_fusion.1), channel_id=1, source_target_pairs={{0,4},{1,5},{2,6},{3,7},{4,0},{5,1},{6,2},{7,3},{8,12},{9,13},{10,... | collective-permute-start | bytes 73736 | tf_op jit(solution)/shard_map/ppermute | solution.py:440

commit v3 on v2

--- a/solution.py
+++ b/solution.py
@@ -1,3 +1,4 @@
+import functools
 import math
 
 import jax
@@ -9,12 +10,12 @@
 
 ITERS = 3
 TILE = 128
-GROUP = 16
+GROUP = 32
 UNIT = 16
 PARTS = 2
 AHEAD = 1
 HUGE = 1e38
-VMEM_LIMIT = 20 * 1024 * 1024
+VMEM_LIMIT = 16 * 1024 * 1024
 
 huber_scale = 0.25
 damping = 0.5
@@ -30,6 +31,15 @@
     )
 
 
+def solve_rows(gains, sums):
+    bound = jnp.maximum(sums[3] * sums[5] - sums[4] * sums[4], 1.0)
+    phase = (sums[5] * sums[1] - sums[4] * sums[2]) / bound
+    delay = (sums[3] * sums[2] - sums[4] * sums[1]) / bound
+    ratio = gains[0] * (sums[0] - sums[3]) / jnp.maximum(sums[3], 1.0)
+    row = lax.broadcasted_iota(jnp.int32, gains.shape, 0)
+    return gains + damping * jnp.where(row == 0, ratio, jnp.where(row == 1, phase, delay))
+
+
 def rows_of(ref, count):
     return [ref[k : k + 1, :] for k in range(count)]
 
@@ -51,7 +61,7 @@
         pass
 
 
-def pair_sums(c, rows, tiles, terms, ahead, cols_ref, acc_ref, rows_ref):
+def pair_sums(c, rows, tiles, terms, ahead, cols_ref, rows_ref):
     for ti in rows:
         for first in range(0, TILE, GROUP):
             for _ in range(AHEAD):
@@ -78,10 +88,8 @@
                     lanes = slice(tj * TILE, (tj + 1) * TILE)
                     for k in range(3):
                         cols_ref[k, :, lanes] += parts[k] if k != 1 else -parts[k]
-            fold_rows(c - 1, row, GROUP, acc_ref, rows_ref)
             for unit in range(GROUP // UNIT):
-                for k in range(3):
-                    acc_ref[k, row + unit * UNIT : row + (unit + 1) * UNIT, :] = totals[unit][k]
+                fold_rows(c, row + unit * UNIT, totals[unit], rows_ref)
     drain(ahead)
 
 
@@ -91,13 +99,11 @@
     return [order[k : k + size] for k in range(0, len(order), size)]
 
 
-def fold_rows(c, row, count, acc_ref, rows_ref):
-    lanes = lax.broadcasted_iota(jnp.int32, (count, TILE), 1)
-    kept = rows_ref[row : row + count, :]
+def fold_rows(c, row, totals, rows_ref):
+    lanes = lax.broadcasted_iota(jnp.int32, (UNIT, TILE), 1)
     for k in range(3):
-        total = jnp.sum(acc_ref[k, row : row + count, :], axis=1, keepdims=True)
-        kept = jnp.where(lanes == 8 * k + c, total, kept)
-    rows_ref[row : row + count, :] = kept
+        total = jnp.broadcast_to(jnp.sum(totals[k], axis=1, keepdims=True), (UNIT, TILE))
+        pltpu.store(rows_ref.at[row : row + UNIT, :], total, mask=lanes == 8 * k + c)
 
 
 def store_cols(c, cols_ref, colsum_ref):
@@ -129,7 +135,7 @@
 
 
 def first_kernel(mask_ref, weight_ref, freq_ref, x_ref, vis_ref, size_ref, sums_ref,
-                 wide_ref, right_ref, left_ref, maskrow_ref, base_ref, cols_ref, acc_ref,
+                 wide_ref, right_ref, left_ref, maskrow_ref, base_ref, ahead_ref, cols_ref,
                  rows_ref, colsum_ref):
     c = pl.program_id(0)
     inputs, chans, width = x_ref.shape
@@ -161,13 +167,17 @@
             ).astype(jnp.bfloat16)
             for tj in range(ti, tiles):
                 at = slice((tj - ti) * TILE, (tj - ti + 1) * TILE)
+                place_part, k = place[ti, tj]
                 for p in (0, 1):
-                    vis_ref[(c,) + place[ti, tj] + (p,)] = twice[p * TILE : (p + 1) * TILE, at]
+                    value = twice[p * TILE : (p + 1) * TILE, at]
+                    if place_part == 0:
+                        ahead_ref[k, p] = value
+                    else:
+                        vis_ref[c, place_part, k, p] = value
 
     @pl.when(c == 0)
     def _():
         rows_ref[...] = jnp.zeros_like(rows_ref)
-        acc_ref[...] = jnp.zeros_like(acc_ref)
         for t in range(tiles):
             at = slice(t * TILE, (t + 1) * TILE)
             block = x_ref[at].astype(jnp.float32)
@@ -200,7 +210,12 @@
         part, k = place[ti, tj]
         vis = []
         for p in (0, 1):
-            vis.append(vis_ref[c, part, k, p, rows, :].astype(jnp.float32))
+            if part == 0:
+                value = ahead_ref[k, p, rows, :]
+                vis_ref[c, part, k, p, rows, :] = value
+            else:
+                value = vis_ref[c, part, k, p, rows, :]
+            vis.append(value.astype(jnp.float32))
         size = vis[0] * vis[0] + vis[1] * vis[1]
         size_ref[c, part, k, rows, :] = size + 1.0
         robust = 1.0 / (size + (base_ref[part, k, rows, :] - 4.0 * vis[0]))
@@ -219,13 +234,12 @@
                 ahead = correlate(jnp.minimum(c + 1, last), 0)
             if part == 0:
                 load_channel(jnp.minimum(c + 1, last))
-            pair_sums(c, parts[part], tiles, terms, ahead, cols_ref, acc_ref, rows_ref)
+            pair_sums(c, parts[part], tiles, terms, ahead, cols_ref, rows_ref)
             if part + 1 == len(parts):
                 store_cols(c, cols_ref, colsum_ref)
 
     @pl.when(c == last)
     def _():
-        fold_rows(c, 0, inputs, acc_ref, rows_ref)
         totals = channel_totals(tiles, rows_ref, colsum_ref, (0.5, 0.5, 1.0))
         store_sums(totals, weight_ref[...], freq_ref[...], sums_ref)
 
@@ -238,10 +252,10 @@
     return out
 
 
-def next_kernel(gains_ref, old_ref, mask_ref, weight_ref, freq_ref, vis_ref, size_ref,
-                sums_ref, new_ref, fit_ref,
-                model_ref, pair_ref, square_ref, left_ref, right_ref, cols_ref, acc_ref, rows_ref,
-                colsum_ref):
+def next_kernel(ways, gains_ref, mask_ref, weight_ref, freq_ref, vis_ref, size_ref, *refs):
+    old_refs = refs[:ways]
+    (sums_ref, new_ref, fit_ref, model_ref, pair_ref, square_ref, left_ref, right_ref, cols_ref,
+     rows_ref, colsum_ref) = refs[ways:]
     c = pl.program_id(0)
     last = pl.num_programs(0) - 1
     inputs = mask_ref.shape[1]
@@ -257,7 +271,9 @@
         slot = lax.rem(c, 2)
         for p in (0, 1):
             own = model_ref[c, 8 * p : 8 * p + 8, :]
-            left_ref[slot, p] = jnp.concatenate([own] * 3 + [zero], axis=0).astype(jnp.bfloat16)
+            own = jnp.concatenate([own] * 3 + [zero], axis=0).astype(jnp.bfloat16)
+            for t in range(tiles):
+                left_ref[slot, t, :, p * TILE : (p + 1) * TILE] = own[:, t * TILE : (t + 1) * TILE]
         right = [
             jnp.where(sub < 3, spread(model_ref[c, k : k + 1, :], 8), spread(model_ref[c, 3 + k : 4 + k, :], 8))
             for k in range(3)
@@ -267,23 +283,21 @@
     def model(c, part):
         slot = lax.rem(c, 2)
         for ti in parts[part]:
-            for p in (0, 1):
-                yield
-                pair = lax.dot_general(
-                    left_ref[slot, p, :, ti * TILE : (ti + 1) * TILE],
-                    right_ref[slot, :, ti * TILE :],
-                    (((0,), (0,)), ((), ())),
-                    preferred_element_type=jnp.float32,
-                )
-                for tj in range(ti, tiles):
-                    at = slice((tj - ti) * TILE, (tj - ti + 1) * TILE)
-                    pair_ref[place[ti, tj] + (p,)] = pair[:, at]
+            yield
+            pair = lax.dot_general(
+                left_ref[slot, ti], right_ref[slot, :, ti * TILE :], (((0,), (0,)), ((), ())),
+                preferred_element_type=jnp.float32,
+            )
+            for tj in range(ti, tiles):
+                at = slice((tj - ti) * TILE, (tj - ti + 1) * TILE)
+                for p in (0, 1):
+                    pair_ref[place[ti, tj] + (p,)] = pair[p * TILE : (p + 1) * TILE, at]
 
     @pl.when(c == 0)
     def _():
         rows_ref[...] = jnp.zeros_like(rows_ref)
-        acc_ref[...] = jnp.zeros_like(acc_ref)
-        gains = solve_update(rows_of(gains_ref, 3), rows_of(old_ref, 6))
+        old = add_up([ref[...] for ref in old_refs])
+        gains = solve_update(rows_of(gains_ref, 3), [old[k : k + 1, :] for k in range(6)])
         new_ref[...] = gains
         angles = gains[1:2] + freq_ref[...] * gains[2:3]
         amplitude = gains[0:1] * mask_ref[...]
@@ -342,13 +356,12 @@
                 ahead = model(jnp.minimum(c + 1, last), 0)
             if part == 0:
                 load_channel(jnp.minimum(c + 1, last))
-            pair_sums(c, parts[part], tiles, terms, ahead, cols_ref, acc_ref, rows_ref)
+            pair_sums(c, parts[part], tiles, terms, ahead, cols_ref, rows_ref)
             if part + 1 == len(parts):
                 store_cols(c, cols_ref, colsum_ref)
 
     @pl.when(c == last)
     def _():
-        fold_rows(c, 0, inputs, acc_ref, rows_ref)
         totals = channel_totals(tiles, rows_ref, colsum_ref, (0.125, 0.125, 0.25))
         store_sums(totals, weight_ref[...], freq_ref[...], sums_ref)
         bound = jnp.maximum(totals[2], 1.0)
@@ -361,6 +374,36 @@
 
 
 RESIDENT = pl.BlockSpec(memory_space=pltpu.VMEM)
+
+
+def held(x):
+    return pltpu.with_memory_space_constraint(x, pltpu.VMEM)
+
+
+def split_kernel(volt_ref, out_ref, sems):
+    devices, _, chans, _ = out_ref.shape
+    copies = [
+        pltpu.make_async_copy(volt_ref.at[:, d * chans : (d + 1) * chans, :], out_ref.at[d], sems.at[d])
+        for d in range(devices)
+    ]
+    for copy in copies:
+        copy.start()
+    for copy in copies:
+        copy.wait()
+
+
+def split_channels(voltages, devices):
+    inputs_dev, channels, width = voltages.shape
+    return pl.pallas_call(
+        split_kernel,
+        in_specs=[pl.BlockSpec(memory_space=pltpu.HBM)],
+        out_specs=pl.BlockSpec(memory_space=pl.ANY),
+        out_shape=jax.ShapeDtypeStruct(
+            (devices, inputs_dev, channels // devices, width), voltages.dtype
+        ),
+        scratch_shapes=[pltpu.SemaphoreType.DMA((devices,))],
+        name="split_channels",
+    )(pltpu.with_memory_space_constraint(voltages, pltpu.HBM))
 
 
 def first_iteration(x, mask, weight, freq):
@@ -383,8 +426,8 @@
             pltpu.VMEM((2, tiles, 2 * TILE, width), jnp.bfloat16),
             pltpu.VMEM((inputs, TILE), jnp.float32),
             pltpu.VMEM((steps, size, TILE, TILE), jnp.float32),
+            pltpu.VMEM((size, 2, TILE, TILE), jnp.bfloat16),
             pltpu.VMEM((3, 8, inputs), jnp.float32),
-            pltpu.VMEM((3, inputs, TILE), jnp.float32),
             pltpu.VMEM((inputs, TILE), jnp.float32),
             pltpu.VMEM((chans, 8, inputs), jnp.float32),
         ],
@@ -393,21 +436,15 @@
     )(mask, weight, freq, x)
 
 
-def held(x):
-    return pltpu.with_memory_space_constraint(x, pltpu.VMEM)
-
-
 def next_iteration(gains, old_sums, mask, weight, freq, vis, size):
     chans, steps, count = size.shape[:3]
     inputs = mask.shape[1]
     tiles = inputs // TILE
     return pl.pallas_call(
-        next_kernel,
+        functools.partial(next_kernel, len(old_sums)),
         grid=(chans,),
-        in_specs=[
-            whole(gains.shape), whole(old_sums.shape), whole(mask.shape), whole(weight.shape),
-            whole(freq.shape),
-        ] + [RESIDENT, RESIDENT],
+        in_specs=[whole(gains.shape), whole(mask.shape), whole(weight.shape), whole(freq.shape)]
+        + [RESIDENT, RESIDENT] + [whole((6, inputs)) for _ in old_sums],
         out_specs=[whole((6, inputs)), whole((3, inputs)), whole((2, chans, inputs))],
         out_shape=[
             jax.ShapeDtypeStruct((6, inputs), jnp.float32),
@@ -418,21 +455,26 @@
             pltpu.VMEM((chans, 16, inputs), jnp.float32),
             pltpu.VMEM((steps, count, 2, TILE, TILE), jnp.float32),
             pltpu.VMEM((steps, count, TILE, TILE), jnp.float32),
-            pltpu.VMEM((2, 2, 32, inputs), jnp.bfloat16),
+            pltpu.VMEM((2, tiles, 32, 2 * TILE), jnp.bfloat16),
             pltpu.VMEM((2, 32, inputs), jnp.bfloat16),
             pltpu.VMEM((3, 8, inputs), jnp.float32),
-            pltpu.VMEM((3, inputs, TILE), jnp.float32),
             pltpu.VMEM((inputs, TILE), jnp.float32),
             pltpu.VMEM((chans, 8, inputs), jnp.float32),
         ],
         compiler_params=pltpu.CompilerParams(vmem_limit_bytes=VMEM_LIMIT),
         name="next_iteration",
-    )(gains, old_sums, mask, weight, freq, held(vis), held(size))
+    )(gains, mask, weight, freq, held(vis), held(size), *old_sums)
+
+
+def add_up(parts):
+    while len(parts) > 1:
+        parts = [a + b for a, b in zip(parts[::2], parts[1::2])]
+    return parts[0]
 
 
 def all_sum(part, devices):
     if devices & (devices - 1):
-        return lax.psum(part, "chan")
+        return [lax.psum(part, "chan")]
     reach = 1
     while reach < devices:
         ways = 4 if devices // reach >= 4 else 2
@@ -440,17 +482,19 @@
             lax.ppermute(part, "chan", [(i, i ^ (k * reach)) for i in range(devices)])
             for k in range(1, ways)
         ]
-        part = (got[0] + got[1]) + (got[2] + got[3]) if ways == 4 else got[0] + got[1]
         reach *= ways
-    return part
+        if reach == devices:
+            return got
+        part = add_up(got)
+    return [part]
 
 
 def local(voltages, antenna_usable_mask, channel_flags):
     devices = lax.axis_size("chan")
     inputs_dev, channels, sample_cols = voltages.shape
     chan_dev = channels // devices
-    blocks = voltages.reshape(inputs_dev, devices, chan_dev, sample_cols)
-    turned = lax.all_to_all(blocks, "chan", split_axis=1, concat_axis=0, tiled=True)
+    blocks = split_channels(voltages, devices)
+    turned = lax.all_to_all(blocks, "chan", split_axis=0, concat_axis=0, tiled=True)
     inputs = inputs_dev * devices
     arrived = turned.reshape(inputs, chan_dev, sample_cols)
     first_channel = lax.axis_index("chan") * chan_dev
@@ -467,8 +511,8 @@
         sums, gains, fitted = next_iteration(
             gains, all_sum(sums, devices), mask, weight, freq, vis, size
         )
-    totals = all_sum(sums, devices)
-    gains = solve_update([gains[k : k + 1] for k in range(3)], [totals[k : k + 1] for k in range(6)])
+    totals = add_up(all_sum(sums, devices))
+    gains = solve_rows(gains, totals)
     return (gains, fitted)
 
 

time: 169 us -> 224 us (1.33)
  Pallas kernels: 66.5 us -> 129 us
  other arithmetic: 6.25 us -> 0.78 us
  local copies, waits for them, and re-layouts: 5.46 us -> 1.44 us
  waiting for transfers between devices: 57.7 us -> 60.5 us
    pallas_call x2 -> x3, Pallas kernels: 43.9 us -> 108 us  [the longest x1 64.8 us: split_channels(): pl.pallas_call(split_kernel, in_specs=[pl.BlockSpec(memory_space=pltpu.HB...]
    reshape x1 -> x0, local copies, waits for them, and re-layouts: 3.46 us -> none  [local(): blocks = voltages.reshape(inputs_dev, devices, chan_dev, sample_cols)]
    add x6 -> x5, other arithmetic: 3.57 us -> 0.72 us  [the longest x1 0.68 us: solve_rows(): gains + damping * jnp.where(row == 0, ratio, jnp.where(row == 1, phase, d...]
  transfers between devices with their start and end apart: 19 -> 19, of which waited for: 14 -> 13; matrix products, arithmetic and copies ran while one was open for 1% -> 0% of each run, Pallas kernels for 0% -> 0%
where the time goes in v3:
time: 224 us
  Pallas kernels  129 us (58%)
  waiting for transfers between devices  60.5 us (27%)
  starting transfers between devices  31.4 us (14%)
    pallas_call x1, Pallas kernels, split_channels(): pl.pallas_call(split_kernel, in_specs=[pl.BlockSpec(memory_space=pltpu.HB...  64.8 us
    pallas_call x2, Pallas kernels, next_iteration(): pl.pallas_call(functools.partial(next_kernel, len(old_sums)), grid=(chans...  42.8 us
    all_to_all x1, waiting for transfers between devices, local(): lax.all_to_all(blocks, 'chan', split_axis=0, concat_axis=0, tiled=True)  41 us
    ppermute x18, starting transfers between devices, all_sum(): lax.ppermute(part, 'chan', [(i, i ^ k * reach) for i in range(devices)])  24.1 us
    pallas_call x1, Pallas kernels, first_iteration(): pl.pallas_call(first_kernel, grid=(chans,), in_specs=[whole(mask.shape),...  21.6 us
    ppermute x18, waiting for transfers between devices, all_sum(): lax.ppermute(part, 'chan', [(i, i ^ k * reach) for i in range(devices)])  19.6 us
    all_to_all x1, starting transfers between devices, local(): lax.all_to_all(blocks, 'chan', split_axis=0, concat_axis=0, tiled=True)  7.4 us
  transfers between devices with their start and end apart: 19, of which 13 were waited for; matrix products, arithmetic and copies ran while one was open for 0% of the time, Pallas kernels for 0%

profile of v3, /device:TPU:0, one launch (start us, length us, event | category | flops | bytes accessed | tf_op | source)
XLA Modules:
  0.0 224.1 jit_solution(10593920233129978684)
XLA Ops:
  0.6 64.8 %split_channels.1 = bf16[16,64,8,128]{3,2,1,0:T(8,128)(2,1)} custom-call(bf16[64,128,128]{2,1,0:T(8,128)(2,1)} %volt_ref.1), custom_call_target="tpu_custom_call" | custom-call | tf_op jit(solution)/shard_map/split_channels/pallas_call | solution.py:397
  65.4 7.4 %all-to-all-start = ((bf16[16,64,8,128]{3,2,1,0:T(8,128)(2,1)}), bf16[16,64,8,128]{3,2,1,0:T(8,128)(2,1)S(1)}, u32[]{:S(2)}, u32[]{:S(2)}) async-start(bf16[16,64,8,128]{3,2,1,0:T(8,128)(2,1)} %split_channels.1), calls=%async_computation | async-start | bytes 4194304 | tf_op jit(solution)/shard_map/all_to_all | solution.py:497
  73.0 41.0 %all-to-all-done = bf16[16,64,8,128]{3,2,1,0:T(8,128)(2,1)S(1)} async-done(((bf16[16,64,8,128]{3,2,1,0:T(8,128)(2,1)}), bf16[16,64,8,128]{3,2,1,0:T(8,128)(2,1)S(1)}, u32[]{:S(2)}, u32[]{:S(2)}) %all-to-all-start) | async-done | bytes 2097184 | tf_op jit(solution)/shard_map/all_to_all | solution.py:497
  113.9 1.3 copy-done.1
  115.3 21.6 %first_iteration.1 = (bf16[8,2,18,2,128,128]{5,4,3,2,1,0:T(8,128)(2,1)S(1)}, f32[8,2,18,128,128]{4,3,2,1,0:T(8,128)S(1)}, f32[6,1024]{1,0:T(8,128)S(1)}) custom-call(f32[1,1024]{1,0:T(1,128)S(1)} %bitcast.7, f32[8,1]{1,0:T(8,128)S(1)} %copy.6.weight_ref, f32[8,1]{1,0:T(8,128)S(1)} %add_multiply_fusion.freq_ref, bf16[1024,8,128]{2,1,0:T(8,128)(2,1)} %bitcast.10), custom_call_target="tpu_custom_call" | custom-call | tf_op jit(solution)/shard_map/first_iteration/pallas_call | solution.py:413
  136.9 0.8 collective-permute-start
  137.8 3.4 %collective-permute-start.1 = (f32[6,1024]{1,0:T(8,128)S(1)}, f32[6,1024]{1,0:T(8,128)S(1)}, u32[]{:S(2)}, u32[]{:S(2)}) collective-permute-start(f32[6,1024]{1,0:T(8,128)S(1)} %get-tuple-element.12), channel_id=1, source_target_pairs={{0,2},{1,3},{2,0},{3,1},{4,6},{5,7},{6,4},{7,5},{8,10},{9,11},{10,... | collective-permute-start | bytes 73736 | tf_op jit(solution)/shard_map/ppermute | solution.py:482
  141.1 1.9 collective-permute-done.1
  143.0 1.8 collective-permute-done.2
  144.8 5.7 %collective-permute-start.3 = (f32[6,1024]{1,0:T(8,128)S(1)}, f32[6,1024]{1,0:T(8,128)S(1)}, u32[]{:S(2)}, u32[]{:S(2)}) collective-permute-start(f32[6,1024]{1,0:T(8,128)S(1)} %add_add_fusion.3.refs_0_), channel_id=1, source_target_pairs={{0,4},{1,5},{2,6},{3,7},{4,0},{5,1},{6,2},{7,3},{8,12},{9,13},{10,... | collective-permute-start | bytes 73736 | tf_op jit(solution)/shard_map/ppermute | solution.py:482
  150.5 1.4 collective-permute-start.4
  151.9 1.0 collective-permute-start.5
  152.9 2.5 %collective-permute-done.4.refs_2_ = f32[6,1024]{1,0:T(8,128)S(1)} collective-permute-done((f32[6,1024]{1,0:T(8,128)S(1)}, f32[6,1024]{1,0:T(8,128)S(1)}, u32[]{:S(2)}, u32[]{:S(2)}) %collective-permute-start.4) | collective-permute-done | bytes 24608 | tf_op jit(solution)/shard_map/ppermute | solution.py:482
  155.5 2.1 collective-permute-done.5.refs_3_
  157.6 21.4 %next_iteration.2 = (f32[6,1024]{1,0:T(8,128)S(1)}, f32[3,1024]{1,0:T(4,128)S(1)}, f32[2,8,1024]{2,1,0:T(8,128)}) custom-call(f32[3,1024]{1,0:T(4,128)S(1)} %copy-done, f32[1,1024]{1,0:T(1,128)S(1)} %bitcast.8, f32[8,1]{1,0:T(8,128)S(1)} %copy.6.weight_ref, f32[8,1]{1,0:T(8,128)S(1)} %add_multiply_fusion.freq_ref, ...), custom_call_target="tpu_custom_call" | custom-call | tf_op jit(solution)/shard_map/next_iteration/pallas_call | solution.py:443
  179.3 1.5 collective-permute-start.8
  180.9 2.3 %collective-permute-done.7 = f32[6,1024]{1,0:T(8,128)S(1)} collective-permute-done((f32[6,1024]{1,0:T(8,128)S(1)}, f32[6,1024]{1,0:T(8,128)S(1)}, u32[]{:S(2)}, u32[]{:S(2)}) %collective-permute-start.7) | collective-permute-done | bytes 24608 | tf_op jit(solution)/shard_map/ppermute | solution.py:482
  183.3 1.7 collective-permute-start.11
  185.0 1.7 collective-permute-start.9
  186.7 1.7 collective-permute-done.10.refs_2_
  188.4 0.7 collective-permute-done.11.refs_3_
  189.3 21.4 %next_iteration.3 = (f32[6,1024]{1,0:T(8,128)S(1)}, f32[3,1024]{1,0:T(4,128)S(1)}, f32[2,8,1024]{2,1,0:T(8,128)}) custom-call(f32[3,1024]{1,0:T(4,128)S(1)} %get-tuple-element.13.gains_ref, f32[1,1024]{1,0:T(1,128)S(1)} %bitcast.9, f32[8,1]{1,0:T(8,128)S(1)} %copy.6.weight_ref, f32[8,1]{1,0:T(8,128)S(1)} %add_multiply_fusion.freq_ref, ...), custom_call_target="tpu_custom_call" | custom-call | tf_op jit(solution)/shard_map/next_iteration/pallas_call | solution.py:443
  210.7 1.1 collective-permute-start.13
  211.8 0.8 collective-permute-start.14
  212.5 2.1 collective-permute-done.13
  214.6 0.5 collective-permute-done.14
  215.1 1.6 collective-permute-start.15
  216.7 1.0 collective-permute-start.16
  217.7 1.9 collective-permute-start.17
  219.6 2.6 %collective-permute-done.16 = f32[6,1024]{1,0:T(8,128)S(1)} collective-permute-done((f32[6,1024]{1,0:T(8,128)S(1)}, f32[6,1024]{1,0:T(8,128)S(1)}, u32[]{:S(2)}, u32[]{:S(2)}) %collective-permute-start.16) | collective-permute-done | bytes 24608 | tf_op jit(solution)/shard_map/ppermute | solution.py:482
  222.2 1.2 collective-permute-done.17
  223.4 0.7 multiply_add_fusion
  (29 shorter events, 0.8 us)
Async XLA Ops:
  65.4 7.4 %copy-start.3 = (s32[8]{0:T(128)S(1)}, s32[8]{0:T(128)}, u32[]{:S(2)}) copy-start(s32[8]{0:T(128)} %param.5) | copy-start | bytes 100
  65.4 7.5 %copy-start.2 = (s32[1024]{0:T(1024)S(1)}, s32[1024]{0:T(1024)}, u32[]{:S(2)}) copy-start(s32[1024]{0:T(1024)} %param.4) | copy-start | bytes 12292
  65.4 48.5 %all-to-all-start = ((bf16[16,64,8,128]{3,2,1,0:T(8,128)(2,1)}), bf16[16,64,8,128]{3,2,1,0:T(8,128)(2,1)S(1)}, u32[]{:S(2)}, u32[]{:S(2)}) async-start(bf16[16,64,8,128]{3,2,1,0:T(8,128)(2,1)} %split_channels.1), calls=%async_computation | async-start | bytes 4194304 | tf_op jit(solution)/shard_map/all_to_all | solution.py:497
  72.8 84.8 %copy-start = (f32[3,1024]{1,0:T(4,128)S(1)}, f32[3,1024]{1,0:T(4,128)}, u32[]{:S(2)}) copy-start(f32[3,1024]{1,0:T(4,128)} %constant.8.clone.1.gains_ref) | copy-start | bytes 36868
  113.9 1.3 copy-start.1
  136.9 4.2 %collective-permute-start = (f32[6,1024]{1,0:T(8,128)S(1)}, f32[6,1024]{1,0:T(8,128)S(1)}, u32[]{:S(2)}, u32[]{:S(2)}) collective-permute-start(f32[6,1024]{1,0:T(8,128)S(1)} %get-tuple-element.12), channel_id=1, source_target_pairs={{0,1},{1,0},{2,3},{3,2},{4,5},{5,4},{6,7},{7,6},{8,9},{9,8},{10,11... | collective-permute-start | bytes 73736 | tf_op jit(solution)/shard_map/ppermute | solution.py:482
  137.8 5.3 %collective-permute-start.1 = (f32[6,1024]{1,0:T(8,128)S(1)}, f32[6,1024]{1,0:T(8,128)S(1)}, u32[]{:S(2)}, u32[]{:S(2)}) collective-permute-start(f32[6,1024]{1,0:T(8,128)S(1)} %get-tuple-element.12), channel_id=1, source_target_pairs={{0,2},{1,3},{2,0},{3,1},{4,6},{5,7},{6,4},{7,5},{8,10},{9,11},{10,... | collective-permute-start | bytes 73736 | tf_op jit(solution)/shard_map/ppermute | solution.py:482
  141.1 3.7 %collective-permute-start.2 = (f32[6,1024]{1,0:T(8,128)S(1)}, f32[6,1024]{1,0:T(8,128)S(1)}, u32[]{:S(2)}, u32[]{:S(2)}) collective-permute-start(f32[6,1024]{1,0:T(8,128)S(1)} %get-tuple-element.12), channel_id=1, source_target_pairs={{0,3},{1,2},{2,1},{3,0},{4,7},{5,6},{6,5},{7,4},{8,11},{9,10},{10,... | collective-permute-start | bytes 73736 | tf_op jit(solution)/shard_map/ppermute | solution.py:482
  144.8 8.1 %collective-permute-start.3 = (f32[6,1024]{1,0:T(8,128)S(1)}, f32[6,1024]{1,0:T(8,128)S(1)}, u32[]{:S(2)}, u32[]{:S(2)}) collective-permute-start(f32[6,1024]{1,0:T(8,128)S(1)} %add_add_fusion.3.refs_0_), channel_id=1, source_target_pairs={{0,4},{1,5},{2,6},{3,7},{4,0},{5,1},{6,2},{7,3},{8,12},{9,13},{10,... | collective-permute-start | bytes 73736 | tf_op jit(solution)/shard_map/ppermute | solution.py:482
  150.5 5.0 %collective-permute-start.4 = (f32[6,1024]{1,0:T(8,128)S(1)}, f32[6,1024]{1,0:T(8,128)S(1)}, u32[]{:S(2)}, u32[]{:S(2)}) collective-permute-start(f32[6,1024]{1,0:T(8,128)S(1)} %add_add_fusion.3.refs_0_), channel_id=1, source_target_pairs={{0,8},{1,9},{2,10},{3,11},{4,12},{5,13},{6,14},{7,15},{8,0},{9,1},... | collective-permute-start | bytes 73736 | tf_op jit(solution)/shard_map/ppermute | solution.py:482
  151.9 5.7 %collective-permute-start.5 = (f32[6,1024]{1,0:T(8,128)S(1)}, f32[6,1024]{1,0:T(8,128)S(1)}, u32[]{:S(2)}, u32[]{:S(2)}) collective-permute-start(f32[6,1024]{1,0:T(8,128)S(1)} %add_add_fusion.3.refs_0_), channel_id=1, source_target_pairs={{0,12},{1,13},{2,14},{3,15},{4,8},{5,9},{6,10},{7,11},{8,4},{9,5},... | collective-permute-start | bytes 73736 | tf_op jit(solution)/shard_map/ppermute | solution.py:482
  179.0 1.9 collective-permute-start.6
  179.0 4.2 %collective-permute-start.7 = (f32[6,1024]{1,0:T(8,128)S(1)}, f32[6,1024]{1,0:T(8,128)S(1)}, u32[]{:S(2)}, u32[]{:S(2)}) collective-permute-start(f32[6,1024]{1,0:T(8,128)S(1)} %get-tuple-element.14), channel_id=1, source_target_pairs={{0,2},{1,3},{2,0},{3,1},{4,6},{5,7},{6,4},{7,5},{8,10},{9,11},{10,... | collective-permute-start | bytes 73736 | tf_op jit(solution)/shard_map/ppermute | solution.py:482
  179.3 3.8 %collective-permute-start.8 = (f32[6,1024]{1,0:T(8,128)S(1)}, f32[6,1024]{1,0:T(8,128)S(1)}, u32[]{:S(2)}, u32[]{:S(2)}) collective-permute-start(f32[6,1024]{1,0:T(8,128)S(1)} %get-tuple-element.14), channel_id=1, source_target_pairs={{0,3},{1,2},{2,1},{3,0},{4,7},{5,6},{6,5},{7,4},{8,11},{9,10},{10,... | collective-permute-start | bytes 73736 | tf_op jit(solution)/shard_map/ppermute | solution.py:482
  183.2 5.2 %collective-permute-start.10 = (f32[6,1024]{1,0:T(8,128)S(1)}, f32[6,1024]{1,0:T(8,128)S(1)}, u32[]{:S(2)}, u32[]{:S(2)}) collective-permute-start(f32[6,1024]{1,0:T(8,128)S(1)} %add_add_fusion.2.refs_0_), channel_id=1, source_target_pairs={{0,8},{1,9},{2,10},{3,11},{4,12},{5,13},{6,14},{7,15},{8,0},{9,1},... | collective-permute-start | bytes 73736 | tf_op jit(solution)/shard_map/ppermute | solution.py:482
  183.3 5.9 %collective-permute-start.11 = (f32[6,1024]{1,0:T(8,128)S(1)}, f32[6,1024]{1,0:T(8,128)S(1)}, u32[]{:S(2)}, u32[]{:S(2)}) collective-permute-start(f32[6,1024]{1,0:T(8,128)S(1)} %add_add_fusion.2.refs_0_), channel_id=1, source_target_pairs={{0,12},{1,13},{2,14},{3,15},{4,8},{5,9},{6,10},{7,11},{8,4},{9,5},... | collective-permute-start | bytes 73736 | tf_op jit(solution)/shard_map/ppermute | solution.py:482
  185.0 4.3 %collective-permute-start.9 = (f32[6,1024]{1,0:T(8,128)S(1)}, f32[6,1024]{1,0:T(8,128)S(1)}, u32[]{:S(2)}, u32[]{:S(2)}) collective-permute-start(f32[6,1024]{1,0:T(8,128)S(1)} %add_add_fusion.2.refs_0_), channel_id=1, source_target_pairs={{0,4},{1,5},{2,6},{3,7},{4,0},{5,1},{6,2},{7,3},{8,12},{9,13},{10,... | collective-permute-start | bytes 73736 | tf_op jit(solution)/shard_map/ppermute | solution.py:482
  210.7 1.9 collective-permute-start.12
  210.7 3.9 %collective-permute-start.13 = (f32[6,1024]{1,0:T(8,128)S(1)}, f32[6,1024]{1,0:T(8,128)S(1)}, u32[]{:S(2)}, u32[]{:S(2)}) collective-permute-start(f32[6,1024]{1,0:T(8,128)S(1)} %get-tuple-element.16), channel_id=1, source_target_pairs={{0,2},{1,3},{2,0},{3,1},{4,6},{5,7},{6,4},{7,5},{8,10},{9,11},{10,... | collective-permute-start | bytes 73736 | tf_op jit(solution)/shard_map/ppermute | solution.py:482
  211.8 3.3 %collective-permute-start.14 = (f32[6,1024]{1,0:T(8,128)S(1)}, f32[6,1024]{1,0:T(8,128)S(1)}, u32[]{:S(2)}, u32[]{:S(2)}) collective-permute-start(f32[6,1024]{1,0:T(8,128)S(1)} %get-tuple-element.16), channel_id=1, source_target_pairs={{0,3},{1,2},{2,1},{3,0},{4,7},{5,6},{6,5},{7,4},{8,11},{9,10},{10,... | collective-permute-start | bytes 73736 | tf_op jit(solution)/shard_map/ppermute | solution.py:482
  215.1 4.5 %collective-permute-start.15 = (f32[6,1024]{1,0:T(8,128)S(1)}, f32[6,1024]{1,0:T(8,128)S(1)}, u32[]{:S(2)}, u32[]{:S(2)}) collective-permute-start(f32[6,1024]{1,0:T(8,128)S(1)} %add_add_fusion.1), channel_id=1, source_target_pairs={{0,4},{1,5},{2,6},{3,7},{4,0},{5,1},{6,2},{7,3},{8,12},{9,13},{10,... | collective-permute-start | bytes 73736 | tf_op jit(solution)/shard_map/ppermute | solution.py:482
  216.7 5.5 %collective-permute-start.16 = (f32[6,1024]{1,0:T(8,128)S(1)}, f32[6,1024]{1,0:T(8,128)S(1)}, u32[]{:S(2)}, u32[]{:S(2)}) collective-permute-start(f32[6,1024]{1,0:T(8,128)S(1)} %add_add_fusion.1), channel_id=1, source_target_pairs={{0,8},{1,9},{2,10},{3,11},{4,12},{5,13},{6,14},{7,15},{8,0},{9,1},... | collective-permute-start | bytes 73736 | tf_op jit(solution)/shard_map/ppermute | solution.py:482
  217.7 5.7 %collective-permute-start.17 = (f32[6,1024]{1,0:T(8,128)S(1)}, f32[6,1024]{1,0:T(8,128)S(1)}, u32[]{:S(2)}, u32[]{:S(2)}) collective-permute-start(f32[6,1024]{1,0:T(8,128)S(1)} %add_add_fusion.1), channel_id=1, source_target_pairs={{0,12},{1,13},{2,14},{3,15},{4,8},{5,9},{6,10},{7,11},{8,4},{9,5},... | collective-permute-start | bytes 73736 | tf_op jit(solution)/shard_map/ppermute | solution.py:482

commit v4 on v3

--- a/solution.py
+++ b/solution.py
@@ -1,4 +1,5 @@
 import functools
+import itertools
 import math
 
 import jax
@@ -10,10 +11,8 @@
 
 ITERS = 3
 TILE = 128
-GROUP = 32
 UNIT = 16
 PARTS = 2
-AHEAD = 1
 HUGE = 1e38
 VMEM_LIMIT = 16 * 1024 * 1024
 
@@ -61,16 +60,16 @@
         pass
 
 
-def pair_sums(c, rows, tiles, terms, ahead, cols_ref, rows_ref):
+def pair_sums(c, rows, tiles, group, terms, ahead, cols_ref, rows_ref):
     for ti in rows:
-        for first in range(0, TILE, GROUP):
-            for _ in range(AHEAD):
+        for first in range(0, TILE, group):
+            for _ in range(1 + group // 64):
                 next(ahead, None)
             row = ti * TILE + first
-            totals = [None] * (GROUP // UNIT)
+            totals = [None] * (group // UNIT)
             for tj in range(ti, tiles):
                 parts = None
-                for unit in range(GROUP // UNIT):
+                for unit in range(group // UNIT):
                     at = first + unit * UNIT
                     keep = None
                     if tj == ti:
@@ -88,7 +87,7 @@
                     lanes = slice(tj * TILE, (tj + 1) * TILE)
                     for k in range(3):
                         cols_ref[k, :, lanes] += parts[k] if k != 1 else -parts[k]
-            for unit in range(GROUP // UNIT):
+            for unit in range(group // UNIT):
                 fold_rows(c, row + unit * UNIT, totals[unit], rows_ref)
     drain(ahead)
 
@@ -134,7 +133,7 @@
     )
 
 
-def first_kernel(mask_ref, weight_ref, freq_ref, x_ref, vis_ref, size_ref, sums_ref,
+def first_kernel(mask_ref, weight_ref, freq_ref, arrived_ref, vis_ref, size_ref, sums_ref, x_ref, sem,
                  wide_ref, right_ref, left_ref, maskrow_ref, base_ref, ahead_ref, cols_ref,
                  rows_ref, colsum_ref):
     c = pl.program_id(0)
@@ -148,6 +147,7 @@
         lanes = lax.broadcasted_iota(jnp.int32, (TILE, width), 1)
         slot = lax.rem(c, 2)
         for t in range(tiles):
+            yield
             at = slice(t * TILE, (t + 1) * TILE)
             rows = wide_ref[pl.ds(t * TILE * chans + c, TILE, stride=chans), :]
             rows = rows * maskrow_ref[at, :]
@@ -177,7 +177,10 @@
 
     @pl.when(c == 0)
     def _():
+        copy = pltpu.make_async_copy(arrived_ref, x_ref, sem)
+        copy.start()
         rows_ref[...] = jnp.zeros_like(rows_ref)
+        copy.wait()
         for t in range(tiles):
             at = slice(t * TILE, (t + 1) * TILE)
             block = x_ref[at].astype(jnp.float32)
@@ -199,7 +202,7 @@
 
     @pl.when(c == 0)
     def _():
-        load_channel(c)
+        drain(load_channel(c))
 
     @pl.when(c == 0)
     def _():
@@ -233,8 +236,8 @@
             else:
                 ahead = correlate(jnp.minimum(c + 1, last), 0)
             if part == 0:
-                load_channel(jnp.minimum(c + 1, last))
-            pair_sums(c, parts[part], tiles, terms, ahead, cols_ref, rows_ref)
+                ahead = itertools.chain(ahead, load_channel(jnp.minimum(c + 1, last)))
+            pair_sums(c, parts[part], tiles, TILE, terms, ahead, cols_ref, rows_ref)
             if part + 1 == len(parts):
                 store_cols(c, cols_ref, colsum_ref)
 
@@ -268,6 +271,7 @@
         return jnp.broadcast_to(piece, (count, inputs))
 
     def load_channel(c):
+        yield
         slot = lax.rem(c, 2)
         for p in (0, 1):
             own = model_ref[c, 8 * p : 8 * p + 8, :]
@@ -329,7 +333,7 @@
 
     @pl.when(c == 0)
     def _():
-        load_channel(c)
+        drain(load_channel(c))
         drain(model(c, 0))
 
     def terms(ti, tj, first, keep):
@@ -355,8 +359,8 @@
             else:
                 ahead = model(jnp.minimum(c + 1, last), 0)
             if part == 0:
-                load_channel(jnp.minimum(c + 1, last))
-            pair_sums(c, parts[part], tiles, terms, ahead, cols_ref, rows_ref)
+                ahead = itertools.chain(ahead, load_channel(jnp.minimum(c + 1, last)))
+            pair_sums(c, parts[part], tiles, 32, terms, ahead, cols_ref, rows_ref)
             if part + 1 == len(parts):
                 store_cols(c, cols_ref, colsum_ref)
 
@@ -380,30 +384,24 @@
     return pltpu.with_memory_space_constraint(x, pltpu.VMEM)
 
 
-def split_kernel(volt_ref, out_ref, sems):
+def split_kernel(volt_ref, out_ref):
     devices, _, chans, _ = out_ref.shape
-    copies = [
-        pltpu.make_async_copy(volt_ref.at[:, d * chans : (d + 1) * chans, :], out_ref.at[d], sems.at[d])
-        for d in range(devices)
-    ]
-    for copy in copies:
-        copy.start()
-    for copy in copies:
-        copy.wait()
+    for d in range(devices):
+        out_ref[d] = volt_ref[:, d * chans : (d + 1) * chans, :]
 
 
 def split_channels(voltages, devices):
     inputs_dev, channels, width = voltages.shape
+    chans, rows = channels // devices, max(inputs_dev // 2, 1)
     return pl.pallas_call(
         split_kernel,
-        in_specs=[pl.BlockSpec(memory_space=pltpu.HBM)],
-        out_specs=pl.BlockSpec(memory_space=pl.ANY),
-        out_shape=jax.ShapeDtypeStruct(
-            (devices, inputs_dev, channels // devices, width), voltages.dtype
-        ),
-        scratch_shapes=[pltpu.SemaphoreType.DMA((devices,))],
+        grid=(inputs_dev // rows,),
+        in_specs=[pl.BlockSpec((rows, channels, width), lambda i: (i, 0, 0))],
+        out_specs=pl.BlockSpec((devices, rows, chans, width), lambda i: (0, i, 0, 0)),
+        out_shape=jax.ShapeDtypeStruct((devices, inputs_dev, chans, width), voltages.dtype),
+        compiler_params=pltpu.CompilerParams(vmem_limit_bytes=VMEM_LIMIT),
         name="split_channels",
-    )(pltpu.with_memory_space_constraint(voltages, pltpu.HBM))
+    )(voltages)
 
 
 def first_iteration(x, mask, weight, freq):
@@ -413,7 +411,8 @@
     return pl.pallas_call(
         first_kernel,
         grid=(chans,),
-        in_specs=[whole(mask.shape), whole(weight.shape), whole(freq.shape), whole(x.shape)],
+        in_specs=[whole(mask.shape), whole(weight.shape), whole(freq.shape),
+                  pl.BlockSpec(memory_space=pl.ANY)],
         out_specs=[RESIDENT, RESIDENT, whole((6, inputs))],
         out_shape=[
             pltpu.VMEM((chans, steps, size, 2, TILE, TILE), jnp.bfloat16),
@@ -421,6 +420,8 @@
             jax.ShapeDtypeStruct((6, inputs), jnp.float32),
         ],
         scratch_shapes=[
+            pltpu.VMEM((inputs, chans, width), x.dtype),
+            pltpu.SemaphoreType.DMA,
             pltpu.VMEM((inputs * chans, width), jnp.float32),
             pltpu.VMEM((2, inputs, width), jnp.bfloat16),
             pltpu.VMEM((2, tiles, 2 * TILE, width), jnp.bfloat16),

time: 224 us -> 160 us (0.71)
  Pallas kernels: 129 us -> 63 us
    pallas_call x1, Pallas kernels: 64.8 us -> 1.49 us  [split_channels(): pl.pallas_call(split_kernel, grid=(inputs_dev // rows,), in_specs=[pl.Blo...]
  transfers between devices with their start and end apart: 19 -> 19, of which waited for: 13 -> 12; matrix products, arithmetic and copies ran while one was open for 0% -> 0% of each run, Pallas kernels for 0% -> 0%
where the time goes in v4:
time: 160 us
  Pallas kernels  63 us (39%)
  waiting for transfers between devices  60.5 us (38%)
  starting transfers between devices  31.6 us (20%)
  local copies, waits for them, and re-layouts  3.02 us (2%)
    all_to_all x1, waiting for transfers between devices, local(): lax.all_to_all(blocks, 'chan', split_axis=0, concat_axis=0, tiled=True)  41 us
    pallas_call x2, Pallas kernels, next_iteration(): pl.pallas_call(functools.partial(next_kernel, len(old_sums)), grid=(chans...  40.9 us
    ppermute x18, starting transfers between devices, all_sum(): lax.ppermute(part, 'chan', [(i, i ^ k * reach) for i in range(devices)])  24.1 us
    pallas_call x1, Pallas kernels, first_iteration(): pl.pallas_call(first_kernel, grid=(chans,), in_specs=[whole(mask.shape),...  20.6 us
    ppermute x18, waiting for transfers between devices, all_sum(): lax.ppermute(part, 'chan', [(i, i ^ k * reach) for i in range(devices)])  19.6 us
    all_to_all x1, starting transfers between devices, local(): lax.all_to_all(blocks, 'chan', split_axis=0, concat_axis=0, tiled=True)  7.52 us
  transfers between devices with their start and end apart: 19, of which 12 were waited for; matrix products, arithmetic and copies ran while one was open for 0% of the time, Pallas kernels for 0%

profile of v4, /device:TPU:0, one launch (start us, length us, event | category | flops | bytes accessed | tf_op | source)
XLA Modules:
  0.0 159.7 jit_solution(5320824158757056256)
XLA Ops:
  0.6 1.6 copy-done
  2.2 1.5 split_channels.1
  3.7 7.5 %all-to-all-start = ((bf16[16,64,8,128]{3,2,1,0:T(8,128)(2,1)}), bf16[16,64,8,128]{3,2,1,0:T(8,128)(2,1)S(1)}, u32[]{:S(2)}, u32[]{:S(2)}) async-start(bf16[16,64,8,128]{3,2,1,0:T(8,128)(2,1)} %split_channels.1), calls=%async_computation | async-start | bytes 4194304 | tf_op jit(solution)/shard_map/all_to_all | solution.py:498
  11.4 41.0 %all-to-all-done = bf16[16,64,8,128]{3,2,1,0:T(8,128)(2,1)S(1)} async-done(((bf16[16,64,8,128]{3,2,1,0:T(8,128)(2,1)}), bf16[16,64,8,128]{3,2,1,0:T(8,128)(2,1)S(1)}, u32[]{:S(2)}, u32[]{:S(2)}) %all-to-all-start) | async-done | bytes 2097184 | tf_op jit(solution)/shard_map/all_to_all | solution.py:498
  52.4 1.3 copy-done.2
  53.7 20.6 %first_iteration.1 = (bf16[8,2,18,2,128,128]{5,4,3,2,1,0:T(8,128)(2,1)S(1)}, f32[8,2,18,128,128]{4,3,2,1,0:T(8,128)S(1)}, f32[6,1024]{1,0:T(8,128)S(1)}) custom-call(f32[1,1024]{1,0:T(1,128)S(1)} %bitcast.7, f32[8,1]{1,0:T(8,128)S(1)} %copy.6.weight_ref, f32[8,1]{1,0:T(8,128)S(1)} %add_multiply_fusion.freq_ref, bf16[1024,8,128]{2,1,0:T(8,128)(2,1)} %bitcast.10), custom_call_target="tpu_custom_call" | custom-call | tf_op jit(solution)/shard_map/first_iteration/pallas_call | solution.py:411
  74.3 0.8 collective-permute-start
  75.1 3.4 %collective-permute-start.1 = (f32[6,1024]{1,0:T(8,128)S(1)}, f32[6,1024]{1,0:T(8,128)S(1)}, u32[]{:S(2)}, u32[]{:S(2)}) collective-permute-start(f32[6,1024]{1,0:T(8,128)S(1)} %get-tuple-element.12), channel_id=1, source_target_pairs={{0,2},{1,3},{2,0},{3,1},{4,6},{5,7},{6,4},{7,5},{8,10},{9,11},{10,... | collective-permute-start | bytes 73736 | tf_op jit(solution)/shard_map/ppermute | solution.py:483
  78.5 1.9 %collective-permute-done.1 = f32[6,1024]{1,0:T(8,128)S(1)} collective-permute-done((f32[6,1024]{1,0:T(8,128)S(1)}, f32[6,1024]{1,0:T(8,128)S(1)}, u32[]{:S(2)}, u32[]{:S(2)}) %collective-permute-start.1) | collective-permute-done | bytes 24608 | tf_op jit(solution)/shard_map/ppermute | solution.py:483
  80.4 1.8 %collective-permute-done.2 = f32[6,1024]{1,0:T(8,128)S(1)} collective-permute-done((f32[6,1024]{1,0:T(8,128)S(1)}, f32[6,1024]{1,0:T(8,128)S(1)}, u32[]{:S(2)}, u32[]{:S(2)}) %collective-permute-start.2) | collective-permute-done | bytes 24608 | tf_op jit(solution)/shard_map/ppermute | solution.py:483
  82.2 5.7 %collective-permute-start.3 = (f32[6,1024]{1,0:T(8,128)S(1)}, f32[6,1024]{1,0:T(8,128)S(1)}, u32[]{:S(2)}, u32[]{:S(2)}) collective-permute-start(f32[6,1024]{1,0:T(8,128)S(1)} %add_add_fusion.3.refs_0_), channel_id=1, source_target_pairs={{0,4},{1,5},{2,6},{3,7},{4,0},{5,1},{6,2},{7,3},{8,12},{9,13},{10,... | collective-permute-start | bytes 73736 | tf_op jit(solution)/shard_map/ppermute | solution.py:483
  87.9 1.4 collective-permute-start.4
  89.3 1.0 collective-permute-start.5
  90.3 2.5 %collective-permute-done.4.refs_2_ = f32[6,1024]{1,0:T(8,128)S(1)} collective-permute-done((f32[6,1024]{1,0:T(8,128)S(1)}, f32[6,1024]{1,0:T(8,128)S(1)}, u32[]{:S(2)}, u32[]{:S(2)}) %collective-permute-start.4) | collective-permute-done | bytes 24608 | tf_op jit(solution)/shard_map/ppermute | solution.py:483
  92.8 2.2 %collective-permute-done.5.refs_3_ = f32[6,1024]{1,0:T(8,128)S(1)} collective-permute-done((f32[6,1024]{1,0:T(8,128)S(1)}, f32[6,1024]{1,0:T(8,128)S(1)}, u32[]{:S(2)}, u32[]{:S(2)}) %collective-permute-start.5) | collective-permute-done | bytes 24608 | tf_op jit(solution)/shard_map/ppermute | solution.py:483
  95.0 20.5 %next_iteration.2 = (f32[6,1024]{1,0:T(8,128)S(1)}, f32[3,1024]{1,0:T(4,128)S(1)}, f32[2,8,1024]{2,1,0:T(8,128)}) custom-call(f32[3,1024]{1,0:T(4,128)S(1)} %copy-done.1, f32[1,1024]{1,0:T(1,128)S(1)} %bitcast.8, f32[8,1]{1,0:T(8,128)S(1)} %copy.6.weight_ref, f32[8,1]{1,0:T(8,128)S(1)} %add_multiply_fusion.freq_ref, ...), custom_call_target="tpu_custom_call" | custom-call | tf_op jit(solution)/shard_map/next_iteration/pallas_call | solution.py:444
  115.8 1.6 collective-permute-start.8
  117.4 2.3 %collective-permute-done.7 = f32[6,1024]{1,0:T(8,128)S(1)} collective-permute-done((f32[6,1024]{1,0:T(8,128)S(1)}, f32[6,1024]{1,0:T(8,128)S(1)}, u32[]{:S(2)}, u32[]{:S(2)}) %collective-permute-start.7) | collective-permute-done | bytes 24608 | tf_op jit(solution)/shard_map/ppermute | solution.py:483
  119.8 1.7 %collective-permute-start.11 = (f32[6,1024]{1,0:T(8,128)S(1)}, f32[6,1024]{1,0:T(8,128)S(1)}, u32[]{:S(2)}, u32[]{:S(2)}) collective-permute-start(f32[6,1024]{1,0:T(8,128)S(1)} %add_add_fusion.2.refs_0_), channel_id=1, source_target_pairs={{0,12},{1,13},{2,14},{3,15},{4,8},{5,9},{6,10},{7,11},{8,4},{9,5},... | collective-permute-start | bytes 73736 | tf_op jit(solution)/shard_map/ppermute | solution.py:483
  121.4 1.8 %collective-permute-start.9 = (f32[6,1024]{1,0:T(8,128)S(1)}, f32[6,1024]{1,0:T(8,128)S(1)}, u32[]{:S(2)}, u32[]{:S(2)}) collective-permute-start(f32[6,1024]{1,0:T(8,128)S(1)} %add_add_fusion.2.refs_0_), channel_id=1, source_target_pairs={{0,4},{1,5},{2,6},{3,7},{4,0},{5,1},{6,2},{7,3},{8,12},{9,13},{10,... | collective-permute-start | bytes 73736 | tf_op jit(solution)/shard_map/ppermute | solution.py:483
  123.2 1.7 %collective-permute-done.10.refs_2_ = f32[6,1024]{1,0:T(8,128)S(1)} collective-permute-done((f32[6,1024]{1,0:T(8,128)S(1)}, f32[6,1024]{1,0:T(8,128)S(1)}, u32[]{:S(2)}, u32[]{:S(2)}) %collective-permute-start.10) | collective-permute-done | bytes 24608 | tf_op jit(solution)/shard_map/ppermute | solution.py:483
  124.9 0.7 collective-permute-done.11.refs_3_
  125.7 20.5 %next_iteration.3 = (f32[6,1024]{1,0:T(8,128)S(1)}, f32[3,1024]{1,0:T(4,128)S(1)}, f32[2,8,1024]{2,1,0:T(8,128)}) custom-call(f32[3,1024]{1,0:T(4,128)S(1)} %get-tuple-element.13.gains_ref, f32[1,1024]{1,0:T(1,128)S(1)} %bitcast.9, f32[8,1]{1,0:T(8,128)S(1)} %copy.6.weight_ref, f32[8,1]{1,0:T(8,128)S(1)} %add_multiply_fusion.freq_ref, ...), custom_call_target="tpu_custom_call" | custom-call | tf_op jit(solution)/shard_map/next_iteration/pallas_call | solution.py:444
  146.2 1.1 collective-permute-start.13
  147.2 0.8 collective-permute-start.14
  148.0 2.1 %collective-permute-done.13 = f32[6,1024]{1,0:T(8,128)S(1)} collective-permute-done((f32[6,1024]{1,0:T(8,128)S(1)}, f32[6,1024]{1,0:T(8,128)S(1)}, u32[]{:S(2)}, u32[]{:S(2)}) %collective-permute-start.13) | collective-permute-done | bytes 24608 | tf_op jit(solution)/shard_map/ppermute | solution.py:483
  150.6 1.6 %collective-permute-start.15 = (f32[6,1024]{1,0:T(8,128)S(1)}, f32[6,1024]{1,0:T(8,128)S(1)}, u32[]{:S(2)}, u32[]{:S(2)}) collective-permute-start(f32[6,1024]{1,0:T(8,128)S(1)} %add_add_fusion.1), channel_id=1, source_target_pairs={{0,4},{1,5},{2,6},{3,7},{4,0},{5,1},{6,2},{7,3},{8,12},{9,13},{10,... | collective-permute-start | bytes 73736 | tf_op jit(solution)/shard_map/ppermute | solution.py:483
  152.2 1.0 collective-permute-start.16
  153.2 1.8 %collective-permute-start.17 = (f32[6,1024]{1,0:T(8,128)S(1)}, f32[6,1024]{1,0:T(8,128)S(1)}, u32[]{:S(2)}, u32[]{:S(2)}) collective-permute-start(f32[6,1024]{1,0:T(8,128)S(1)} %add_add_fusion.1), channel_id=1, source_target_pairs={{0,12},{1,13},{2,14},{3,15},{4,8},{5,9},{6,10},{7,11},{8,4},{9,5},... | collective-permute-start | bytes 73736 | tf_op jit(solution)/shard_map/ppermute | solution.py:483
  155.1 2.6 %collective-permute-done.16 = f32[6,1024]{1,0:T(8,128)S(1)} collective-permute-done((f32[6,1024]{1,0:T(8,128)S(1)}, f32[6,1024]{1,0:T(8,128)S(1)}, u32[]{:S(2)}, u32[]{:S(2)}) %collective-permute-start.16) | collective-permute-done | bytes 24608 | tf_op jit(solution)/shard_map/ppermute | solution.py:483
  157.7 1.3 collective-permute-done.17
  159.0 0.7 multiply_add_fusion
  (31 shorter events, 1.1 us)
Async XLA Ops:
  0.6 1.6 copy-start
  3.7 7.5 %copy-start.4 = (s32[8]{0:T(128)S(1)}, s32[8]{0:T(128)}, u32[]{:S(2)}) copy-start(s32[8]{0:T(128)} %param.5) | copy-start | bytes 100
  3.7 7.6 %copy-start.3 = (s32[1024]{0:T(1024)S(1)}, s32[1024]{0:T(1024)}, u32[]{:S(2)}) copy-start(s32[1024]{0:T(1024)} %param.4) | copy-start | bytes 12292
  3.7 48.6 %all-to-all-start = ((bf16[16,64,8,128]{3,2,1,0:T(8,128)(2,1)}), bf16[16,64,8,128]{3,2,1,0:T(8,128)(2,1)S(1)}, u32[]{:S(2)}, u32[]{:S(2)}) async-start(bf16[16,64,8,128]{3,2,1,0:T(8,128)(2,1)} %split_channels.1), calls=%async_computation | async-start | bytes 4194304 | tf_op jit(solution)/shard_map/all_to_all | solution.py:498
  11.2 83.8 %copy-start.1 = (f32[3,1024]{1,0:T(4,128)S(1)}, f32[3,1024]{1,0:T(4,128)}, u32[]{:S(2)}) copy-start(f32[3,1024]{1,0:T(4,128)} %constant.8.clone.1.gains_ref) | copy-start | bytes 36868
  52.3 1.3 copy-start.2
  74.3 4.2 %collective-permute-start = (f32[6,1024]{1,0:T(8,128)S(1)}, f32[6,1024]{1,0:T(8,128)S(1)}, u32[]{:S(2)}, u32[]{:S(2)}) collective-permute-start(f32[6,1024]{1,0:T(8,128)S(1)} %get-tuple-element.12), channel_id=1, source_target_pairs={{0,1},{1,0},{2,3},{3,2},{4,5},{5,4},{6,7},{7,6},{8,9},{9,8},{10,11... | collective-permute-start | bytes 73736 | tf_op jit(solution)/shard_map/ppermute | solution.py:483
  75.1 5.3 %collective-permute-start.1 = (f32[6,1024]{1,0:T(8,128)S(1)}, f32[6,1024]{1,0:T(8,128)S(1)}, u32[]{:S(2)}, u32[]{:S(2)}) collective-permute-start(f32[6,1024]{1,0:T(8,128)S(1)} %get-tuple-element.12), channel_id=1, source_target_pairs={{0,2},{1,3},{2,0},{3,1},{4,6},{5,7},{6,4},{7,5},{8,10},{9,11},{10,... | collective-permute-start | bytes 73736 | tf_op jit(solution)/shard_map/ppermute | solution.py:483
  78.5 3.7 %collective-permute-start.2 = (f32[6,1024]{1,0:T(8,128)S(1)}, f32[6,1024]{1,0:T(8,128)S(1)}, u32[]{:S(2)}, u32[]{:S(2)}) collective-permute-start(f32[6,1024]{1,0:T(8,128)S(1)} %get-tuple-element.12), channel_id=1, source_target_pairs={{0,3},{1,2},{2,1},{3,0},{4,7},{5,6},{6,5},{7,4},{8,11},{9,10},{10,... | collective-permute-start | bytes 73736 | tf_op jit(solution)/shard_map/ppermute | solution.py:483
  82.2 8.1 %collective-permute-start.3 = (f32[6,1024]{1,0:T(8,128)S(1)}, f32[6,1024]{1,0:T(8,128)S(1)}, u32[]{:S(2)}, u32[]{:S(2)}) collective-permute-start(f32[6,1024]{1,0:T(8,128)S(1)} %add_add_fusion.3.refs_0_), channel_id=1, source_target_pairs={{0,4},{1,5},{2,6},{3,7},{4,0},{5,1},{6,2},{7,3},{8,12},{9,13},{10,... | collective-permute-start | bytes 73736 | tf_op jit(solution)/shard_map/ppermute | solution.py:483
  87.9 5.0 %collective-permute-start.4 = (f32[6,1024]{1,0:T(8,128)S(1)}, f32[6,1024]{1,0:T(8,128)S(1)}, u32[]{:S(2)}, u32[]{:S(2)}) collective-permute-start(f32[6,1024]{1,0:T(8,128)S(1)} %add_add_fusion.3.refs_0_), channel_id=1, source_target_pairs={{0,8},{1,9},{2,10},{3,11},{4,12},{5,13},{6,14},{7,15},{8,0},{9,1},... | collective-permute-start | bytes 73736 | tf_op jit(solution)/shard_map/ppermute | solution.py:483
  89.3 5.7 %collective-permute-start.5 = (f32[6,1024]{1,0:T(8,128)S(1)}, f32[6,1024]{1,0:T(8,128)S(1)}, u32[]{:S(2)}, u32[]{:S(2)}) collective-permute-start(f32[6,1024]{1,0:T(8,128)S(1)} %add_add_fusion.3.refs_0_), channel_id=1, source_target_pairs={{0,12},{1,13},{2,14},{3,15},{4,8},{5,9},{6,10},{7,11},{8,4},{9,5},... | collective-permute-start | bytes 73736 | tf_op jit(solution)/shard_map/ppermute | solution.py:483
  115.5 1.9 %collective-permute-start.6 = (f32[6,1024]{1,0:T(8,128)S(1)}, f32[6,1024]{1,0:T(8,128)S(1)}, u32[]{:S(2)}, u32[]{:S(2)}) collective-permute-start(f32[6,1024]{1,0:T(8,128)S(1)} %get-tuple-element.14), channel_id=1, source_target_pairs={{0,1},{1,0},{2,3},{3,2},{4,5},{5,4},{6,7},{7,6},{8,9},{9,8},{10,11... | collective-permute-start | bytes 73736 | tf_op jit(solution)/shard_map/ppermute | solution.py:483
  115.5 4.2 %collective-permute-start.7 = (f32[6,1024]{1,0:T(8,128)S(1)}, f32[6,1024]{1,0:T(8,128)S(1)}, u32[]{:S(2)}, u32[]{:S(2)}) collective-permute-start(f32[6,1024]{1,0:T(8,128)S(1)} %get-tuple-element.14), channel_id=1, source_target_pairs={{0,2},{1,3},{2,0},{3,1},{4,6},{5,7},{6,4},{7,5},{8,10},{9,11},{10,... | collective-permute-start | bytes 73736 | tf_op jit(solution)/shard_map/ppermute | solution.py:483
  115.8 3.9 %collective-permute-start.8 = (f32[6,1024]{1,0:T(8,128)S(1)}, f32[6,1024]{1,0:T(8,128)S(1)}, u32[]{:S(2)}, u32[]{:S(2)}) collective-permute-start(f32[6,1024]{1,0:T(8,128)S(1)} %get-tuple-element.14), channel_id=1, source_target_pairs={{0,3},{1,2},{2,1},{3,0},{4,7},{5,6},{6,5},{7,4},{8,11},{9,10},{10,... | collective-permute-start | bytes 73736 | tf_op jit(solution)/shard_map/ppermute | solution.py:483
  119.7 5.2 %collective-permute-start.10 = (f32[6,1024]{1,0:T(8,128)S(1)}, f32[6,1024]{1,0:T(8,128)S(1)}, u32[]{:S(2)}, u32[]{:S(2)}) collective-permute-start(f32[6,1024]{1,0:T(8,128)S(1)} %add_add_fusion.2.refs_0_), channel_id=1, source_target_pairs={{0,8},{1,9},{2,10},{3,11},{4,12},{5,13},{6,14},{7,15},{8,0},{9,1},... | collective-permute-start | bytes 73736 | tf_op jit(solution)/shard_map/ppermute | solution.py:483
  119.8 5.9 %collective-permute-start.11 = (f32[6,1024]{1,0:T(8,128)S(1)}, f32[6,1024]{1,0:T(8,128)S(1)}, u32[]{:S(2)}, u32[]{:S(2)}) collective-permute-start(f32[6,1024]{1,0:T(8,128)S(1)} %add_add_fusion.2.refs_0_), channel_id=1, source_target_pairs={{0,12},{1,13},{2,14},{3,15},{4,8},{5,9},{6,10},{7,11},{8,4},{9,5},... | collective-permute-start | bytes 73736 | tf_op jit(solution)/shard_map/ppermute | solution.py:483
  121.4 4.3 %collective-permute-start.9 = (f32[6,1024]{1,0:T(8,128)S(1)}, f32[6,1024]{1,0:T(8,128)S(1)}, u32[]{:S(2)}, u32[]{:S(2)}) collective-permute-start(f32[6,1024]{1,0:T(8,128)S(1)} %add_add_fusion.2.refs_0_), channel_id=1, source_target_pairs={{0,4},{1,5},{2,6},{3,7},{4,0},{5,1},{6,2},{7,3},{8,12},{9,13},{10,... | collective-permute-start | bytes 73736 | tf_op jit(solution)/shard_map/ppermute | solution.py:483
  146.1 1.9 %collective-permute-start.12 = (f32[6,1024]{1,0:T(8,128)S(1)}, f32[6,1024]{1,0:T(8,128)S(1)}, u32[]{:S(2)}, u32[]{:S(2)}) collective-permute-start(f32[6,1024]{1,0:T(8,128)S(1)} %get-tuple-element.16), channel_id=1, source_target_pairs={{0,1},{1,0},{2,3},{3,2},{4,5},{5,4},{6,7},{7,6},{8,9},{9,8},{10,11... | collective-permute-start | bytes 73736 | tf_op jit(solution)/shard_map/ppermute | solution.py:483
  146.2 3.9 %collective-permute-start.13 = (f32[6,1024]{1,0:T(8,128)S(1)}, f32[6,1024]{1,0:T(8,128)S(1)}, u32[]{:S(2)}, u32[]{:S(2)}) collective-permute-start(f32[6,1024]{1,0:T(8,128)S(1)} %get-tuple-element.16), channel_id=1, source_target_pairs={{0,2},{1,3},{2,0},{3,1},{4,6},{5,7},{6,4},{7,5},{8,10},{9,11},{10,... | collective-permute-start | bytes 73736 | tf_op jit(solution)/shard_map/ppermute | solution.py:483
  147.2 3.3 %collective-permute-start.14 = (f32[6,1024]{1,0:T(8,128)S(1)}, f32[6,1024]{1,0:T(8,128)S(1)}, u32[]{:S(2)}, u32[]{:S(2)}) collective-permute-start(f32[6,1024]{1,0:T(8,128)S(1)} %get-tuple-element.16), channel_id=1, source_target_pairs={{0,3},{1,2},{2,1},{3,0},{4,7},{5,6},{6,5},{7,4},{8,11},{9,10},{10,... | collective-permute-start | bytes 73736 | tf_op jit(solution)/shard_map/ppermute | solution.py:483
  150.6 4.5 %collective-permute-start.15 = (f32[6,1024]{1,0:T(8,128)S(1)}, f32[6,1024]{1,0:T(8,128)S(1)}, u32[]{:S(2)}, u32[]{:S(2)}) collective-permute-start(f32[6,1024]{1,0:T(8,128)S(1)} %add_add_fusion.1), channel_id=1, source_target_pairs={{0,4},{1,5},{2,6},{3,7},{4,0},{5,1},{6,2},{7,3},{8,12},{9,13},{10,... | collective-permute-start | bytes 73736 | tf_op jit(solution)/shard_map/ppermute | solution.py:483
  152.2 5.4 %collective-permute-start.16 = (f32[6,1024]{1,0:T(8,128)S(1)}, f32[6,1024]{1,0:T(8,128)S(1)}, u32[]{:S(2)}, u32[]{:S(2)}) collective-permute-start(f32[6,1024]{1,0:T(8,128)S(1)} %add_add_fusion.1), channel_id=1, source_target_pairs={{0,8},{1,9},{2,10},{3,11},{4,12},{5,13},{6,14},{7,15},{8,0},{9,1},... | collective-permute-start | bytes 73736 | tf_op jit(solution)/shard_map/ppermute | solution.py:483
  153.2 5.7 %collective-permute-start.17 = (f32[6,1024]{1,0:T(8,128)S(1)}, f32[6,1024]{1,0:T(8,128)S(1)}, u32[]{:S(2)}, u32[]{:S(2)}) collective-permute-start(f32[6,1024]{1,0:T(8,128)S(1)} %add_add_fusion.1), channel_id=1, source_target_pairs={{0,12},{1,13},{2,14},{3,15},{4,8},{5,9},{6,10},{7,11},{8,4},{9,5},... | collective-permute-start | bytes 73736 | tf_op jit(solution)/shard_map/ppermute | solution.py:483

commit v5 on v4

--- a/solution.py
+++ b/solution.py
@@ -422,7 +422,7 @@
         scratch_shapes=[
             pltpu.VMEM((inputs, chans, width), x.dtype),
             pltpu.SemaphoreType.DMA,
-            pltpu.VMEM((inputs * chans, width), jnp.float32),
+            pltpu.VMEM(((inputs + 1) * chans, width), jnp.float32),
             pltpu.VMEM((2, inputs, width), jnp.bfloat16),
             pltpu.VMEM((2, tiles, 2 * TILE, width), jnp.bfloat16),
             pltpu.VMEM((inputs, TILE), jnp.float32),

time: 160 us -> 160 us (level)
  transfers between devices with their start and end apart: 19 -> 19, of which waited for: 12 -> 13; matrix products, arithmetic and copies ran while one was open for 0% -> 0% of each run, Pallas kernels for 0% -> 0%
where the time goes in v5:
time: 160 us
  Pallas kernels  63.2 us (40%)
  waiting for transfers between devices  60.6 us (38%)
  starting transfers between devices  31.6 us (20%)
  local copies, waits for them, and re-layouts  3.02 us (2%)
    all_to_all x1, waiting for transfers between devices, local(): lax.all_to_all(blocks, 'chan', split_axis=0, concat_axis=0, tiled=True)  41 us
    pallas_call x2, Pallas kernels, next_iteration(): pl.pallas_call(functools.partial(next_kernel, len(old_sums)), grid=(chans...  40.9 us
    ppermute x18, starting transfers between devices, all_sum(): lax.ppermute(part, 'chan', [(i, i ^ k * reach) for i in range(devices)])  24.1 us
    pallas_call x1, Pallas kernels, first_iteration(): pl.pallas_call(first_kernel, grid=(chans,), in_specs=[whole(mask.shape),...  20.8 us
    ppermute x18, waiting for transfers between devices, all_sum(): lax.ppermute(part, 'chan', [(i, i ^ k * reach) for i in range(devices)])  19.6 us
    all_to_all x1, starting transfers between devices, local(): lax.all_to_all(blocks, 'chan', split_axis=0, concat_axis=0, tiled=True)  7.52 us
  transfers between devices with their start and end apart: 19, of which 13 were waited for; matrix products, arithmetic and copies ran while one was open for 0% of the time, Pallas kernels for 0%

profile of v5, /device:TPU:0, one launch (start us, length us, event | category | flops | bytes accessed | tf_op | source)
XLA Modules:
  0.0 159.8 jit_solution(17749328810954153226)
XLA Ops:
  0.6 1.6 copy-done
  2.2 1.5 split_channels.1
  3.7 7.5 %all-to-all-start = ((bf16[16,64,8,128]{3,2,1,0:T(8,128)(2,1)}), bf16[16,64,8,128]{3,2,1,0:T(8,128)(2,1)S(1)}, u32[]{:S(2)}, u32[]{:S(2)}) async-start(bf16[16,64,8,128]{3,2,1,0:T(8,128)(2,1)} %split_channels.1), calls=%async_computation | async-start | bytes 4194304 | tf_op jit(solution)/shard_map/all_to_all | solution.py:498
  11.4 41.0 %all-to-all-done = bf16[16,64,8,128]{3,2,1,0:T(8,128)(2,1)S(1)} async-done(((bf16[16,64,8,128]{3,2,1,0:T(8,128)(2,1)}), bf16[16,64,8,128]{3,2,1,0:T(8,128)(2,1)S(1)}, u32[]{:S(2)}, u32[]{:S(2)}) %all-to-all-start) | async-done | bytes 2097184 | tf_op jit(solution)/shard_map/all_to_all | solution.py:498
  52.4 1.3 copy-done.2
  53.7 20.8 %first_iteration.1 = (bf16[8,2,18,2,128,128]{5,4,3,2,1,0:T(8,128)(2,1)S(1)}, f32[8,2,18,128,128]{4,3,2,1,0:T(8,128)S(1)}, f32[6,1024]{1,0:T(8,128)S(1)}) custom-call(f32[1,1024]{1,0:T(1,128)S(1)} %bitcast.7, f32[8,1]{1,0:T(8,128)S(1)} %copy.6.weight_ref, f32[8,1]{1,0:T(8,128)S(1)} %add_multiply_fusion.freq_ref, bf16[1024,8,128]{2,1,0:T(8,128)(2,1)} %bitcast.10), custom_call_target="tpu_custom_call" | custom-call | tf_op jit(solution)/shard_map/first_iteration/pallas_call | solution.py:411
  74.5 0.8 collective-permute-start
  75.3 3.4 %collective-permute-start.1 = (f32[6,1024]{1,0:T(8,128)S(1)}, f32[6,1024]{1,0:T(8,128)S(1)}, u32[]{:S(2)}, u32[]{:S(2)}) collective-permute-start(f32[6,1024]{1,0:T(8,128)S(1)} %get-tuple-element.12), channel_id=1, source_target_pairs={{0,2},{1,3},{2,0},{3,1},{4,6},{5,7},{6,4},{7,5},{8,10},{9,11},{10,... | collective-permute-start | bytes 73736 | tf_op jit(solution)/shard_map/ppermute | solution.py:483
  78.7 1.9 %collective-permute-done.1 = f32[6,1024]{1,0:T(8,128)S(1)} collective-permute-done((f32[6,1024]{1,0:T(8,128)S(1)}, f32[6,1024]{1,0:T(8,128)S(1)}, u32[]{:S(2)}, u32[]{:S(2)}) %collective-permute-start.1) | collective-permute-done | bytes 24608 | tf_op jit(solution)/shard_map/ppermute | solution.py:483
  80.6 1.8 %collective-permute-done.2 = f32[6,1024]{1,0:T(8,128)S(1)} collective-permute-done((f32[6,1024]{1,0:T(8,128)S(1)}, f32[6,1024]{1,0:T(8,128)S(1)}, u32[]{:S(2)}, u32[]{:S(2)}) %collective-permute-start.2) | collective-permute-done | bytes 24608 | tf_op jit(solution)/shard_map/ppermute | solution.py:483
  82.4 5.7 %collective-permute-start.3 = (f32[6,1024]{1,0:T(8,128)S(1)}, f32[6,1024]{1,0:T(8,128)S(1)}, u32[]{:S(2)}, u32[]{:S(2)}) collective-permute-start(f32[6,1024]{1,0:T(8,128)S(1)} %add_add_fusion.3.refs_0_), channel_id=1, source_target_pairs={{0,4},{1,5},{2,6},{3,7},{4,0},{5,1},{6,2},{7,3},{8,12},{9,13},{10,... | collective-permute-start | bytes 73736 | tf_op jit(solution)/shard_map/ppermute | solution.py:483
  88.1 1.4 collective-permute-start.4
  89.5 1.0 collective-permute-start.5
  90.5 2.5 %collective-permute-done.4.refs_2_ = f32[6,1024]{1,0:T(8,128)S(1)} collective-permute-done((f32[6,1024]{1,0:T(8,128)S(1)}, f32[6,1024]{1,0:T(8,128)S(1)}, u32[]{:S(2)}, u32[]{:S(2)}) %collective-permute-start.4) | collective-permute-done | bytes 24608 | tf_op jit(solution)/shard_map/ppermute | solution.py:483
  93.1 2.1 %collective-permute-done.5.refs_3_ = f32[6,1024]{1,0:T(8,128)S(1)} collective-permute-done((f32[6,1024]{1,0:T(8,128)S(1)}, f32[6,1024]{1,0:T(8,128)S(1)}, u32[]{:S(2)}, u32[]{:S(2)}) %collective-permute-start.5) | collective-permute-done | bytes 24608 | tf_op jit(solution)/shard_map/ppermute | solution.py:483
  95.2 20.4 %next_iteration.2 = (f32[6,1024]{1,0:T(8,128)S(1)}, f32[3,1024]{1,0:T(4,128)S(1)}, f32[2,8,1024]{2,1,0:T(8,128)}) custom-call(f32[3,1024]{1,0:T(4,128)S(1)} %copy-done.1, f32[1,1024]{1,0:T(1,128)S(1)} %bitcast.8, f32[8,1]{1,0:T(8,128)S(1)} %copy.6.weight_ref, f32[8,1]{1,0:T(8,128)S(1)} %add_multiply_fusion.freq_ref, ...), custom_call_target="tpu_custom_call" | custom-call | tf_op jit(solution)/shard_map/next_iteration/pallas_call | solution.py:444
  116.0 1.5 collective-permute-start.8
  117.5 2.3 %collective-permute-done.7 = f32[6,1024]{1,0:T(8,128)S(1)} collective-permute-done((f32[6,1024]{1,0:T(8,128)S(1)}, f32[6,1024]{1,0:T(8,128)S(1)}, u32[]{:S(2)}, u32[]{:S(2)}) %collective-permute-start.7) | collective-permute-done | bytes 24608 | tf_op jit(solution)/shard_map/ppermute | solution.py:483
  119.9 1.7 %collective-permute-start.11 = (f32[6,1024]{1,0:T(8,128)S(1)}, f32[6,1024]{1,0:T(8,128)S(1)}, u32[]{:S(2)}, u32[]{:S(2)}) collective-permute-start(f32[6,1024]{1,0:T(8,128)S(1)} %add_add_fusion.2.refs_0_), channel_id=1, source_target_pairs={{0,12},{1,13},{2,14},{3,15},{4,8},{5,9},{6,10},{7,11},{8,4},{9,5},... | collective-permute-start | bytes 73736 | tf_op jit(solution)/shard_map/ppermute | solution.py:483
  121.7 1.7 %collective-permute-start.9 = (f32[6,1024]{1,0:T(8,128)S(1)}, f32[6,1024]{1,0:T(8,128)S(1)}, u32[]{:S(2)}, u32[]{:S(2)}) collective-permute-start(f32[6,1024]{1,0:T(8,128)S(1)} %add_add_fusion.2.refs_0_), channel_id=1, source_target_pairs={{0,4},{1,5},{2,6},{3,7},{4,0},{5,1},{6,2},{7,3},{8,12},{9,13},{10,... | collective-permute-start | bytes 73736 | tf_op jit(solution)/shard_map/ppermute | solution.py:483
  123.4 1.7 %collective-permute-done.10.refs_2_ = f32[6,1024]{1,0:T(8,128)S(1)} collective-permute-done((f32[6,1024]{1,0:T(8,128)S(1)}, f32[6,1024]{1,0:T(8,128)S(1)}, u32[]{:S(2)}, u32[]{:S(2)}) %collective-permute-start.10) | collective-permute-done | bytes 24608 | tf_op jit(solution)/shard_map/ppermute | solution.py:483
  125.1 0.7 collective-permute-done.11.refs_3_
  125.9 20.4 %next_iteration.3 = (f32[6,1024]{1,0:T(8,128)S(1)}, f32[3,1024]{1,0:T(4,128)S(1)}, f32[2,8,1024]{2,1,0:T(8,128)}) custom-call(f32[3,1024]{1,0:T(4,128)S(1)} %get-tuple-element.13.gains_ref, f32[1,1024]{1,0:T(1,128)S(1)} %bitcast.9, f32[8,1]{1,0:T(8,128)S(1)} %copy.6.weight_ref, f32[8,1]{1,0:T(8,128)S(1)} %add_multiply_fusion.freq_ref, ...), custom_call_target="tpu_custom_call" | custom-call | tf_op jit(solution)/shard_map/next_iteration/pallas_call | solution.py:444
  146.4 1.1 collective-permute-start.13
  147.5 0.7 collective-permute-start.14
  148.2 2.1 %collective-permute-done.13 = f32[6,1024]{1,0:T(8,128)S(1)} collective-permute-done((f32[6,1024]{1,0:T(8,128)S(1)}, f32[6,1024]{1,0:T(8,128)S(1)}, u32[]{:S(2)}, u32[]{:S(2)}) %collective-permute-start.13) | collective-permute-done | bytes 24608 | tf_op jit(solution)/shard_map/ppermute | solution.py:483
  150.9 1.5 collective-permute-start.15
  152.3 1.0 collective-permute-start.16
  153.4 1.9 %collective-permute-start.17 = (f32[6,1024]{1,0:T(8,128)S(1)}, f32[6,1024]{1,0:T(8,128)S(1)}, u32[]{:S(2)}, u32[]{:S(2)}) collective-permute-start(f32[6,1024]{1,0:T(8,128)S(1)} %add_add_fusion.1), channel_id=1, source_target_pairs={{0,12},{1,13},{2,14},{3,15},{4,8},{5,9},{6,10},{7,11},{8,4},{9,5},... | collective-permute-start | bytes 73736 | tf_op jit(solution)/shard_map/ppermute | solution.py:483
  155.3 2.6 %collective-permute-done.16 = f32[6,1024]{1,0:T(8,128)S(1)} collective-permute-done((f32[6,1024]{1,0:T(8,128)S(1)}, f32[6,1024]{1,0:T(8,128)S(1)}, u32[]{:S(2)}, u32[]{:S(2)}) %collective-permute-start.16) | collective-permute-done | bytes 24608 | tf_op jit(solution)/shard_map/ppermute | solution.py:483
  157.9 1.2 collective-permute-done.17
  159.2 0.7 multiply_add_fusion
  (31 shorter events, 1.5 us)
Async XLA Ops:
  0.6 1.6 copy-start
  3.7 7.5 %copy-start.4 = (s32[8]{0:T(128)S(1)}, s32[8]{0:T(128)}, u32[]{:S(2)}) copy-start(s32[8]{0:T(128)} %param.5) | copy-start | bytes 100
  3.7 7.6 %copy-start.3 = (s32[1024]{0:T(1024)S(1)}, s32[1024]{0:T(1024)}, u32[]{:S(2)}) copy-start(s32[1024]{0:T(1024)} %param.4) | copy-start | bytes 12292
  3.7 48.6 %all-to-all-start = ((bf16[16,64,8,128]{3,2,1,0:T(8,128)(2,1)}), bf16[16,64,8,128]{3,2,1,0:T(8,128)(2,1)S(1)}, u32[]{:S(2)}, u32[]{:S(2)}) async-start(bf16[16,64,8,128]{3,2,1,0:T(8,128)(2,1)} %split_channels.1), calls=%async_computation | async-start | bytes 4194304 | tf_op jit(solution)/shard_map/all_to_all | solution.py:498
  11.2 84.0 %copy-start.1 = (f32[3,1024]{1,0:T(4,128)S(1)}, f32[3,1024]{1,0:T(4,128)}, u32[]{:S(2)}) copy-start(f32[3,1024]{1,0:T(4,128)} %constant.8.clone.1.gains_ref) | copy-start | bytes 36868
  52.3 1.3 copy-start.2
  74.5 4.2 %collective-permute-start = (f32[6,1024]{1,0:T(8,128)S(1)}, f32[6,1024]{1,0:T(8,128)S(1)}, u32[]{:S(2)}, u32[]{:S(2)}) collective-permute-start(f32[6,1024]{1,0:T(8,128)S(1)} %get-tuple-element.12), channel_id=1, source_target_pairs={{0,1},{1,0},{2,3},{3,2},{4,5},{5,4},{6,7},{7,6},{8,9},{9,8},{10,11... | collective-permute-start | bytes 73736 | tf_op jit(solution)/shard_map/ppermute | solution.py:483
  75.3 5.3 %collective-permute-start.1 = (f32[6,1024]{1,0:T(8,128)S(1)}, f32[6,1024]{1,0:T(8,128)S(1)}, u32[]{:S(2)}, u32[]{:S(2)}) collective-permute-start(f32[6,1024]{1,0:T(8,128)S(1)} %get-tuple-element.12), channel_id=1, source_target_pairs={{0,2},{1,3},{2,0},{3,1},{4,6},{5,7},{6,4},{7,5},{8,10},{9,11},{10,... | collective-permute-start | bytes 73736 | tf_op jit(solution)/shard_map/ppermute | solution.py:483
  78.7 3.7 %collective-permute-start.2 = (f32[6,1024]{1,0:T(8,128)S(1)}, f32[6,1024]{1,0:T(8,128)S(1)}, u32[]{:S(2)}, u32[]{:S(2)}) collective-permute-start(f32[6,1024]{1,0:T(8,128)S(1)} %get-tuple-element.12), channel_id=1, source_target_pairs={{0,3},{1,2},{2,1},{3,0},{4,7},{5,6},{6,5},{7,4},{8,11},{9,10},{10,... | collective-permute-start | bytes 73736 | tf_op jit(solution)/shard_map/ppermute | solution.py:483
  82.4 8.1 %collective-permute-start.3 = (f32[6,1024]{1,0:T(8,128)S(1)}, f32[6,1024]{1,0:T(8,128)S(1)}, u32[]{:S(2)}, u32[]{:S(2)}) collective-permute-start(f32[6,1024]{1,0:T(8,128)S(1)} %add_add_fusion.3.refs_0_), channel_id=1, source_target_pairs={{0,4},{1,5},{2,6},{3,7},{4,0},{5,1},{6,2},{7,3},{8,12},{9,13},{10,... | collective-permute-start | bytes 73736 | tf_op jit(solution)/shard_map/ppermute | solution.py:483
  88.1 5.0 %collective-permute-start.4 = (f32[6,1024]{1,0:T(8,128)S(1)}, f32[6,1024]{1,0:T(8,128)S(1)}, u32[]{:S(2)}, u32[]{:S(2)}) collective-permute-start(f32[6,1024]{1,0:T(8,128)S(1)} %add_add_fusion.3.refs_0_), channel_id=1, source_target_pairs={{0,8},{1,9},{2,10},{3,11},{4,12},{5,13},{6,14},{7,15},{8,0},{9,1},... | collective-permute-start | bytes 73736 | tf_op jit(solution)/shard_map/ppermute | solution.py:483
  89.5 5.7 %collective-permute-start.5 = (f32[6,1024]{1,0:T(8,128)S(1)}, f32[6,1024]{1,0:T(8,128)S(1)}, u32[]{:S(2)}, u32[]{:S(2)}) collective-permute-start(f32[6,1024]{1,0:T(8,128)S(1)} %add_add_fusion.3.refs_0_), channel_id=1, source_target_pairs={{0,12},{1,13},{2,14},{3,15},{4,8},{5,9},{6,10},{7,11},{8,4},{9,5},... | collective-permute-start | bytes 73736 | tf_op jit(solution)/shard_map/ppermute | solution.py:483
  115.6 1.9 %collective-permute-start.6 = (f32[6,1024]{1,0:T(8,128)S(1)}, f32[6,1024]{1,0:T(8,128)S(1)}, u32[]{:S(2)}, u32[]{:S(2)}) collective-permute-start(f32[6,1024]{1,0:T(8,128)S(1)} %get-tuple-element.14), channel_id=1, source_target_pairs={{0,1},{1,0},{2,3},{3,2},{4,5},{5,4},{6,7},{7,6},{8,9},{9,8},{10,11... | collective-permute-start | bytes 73736 | tf_op jit(solution)/shard_map/ppermute | solution.py:483
  115.7 4.2 %collective-permute-start.7 = (f32[6,1024]{1,0:T(8,128)S(1)}, f32[6,1024]{1,0:T(8,128)S(1)}, u32[]{:S(2)}, u32[]{:S(2)}) collective-permute-start(f32[6,1024]{1,0:T(8,128)S(1)} %get-tuple-element.14), channel_id=1, source_target_pairs={{0,2},{1,3},{2,0},{3,1},{4,6},{5,7},{6,4},{7,5},{8,10},{9,11},{10,... | collective-permute-start | bytes 73736 | tf_op jit(solution)/shard_map/ppermute | solution.py:483
  116.0 3.8 %collective-permute-start.8 = (f32[6,1024]{1,0:T(8,128)S(1)}, f32[6,1024]{1,0:T(8,128)S(1)}, u32[]{:S(2)}, u32[]{:S(2)}) collective-permute-start(f32[6,1024]{1,0:T(8,128)S(1)} %get-tuple-element.14), channel_id=1, source_target_pairs={{0,3},{1,2},{2,1},{3,0},{4,7},{5,6},{6,5},{7,4},{8,11},{9,10},{10,... | collective-permute-start | bytes 73736 | tf_op jit(solution)/shard_map/ppermute | solution.py:483
  119.8 5.2 %collective-permute-start.10 = (f32[6,1024]{1,0:T(8,128)S(1)}, f32[6,1024]{1,0:T(8,128)S(1)}, u32[]{:S(2)}, u32[]{:S(2)}) collective-permute-start(f32[6,1024]{1,0:T(8,128)S(1)} %add_add_fusion.2.refs_0_), channel_id=1, source_target_pairs={{0,8},{1,9},{2,10},{3,11},{4,12},{5,13},{6,14},{7,15},{8,0},{9,1},... | collective-permute-start | bytes 73736 | tf_op jit(solution)/shard_map/ppermute | solution.py:483
  119.9 5.8 %collective-permute-start.11 = (f32[6,1024]{1,0:T(8,128)S(1)}, f32[6,1024]{1,0:T(8,128)S(1)}, u32[]{:S(2)}, u32[]{:S(2)}) collective-permute-start(f32[6,1024]{1,0:T(8,128)S(1)} %add_add_fusion.2.refs_0_), channel_id=1, source_target_pairs={{0,12},{1,13},{2,14},{3,15},{4,8},{5,9},{6,10},{7,11},{8,4},{9,5},... | collective-permute-start | bytes 73736 | tf_op jit(solution)/shard_map/ppermute | solution.py:483
  121.7 4.3 %collective-permute-start.9 = (f32[6,1024]{1,0:T(8,128)S(1)}, f32[6,1024]{1,0:T(8,128)S(1)}, u32[]{:S(2)}, u32[]{:S(2)}) collective-permute-start(f32[6,1024]{1,0:T(8,128)S(1)} %add_add_fusion.2.refs_0_), channel_id=1, source_target_pairs={{0,4},{1,5},{2,6},{3,7},{4,0},{5,1},{6,2},{7,3},{8,12},{9,13},{10,... | collective-permute-start | bytes 73736 | tf_op jit(solution)/shard_map/ppermute | solution.py:483
  146.4 1.9 %collective-permute-start.12 = (f32[6,1024]{1,0:T(8,128)S(1)}, f32[6,1024]{1,0:T(8,128)S(1)}, u32[]{:S(2)}, u32[]{:S(2)}) collective-permute-start(f32[6,1024]{1,0:T(8,128)S(1)} %get-tuple-element.16), channel_id=1, source_target_pairs={{0,1},{1,0},{2,3},{3,2},{4,5},{5,4},{6,7},{7,6},{8,9},{9,8},{10,11... | collective-permute-start | bytes 73736 | tf_op jit(solution)/shard_map/ppermute | solution.py:483
  146.4 3.9 %collective-permute-start.13 = (f32[6,1024]{1,0:T(8,128)S(1)}, f32[6,1024]{1,0:T(8,128)S(1)}, u32[]{:S(2)}, u32[]{:S(2)}) collective-permute-start(f32[6,1024]{1,0:T(8,128)S(1)} %get-tuple-element.16), channel_id=1, source_target_pairs={{0,2},{1,3},{2,0},{3,1},{4,6},{5,7},{6,4},{7,5},{8,10},{9,11},{10,... | collective-permute-start | bytes 73736 | tf_op jit(solution)/shard_map/ppermute | solution.py:483
  147.5 3.3 %collective-permute-start.14 = (f32[6,1024]{1,0:T(8,128)S(1)}, f32[6,1024]{1,0:T(8,128)S(1)}, u32[]{:S(2)}, u32[]{:S(2)}) collective-permute-start(f32[6,1024]{1,0:T(8,128)S(1)} %get-tuple-element.16), channel_id=1, source_target_pairs={{0,3},{1,2},{2,1},{3,0},{4,7},{5,6},{6,5},{7,4},{8,11},{9,10},{10,... | collective-permute-start | bytes 73736 | tf_op jit(solution)/shard_map/ppermute | solution.py:483
  150.9 4.5 %collective-permute-start.15 = (f32[6,1024]{1,0:T(8,128)S(1)}, f32[6,1024]{1,0:T(8,128)S(1)}, u32[]{:S(2)}, u32[]{:S(2)}) collective-permute-start(f32[6,1024]{1,0:T(8,128)S(1)} %add_add_fusion.1), channel_id=1, source_target_pairs={{0,4},{1,5},{2,6},{3,7},{4,0},{5,1},{6,2},{7,3},{8,12},{9,13},{10,... | collective-permute-start | bytes 73736 | tf_op jit(solution)/shard_map/ppermute | solution.py:483
  152.3 5.5 %collective-permute-start.16 = (f32[6,1024]{1,0:T(8,128)S(1)}, f32[6,1024]{1,0:T(8,128)S(1)}, u32[]{:S(2)}, u32[]{:S(2)}) collective-permute-start(f32[6,1024]{1,0:T(8,128)S(1)} %add_add_fusion.1), channel_id=1, source_target_pairs={{0,8},{1,9},{2,10},{3,11},{4,12},{5,13},{6,14},{7,15},{8,0},{9,1},... | collective-permute-start | bytes 73736 | tf_op jit(solution)/shard_map/ppermute | solution.py:483
  153.4 5.7 %collective-permute-start.17 = (f32[6,1024]{1,0:T(8,128)S(1)}, f32[6,1024]{1,0:T(8,128)S(1)}, u32[]{:S(2)}, u32[]{:S(2)}) collective-permute-start(f32[6,1024]{1,0:T(8,128)S(1)} %add_add_fusion.1), channel_id=1, source_target_pairs={{0,12},{1,13},{2,14},{3,15},{4,8},{5,9},{6,10},{7,11},{8,4},{9,5},... | collective-permute-start | bytes 73736 | tf_op jit(solution)/shard_map/ppermute | solution.py:483

commit v6 on v5

--- a/solution.py
+++ b/solution.py
@@ -401,7 +401,7 @@
         out_shape=jax.ShapeDtypeStruct((devices, inputs_dev, chans, width), voltages.dtype),
         compiler_params=pltpu.CompilerParams(vmem_limit_bytes=VMEM_LIMIT),
         name="split_channels",
-    )(voltages)
+    )(pltpu.with_memory_space_constraint(voltages, pltpu.HBM))
 
 
 def first_iteration(x, mask, weight, freq):

time: 160 us -> 160 us (level)
  no operation moved by 1% of the time
where the time goes in v6:
time: 160 us
  Pallas kernels  64.5 us (40%)
  waiting for transfers between devices  60.5 us (38%)
  starting transfers between devices  31.6 us (20%)
    all_to_all x1, waiting for transfers between devices, local(): lax.all_to_all(blocks, 'chan', split_axis=0, concat_axis=0, tiled=True)  41 us
    pallas_call x2, Pallas kernels, next_iteration(): pl.pallas_call(functools.partial(next_kernel, len(old_sums)), grid=(chans...  40.9 us
    ppermute x18, starting transfers between devices, all_sum(): lax.ppermute(part, 'chan', [(i, i ^ k * reach) for i in range(devices)])  24.1 us
    pallas_call x1, Pallas kernels, first_iteration(): pl.pallas_call(first_kernel, grid=(chans,), in_specs=[whole(mask.shape),...  20.8 us
    ppermute x18, waiting for transfers between devices, all_sum(): lax.ppermute(part, 'chan', [(i, i ^ k * reach) for i in range(devices)])  19.5 us
    all_to_all x1, starting transfers between devices, local(): lax.all_to_all(blocks, 'chan', split_axis=0, concat_axis=0, tiled=True)  7.52 us
  transfers between devices with their start and end apart: 19, of which 13 were waited for; matrix products, arithmetic and copies ran while one was open for 0% of the time, Pallas kernels for 0%

profile of v6, /device:TPU:0, one launch (start us, length us, event | category | flops | bytes accessed | tf_op | source)
XLA Modules:
  0.0 159.5 jit_solution(14231314886125844717)
XLA Ops:
  0.6 2.8 %split_channels.1 = bf16[16,64,8,128]{3,2,1,0:T(8,128)(2,1)} custom-call(bf16[64,128,128]{2,1,0:T(8,128)(2,1)} %volt_ref.1), custom_call_target="tpu_custom_call" | custom-call | tf_op jit(solution)/shard_map/split_channels/pallas_call | solution.py:396
  3.4 7.5 %all-to-all-start = ((bf16[16,64,8,128]{3,2,1,0:T(8,128)(2,1)}), bf16[16,64,8,128]{3,2,1,0:T(8,128)(2,1)S(1)}, u32[]{:S(2)}, u32[]{:S(2)}) async-start(bf16[16,64,8,128]{3,2,1,0:T(8,128)(2,1)} %split_channels.1), calls=%async_computation | async-start | bytes 4194304 | tf_op jit(solution)/shard_map/all_to_all | solution.py:498
  11.1 41.0 %all-to-all-done = bf16[16,64,8,128]{3,2,1,0:T(8,128)(2,1)S(1)} async-done(((bf16[16,64,8,128]{3,2,1,0:T(8,128)(2,1)}), bf16[16,64,8,128]{3,2,1,0:T(8,128)(2,1)S(1)}, u32[]{:S(2)}, u32[]{:S(2)}) %all-to-all-start) | async-done | bytes 2097184 | tf_op jit(solution)/shard_map/all_to_all | solution.py:498
  52.0 1.3 copy-done.1
  53.4 20.8 %first_iteration.1 = (bf16[8,2,18,2,128,128]{5,4,3,2,1,0:T(8,128)(2,1)S(1)}, f32[8,2,18,128,128]{4,3,2,1,0:T(8,128)S(1)}, f32[6,1024]{1,0:T(8,128)S(1)}) custom-call(f32[1,1024]{1,0:T(1,128)S(1)} %bitcast.7, f32[8,1]{1,0:T(8,128)S(1)} %copy.6.weight_ref, f32[8,1]{1,0:T(8,128)S(1)} %add_multiply_fusion.freq_ref, bf16[1024,8,128]{2,1,0:T(8,128)(2,1)} %bitcast.10), custom_call_target="tpu_custom_call" | custom-call | tf_op jit(solution)/shard_map/first_iteration/pallas_call | solution.py:411
  74.2 0.8 collective-permute-start
  75.0 3.4 %collective-permute-start.1 = (f32[6,1024]{1,0:T(8,128)S(1)}, f32[6,1024]{1,0:T(8,128)S(1)}, u32[]{:S(2)}, u32[]{:S(2)}) collective-permute-start(f32[6,1024]{1,0:T(8,128)S(1)} %get-tuple-element.12), channel_id=1, source_target_pairs={{0,2},{1,3},{2,0},{3,1},{4,6},{5,7},{6,4},{7,5},{8,10},{9,11},{10,... | collective-permute-start | bytes 73736 | tf_op jit(solution)/shard_map/ppermute | solution.py:483
  78.4 1.9 %collective-permute-done.1 = f32[6,1024]{1,0:T(8,128)S(1)} collective-permute-done((f32[6,1024]{1,0:T(8,128)S(1)}, f32[6,1024]{1,0:T(8,128)S(1)}, u32[]{:S(2)}, u32[]{:S(2)}) %collective-permute-start.1) | collective-permute-done | bytes 24608 | tf_op jit(solution)/shard_map/ppermute | solution.py:483
  80.3 1.8 %collective-permute-done.2 = f32[6,1024]{1,0:T(8,128)S(1)} collective-permute-done((f32[6,1024]{1,0:T(8,128)S(1)}, f32[6,1024]{1,0:T(8,128)S(1)}, u32[]{:S(2)}, u32[]{:S(2)}) %collective-permute-start.2) | collective-permute-done | bytes 24608 | tf_op jit(solution)/shard_map/ppermute | solution.py:483
  82.1 5.7 %collective-permute-start.3 = (f32[6,1024]{1,0:T(8,128)S(1)}, f32[6,1024]{1,0:T(8,128)S(1)}, u32[]{:S(2)}, u32[]{:S(2)}) collective-permute-start(f32[6,1024]{1,0:T(8,128)S(1)} %add_add_fusion.3.refs_0_), channel_id=1, source_target_pairs={{0,4},{1,5},{2,6},{3,7},{4,0},{5,1},{6,2},{7,3},{8,12},{9,13},{10,... | collective-permute-start | bytes 73736 | tf_op jit(solution)/shard_map/ppermute | solution.py:483
  87.8 1.4 collective-permute-start.4
  89.2 1.1 collective-permute-start.5
  90.2 2.5 %collective-permute-done.4.refs_2_ = f32[6,1024]{1,0:T(8,128)S(1)} collective-permute-done((f32[6,1024]{1,0:T(8,128)S(1)}, f32[6,1024]{1,0:T(8,128)S(1)}, u32[]{:S(2)}, u32[]{:S(2)}) %collective-permute-start.4) | collective-permute-done | bytes 24608 | tf_op jit(solution)/shard_map/ppermute | solution.py:483
  92.8 2.1 %collective-permute-done.5.refs_3_ = f32[6,1024]{1,0:T(8,128)S(1)} collective-permute-done((f32[6,1024]{1,0:T(8,128)S(1)}, f32[6,1024]{1,0:T(8,128)S(1)}, u32[]{:S(2)}, u32[]{:S(2)}) %collective-permute-start.5) | collective-permute-done | bytes 24608 | tf_op jit(solution)/shard_map/ppermute | solution.py:483
  94.9 20.5 %next_iteration.2 = (f32[6,1024]{1,0:T(8,128)S(1)}, f32[3,1024]{1,0:T(4,128)S(1)}, f32[2,8,1024]{2,1,0:T(8,128)}) custom-call(f32[3,1024]{1,0:T(4,128)S(1)} %copy-done, f32[1,1024]{1,0:T(1,128)S(1)} %bitcast.8, f32[8,1]{1,0:T(8,128)S(1)} %copy.6.weight_ref, f32[8,1]{1,0:T(8,128)S(1)} %add_multiply_fusion.freq_ref, ...), custom_call_target="tpu_custom_call" | custom-call | tf_op jit(solution)/shard_map/next_iteration/pallas_call | solution.py:444
  115.7 1.5 collective-permute-start.8
  117.2 2.3 %collective-permute-done.7 = f32[6,1024]{1,0:T(8,128)S(1)} collective-permute-done((f32[6,1024]{1,0:T(8,128)S(1)}, f32[6,1024]{1,0:T(8,128)S(1)}, u32[]{:S(2)}, u32[]{:S(2)}) %collective-permute-start.7) | collective-permute-done | bytes 24608 | tf_op jit(solution)/shard_map/ppermute | solution.py:483
  119.6 1.7 %collective-permute-start.11 = (f32[6,1024]{1,0:T(8,128)S(1)}, f32[6,1024]{1,0:T(8,128)S(1)}, u32[]{:S(2)}, u32[]{:S(2)}) collective-permute-start(f32[6,1024]{1,0:T(8,128)S(1)} %add_add_fusion.2.refs_0_), channel_id=1, source_target_pairs={{0,12},{1,13},{2,14},{3,15},{4,8},{5,9},{6,10},{7,11},{8,4},{9,5},... | collective-permute-start | bytes 73736 | tf_op jit(solution)/shard_map/ppermute | solution.py:483
  121.4 1.7 %collective-permute-start.9 = (f32[6,1024]{1,0:T(8,128)S(1)}, f32[6,1024]{1,0:T(8,128)S(1)}, u32[]{:S(2)}, u32[]{:S(2)}) collective-permute-start(f32[6,1024]{1,0:T(8,128)S(1)} %add_add_fusion.2.refs_0_), channel_id=1, source_target_pairs={{0,4},{1,5},{2,6},{3,7},{4,0},{5,1},{6,2},{7,3},{8,12},{9,13},{10,... | collective-permute-start | bytes 73736 | tf_op jit(solution)/shard_map/ppermute | solution.py:483
  123.1 1.7 %collective-permute-done.10.refs_2_ = f32[6,1024]{1,0:T(8,128)S(1)} collective-permute-done((f32[6,1024]{1,0:T(8,128)S(1)}, f32[6,1024]{1,0:T(8,128)S(1)}, u32[]{:S(2)}, u32[]{:S(2)}) %collective-permute-start.10) | collective-permute-done | bytes 24608 | tf_op jit(solution)/shard_map/ppermute | solution.py:483
  124.8 0.7 collective-permute-done.11.refs_3_
  125.6 20.4 %next_iteration.3 = (f32[6,1024]{1,0:T(8,128)S(1)}, f32[3,1024]{1,0:T(4,128)S(1)}, f32[2,8,1024]{2,1,0:T(8,128)}) custom-call(f32[3,1024]{1,0:T(4,128)S(1)} %get-tuple-element.13.gains_ref, f32[1,1024]{1,0:T(1,128)S(1)} %bitcast.9, f32[8,1]{1,0:T(8,128)S(1)} %copy.6.weight_ref, f32[8,1]{1,0:T(8,128)S(1)} %add_multiply_fusion.freq_ref, ...), custom_call_target="tpu_custom_call" | custom-call | tf_op jit(solution)/shard_map/next_iteration/pallas_call | solution.py:444
  146.1 1.1 collective-permute-start.13
  147.2 0.7 collective-permute-start.14
  147.9 2.1 %collective-permute-done.13 = f32[6,1024]{1,0:T(8,128)S(1)} collective-permute-done((f32[6,1024]{1,0:T(8,128)S(1)}, f32[6,1024]{1,0:T(8,128)S(1)}, u32[]{:S(2)}, u32[]{:S(2)}) %collective-permute-start.13) | collective-permute-done | bytes 24608 | tf_op jit(solution)/shard_map/ppermute | solution.py:483
  150.0 0.6 collective-permute-done.14
  150.6 1.5 collective-permute-start.15
  152.1 1.0 collective-permute-start.16
  153.1 1.9 %collective-permute-start.17 = (f32[6,1024]{1,0:T(8,128)S(1)}, f32[6,1024]{1,0:T(8,128)S(1)}, u32[]{:S(2)}, u32[]{:S(2)}) collective-permute-start(f32[6,1024]{1,0:T(8,128)S(1)} %add_add_fusion.1), channel_id=1, source_target_pairs={{0,12},{1,13},{2,14},{3,15},{4,8},{5,9},{6,10},{7,11},{8,4},{9,5},... | collective-permute-start | bytes 73736 | tf_op jit(solution)/shard_map/ppermute | solution.py:483
  155.0 2.6 %collective-permute-done.16 = f32[6,1024]{1,0:T(8,128)S(1)} collective-permute-done((f32[6,1024]{1,0:T(8,128)S(1)}, f32[6,1024]{1,0:T(8,128)S(1)}, u32[]{:S(2)}, u32[]{:S(2)}) %collective-permute-start.16) | collective-permute-done | bytes 24608 | tf_op jit(solution)/shard_map/ppermute | solution.py:483
  157.6 1.2 collective-permute-done.17
  158.9 0.7 multiply_add_fusion
  (29 shorter events, 0.8 us)
Async XLA Ops:
  3.4 7.5 %copy-start.3 = (s32[8]{0:T(128)S(1)}, s32[8]{0:T(128)}, u32[]{:S(2)}) copy-start(s32[8]{0:T(128)} %param.5) | copy-start | bytes 100
  3.4 7.6 %copy-start.2 = (s32[1024]{0:T(1024)S(1)}, s32[1024]{0:T(1024)}, u32[]{:S(2)}) copy-start(s32[1024]{0:T(1024)} %param.4) | copy-start | bytes 12292
  3.4 48.6 %all-to-all-start = ((bf16[16,64,8,128]{3,2,1,0:T(8,128)(2,1)}), bf16[16,64,8,128]{3,2,1,0:T(8,128)(2,1)S(1)}, u32[]{:S(2)}, u32[]{:S(2)}) async-start(bf16[16,64,8,128]{3,2,1,0:T(8,128)(2,1)} %split_channels.1), calls=%async_computation | async-start | bytes 4194304 | tf_op jit(solution)/shard_map/all_to_all | solution.py:498
  10.9 84.0 %copy-start = (f32[3,1024]{1,0:T(4,128)S(1)}, f32[3,1024]{1,0:T(4,128)}, u32[]{:S(2)}) copy-start(f32[3,1024]{1,0:T(4,128)} %constant.8.clone.1.gains_ref) | copy-start | bytes 36868
  52.0 1.3 copy-start.1
  74.2 4.2 %collective-permute-start = (f32[6,1024]{1,0:T(8,128)S(1)}, f32[6,1024]{1,0:T(8,128)S(1)}, u32[]{:S(2)}, u32[]{:S(2)}) collective-permute-start(f32[6,1024]{1,0:T(8,128)S(1)} %get-tuple-element.12), channel_id=1, source_target_pairs={{0,1},{1,0},{2,3},{3,2},{4,5},{5,4},{6,7},{7,6},{8,9},{9,8},{10,11... | collective-permute-start | bytes 73736 | tf_op jit(solution)/shard_map/ppermute | solution.py:483
  75.0 5.3 %collective-permute-start.1 = (f32[6,1024]{1,0:T(8,128)S(1)}, f32[6,1024]{1,0:T(8,128)S(1)}, u32[]{:S(2)}, u32[]{:S(2)}) collective-permute-start(f32[6,1024]{1,0:T(8,128)S(1)} %get-tuple-element.12), channel_id=1, source_target_pairs={{0,2},{1,3},{2,0},{3,1},{4,6},{5,7},{6,4},{7,5},{8,10},{9,11},{10,... | collective-permute-start | bytes 73736 | tf_op jit(solution)/shard_map/ppermute | solution.py:483
  78.4 3.7 %collective-permute-start.2 = (f32[6,1024]{1,0:T(8,128)S(1)}, f32[6,1024]{1,0:T(8,128)S(1)}, u32[]{:S(2)}, u32[]{:S(2)}) collective-permute-start(f32[6,1024]{1,0:T(8,128)S(1)} %get-tuple-element.12), channel_id=1, source_target_pairs={{0,3},{1,2},{2,1},{3,0},{4,7},{5,6},{6,5},{7,4},{8,11},{9,10},{10,... | collective-permute-start | bytes 73736 | tf_op jit(solution)/shard_map/ppermute | solution.py:483
  82.1 8.1 %collective-permute-start.3 = (f32[6,1024]{1,0:T(8,128)S(1)}, f32[6,1024]{1,0:T(8,128)S(1)}, u32[]{:S(2)}, u32[]{:S(2)}) collective-permute-start(f32[6,1024]{1,0:T(8,128)S(1)} %add_add_fusion.3.refs_0_), channel_id=1, source_target_pairs={{0,4},{1,5},{2,6},{3,7},{4,0},{5,1},{6,2},{7,3},{8,12},{9,13},{10,... | collective-permute-start | bytes 73736 | tf_op jit(solution)/shard_map/ppermute | solution.py:483
  87.8 5.0 %collective-permute-start.4 = (f32[6,1024]{1,0:T(8,128)S(1)}, f32[6,1024]{1,0:T(8,128)S(1)}, u32[]{:S(2)}, u32[]{:S(2)}) collective-permute-start(f32[6,1024]{1,0:T(8,128)S(1)} %add_add_fusion.3.refs_0_), channel_id=1, source_target_pairs={{0,8},{1,9},{2,10},{3,11},{4,12},{5,13},{6,14},{7,15},{8,0},{9,1},... | collective-permute-start | bytes 73736 | tf_op jit(solution)/shard_map/ppermute | solution.py:483
  89.2 5.7 %collective-permute-start.5 = (f32[6,1024]{1,0:T(8,128)S(1)}, f32[6,1024]{1,0:T(8,128)S(1)}, u32[]{:S(2)}, u32[]{:S(2)}) collective-permute-start(f32[6,1024]{1,0:T(8,128)S(1)} %add_add_fusion.3.refs_0_), channel_id=1, source_target_pairs={{0,12},{1,13},{2,14},{3,15},{4,8},{5,9},{6,10},{7,11},{8,4},{9,5},... | collective-permute-start | bytes 73736 | tf_op jit(solution)/shard_map/ppermute | solution.py:483
  115.4 1.9 %collective-permute-start.6 = (f32[6,1024]{1,0:T(8,128)S(1)}, f32[6,1024]{1,0:T(8,128)S(1)}, u32[]{:S(2)}, u32[]{:S(2)}) collective-permute-start(f32[6,1024]{1,0:T(8,128)S(1)} %get-tuple-element.14), channel_id=1, source_target_pairs={{0,1},{1,0},{2,3},{3,2},{4,5},{5,4},{6,7},{7,6},{8,9},{9,8},{10,11... | collective-permute-start | bytes 73736 | tf_op jit(solution)/shard_map/ppermute | solution.py:483
  115.4 4.2 %collective-permute-start.7 = (f32[6,1024]{1,0:T(8,128)S(1)}, f32[6,1024]{1,0:T(8,128)S(1)}, u32[]{:S(2)}, u32[]{:S(2)}) collective-permute-start(f32[6,1024]{1,0:T(8,128)S(1)} %get-tuple-element.14), channel_id=1, source_target_pairs={{0,2},{1,3},{2,0},{3,1},{4,6},{5,7},{6,4},{7,5},{8,10},{9,11},{10,... | collective-permute-start | bytes 73736 | tf_op jit(solution)/shard_map/ppermute | solution.py:483
  115.7 3.8 %collective-permute-start.8 = (f32[6,1024]{1,0:T(8,128)S(1)}, f32[6,1024]{1,0:T(8,128)S(1)}, u32[]{:S(2)}, u32[]{:S(2)}) collective-permute-start(f32[6,1024]{1,0:T(8,128)S(1)} %get-tuple-element.14), channel_id=1, source_target_pairs={{0,3},{1,2},{2,1},{3,0},{4,7},{5,6},{6,5},{7,4},{8,11},{9,10},{10,... | collective-permute-start | bytes 73736 | tf_op jit(solution)/shard_map/ppermute | solution.py:483
  119.5 5.2 %collective-permute-start.10 = (f32[6,1024]{1,0:T(8,128)S(1)}, f32[6,1024]{1,0:T(8,128)S(1)}, u32[]{:S(2)}, u32[]{:S(2)}) collective-permute-start(f32[6,1024]{1,0:T(8,128)S(1)} %add_add_fusion.2.refs_0_), channel_id=1, source_target_pairs={{0,8},{1,9},{2,10},{3,11},{4,12},{5,13},{6,14},{7,15},{8,0},{9,1},... | collective-permute-start | bytes 73736 | tf_op jit(solution)/shard_map/ppermute | solution.py:483
  119.6 5.9 %collective-permute-start.11 = (f32[6,1024]{1,0:T(8,128)S(1)}, f32[6,1024]{1,0:T(8,128)S(1)}, u32[]{:S(2)}, u32[]{:S(2)}) collective-permute-start(f32[6,1024]{1,0:T(8,128)S(1)} %add_add_fusion.2.refs_0_), channel_id=1, source_target_pairs={{0,12},{1,13},{2,14},{3,15},{4,8},{5,9},{6,10},{7,11},{8,4},{9,5},... | collective-permute-start | bytes 73736 | tf_op jit(solution)/shard_map/ppermute | solution.py:483
  121.4 4.3 %collective-permute-start.9 = (f32[6,1024]{1,0:T(8,128)S(1)}, f32[6,1024]{1,0:T(8,128)S(1)}, u32[]{:S(2)}, u32[]{:S(2)}) collective-permute-start(f32[6,1024]{1,0:T(8,128)S(1)} %add_add_fusion.2.refs_0_), channel_id=1, source_target_pairs={{0,4},{1,5},{2,6},{3,7},{4,0},{5,1},{6,2},{7,3},{8,12},{9,13},{10,... | collective-permute-start | bytes 73736 | tf_op jit(solution)/shard_map/ppermute | solution.py:483
  146.1 1.9 %collective-permute-start.12 = (f32[6,1024]{1,0:T(8,128)S(1)}, f32[6,1024]{1,0:T(8,128)S(1)}, u32[]{:S(2)}, u32[]{:S(2)}) collective-permute-start(f32[6,1024]{1,0:T(8,128)S(1)} %get-tuple-element.16), channel_id=1, source_target_pairs={{0,1},{1,0},{2,3},{3,2},{4,5},{5,4},{6,7},{7,6},{8,9},{9,8},{10,11... | collective-permute-start | bytes 73736 | tf_op jit(solution)/shard_map/ppermute | solution.py:483
  146.1 3.9 %collective-permute-start.13 = (f32[6,1024]{1,0:T(8,128)S(1)}, f32[6,1024]{1,0:T(8,128)S(1)}, u32[]{:S(2)}, u32[]{:S(2)}) collective-permute-start(f32[6,1024]{1,0:T(8,128)S(1)} %get-tuple-element.16), channel_id=1, source_target_pairs={{0,2},{1,3},{2,0},{3,1},{4,6},{5,7},{6,4},{7,5},{8,10},{9,11},{10,... | collective-permute-start | bytes 73736 | tf_op jit(solution)/shard_map/ppermute | solution.py:483
  147.2 3.3 %collective-permute-start.14 = (f32[6,1024]{1,0:T(8,128)S(1)}, f32[6,1024]{1,0:T(8,128)S(1)}, u32[]{:S(2)}, u32[]{:S(2)}) collective-permute-start(f32[6,1024]{1,0:T(8,128)S(1)} %get-tuple-element.16), channel_id=1, source_target_pairs={{0,3},{1,2},{2,1},{3,0},{4,7},{5,6},{6,5},{7,4},{8,11},{9,10},{10,... | collective-permute-start | bytes 73736 | tf_op jit(solution)/shard_map/ppermute | solution.py:483
  150.6 4.5 %collective-permute-start.15 = (f32[6,1024]{1,0:T(8,128)S(1)}, f32[6,1024]{1,0:T(8,128)S(1)}, u32[]{:S(2)}, u32[]{:S(2)}) collective-permute-start(f32[6,1024]{1,0:T(8,128)S(1)} %add_add_fusion.1), channel_id=1, source_target_pairs={{0,4},{1,5},{2,6},{3,7},{4,0},{5,1},{6,2},{7,3},{8,12},{9,13},{10,... | collective-permute-start | bytes 73736 | tf_op jit(solution)/shard_map/ppermute | solution.py:483
  152.1 5.5 %collective-permute-start.16 = (f32[6,1024]{1,0:T(8,128)S(1)}, f32[6,1024]{1,0:T(8,128)S(1)}, u32[]{:S(2)}, u32[]{:S(2)}) collective-permute-start(f32[6,1024]{1,0:T(8,128)S(1)} %add_add_fusion.1), channel_id=1, source_target_pairs={{0,8},{1,9},{2,10},{3,11},{4,12},{5,13},{6,14},{7,15},{8,0},{9,1},... | collective-permute-start | bytes 73736 | tf_op jit(solution)/shard_map/ppermute | solution.py:483
  153.1 5.7 %collective-permute-start.17 = (f32[6,1024]{1,0:T(8,128)S(1)}, f32[6,1024]{1,0:T(8,128)S(1)}, u32[]{:S(2)}, u32[]{:S(2)}) collective-permute-start(f32[6,1024]{1,0:T(8,128)S(1)} %add_add_fusion.1), channel_id=1, source_target_pairs={{0,12},{1,13},{2,14},{3,15},{4,8},{5,9},{6,10},{7,11},{8,4},{9,5},... | collective-permute-start | bytes 73736 | tf_op jit(solution)/shard_map/ppermute | solution.py:483
